TPU v7x, 768 devices: a whole 4x8x12 slice. The times are simulated.
768 devices in a mesh: gx: 12 (over z), gy: 64 (over x, y, core).
Axes of the slice: x: 4, y: 8, z: 12, core: 2. Of those that a mesh axis runs over, the one named last changes fastest.
Arguments:
- diffusivity: float32 [50, 512, 1536], P(None, 'gy', 'gx'), may hold values from 0.02 to 0.125
- land_mask: int32 [512, 1536], P('gy', 'gx'), may hold values 0 or 1
- innovation: float32 [50, 98304], P(None, ('gx', 'gy')), may hold values from -6 to 6
- inverse_variance: float32 [50, 98304], P(None, ('gx', 'gy')), may hold values from 0.5 to 4
- owner_ids: int32 [98304, 1], P(('gx', 'gy')), may hold values from 0 to 63; in each aligned block of 128 rows (0 to 127, 128 to 255, ...) at most 4 rows name the same one
- cell_index: int32 [768, 256], P(('gx', 'gy')), may hold values from 0 to 888
- corner_weights: float32 [4, 768, 256], P(None, ('gx', 'gy'))
Outputs:
- control: float32 [50, 512, 1536], P(None, 'gy', 'gx')
- residual: float32 [50, 512, 1536], P(None, 'gy', 'gx')
Inputs may be any that keep to these rules, and one draw needn't show every extreme that they name: `owner_ids`: among the records of one device no tile index is named more than 4 times, and one is named exactly 4 times.
All inputs are finite; a program needn't handle non-finite values. No bound on the sum of `land_mask` on one device may be relied on, other than what follows from the above.
Results may differ from a plain program's by a relative error of at most 0.012.
Values sent between devices are 32-bit elements; how exact they have to be, the bound alone decides.
No kernel may reach another device: no remote copies, remote signals or barrier semaphores. Data moves between devices by JAX's collectives and lax.ppermute only.
A program may use at most 32 MiB of HBM per device.

v0:
```python
import jax
import jax.numpy as jnp
from jax import lax
from jax.sharding import PartitionSpec as P

CAP = 4
STEPS = 5
ITERS = 2


def extended(block, sides, width):
    for axis, dim in sides:
        count = lax.axis_size(axis)
        forward = [(i, i + 1) for i in range(count - 1)]
        forward.append((count - 1, 0))
        backward = [(target, source) for source, target in forward]
        low = lax.ppermute(
            lax.slice_in_dim(block, block.shape[dim] - width, None, axis=dim), axis, forward
        )
        high = lax.ppermute(lax.slice_in_dim(block, 0, width, axis=dim), axis, backward)
        block = jnp.concatenate([low, block, high], axis=dim)
    return block


def diffuse_short(field, sroot, ocean, north_keep, south_keep):
    field = ocean * field
    for step in range(STEPS):
        scaled = sroot * field
        padded = extended(scaled, (("gx", 2), ("gy", 1)), 1)
        beside_all = padded[:, 2:, 1:-1] * north_keep + padded[:, :-2, 1:-1] * south_keep
        beside_all = beside_all + padded[:, 1:-1, 2:] + padded[:, 1:-1, :-2]
        field = ocean * (field + sroot * (beside_all - 4.0 * scaled))
    return field


def sample(field, cells, weights):
    flat = field.reshape(field.shape[0], -1)
    total = weights[0][None, :] * jnp.take(flat, cells[0], axis=1)
    for corner in range(1, 4):
        total = total + weights[corner][None, :] * jnp.take(flat, cells[corner], axis=1)
    return total


def spread(misfit, cells, weights, like):
    flat = jnp.zeros((like.shape[0], like.shape[1] * like.shape[2]), jnp.float32)
    terms = (
        (weights[:, None, :] * misfit[None, :, :]).transpose(1, 0, 2).reshape(misfit.shape[0], -1)
    )
    flat = flat.at[:, cells.reshape(-1)].add(terms)
    return flat.reshape(like.shape)


def to_tiles(buffer):
    return lax.all_to_all(buffer, "gy", split_axis=1, concat_axis=1, tiled=True)


def total(value):
    return lax.psum(value, ("gx", "gy"))


def on_device(
    diffusivity, land_mask, innovation, inverse_variance, owner_ids, cell_index, corner_weights
):
    chan, rows_here, cols_here = diffusivity.shape
    count_y = lax.axis_size("gy")
    here_y = lax.axis_index("gy")
    ocean = land_mask.astype(jnp.float32)[None, :, :]
    sroot = jnp.sqrt(diffusivity)
    row_ids = jnp.arange(rows_here, dtype=jnp.int32)
    north_keep = jnp.where(
        row_ids == rows_here - 1, (here_y < count_y - 1).astype(jnp.float32), 1.0
    )[None, :, None]
    south_keep = jnp.where(row_ids == 0, (here_y > 0).astype(jnp.float32), 1.0)[None, :, None]

    def diffuse(field):
        return diffuse_short(field, sroot, ocean, north_keep, south_keep)

    owner = owner_ids[:, 0]
    onehot = (owner[:, None] == jnp.arange(count_y, dtype=jnp.int32)[None, :]).astype(jnp.int32)
    rank = jnp.sum((jnp.cumsum(onehot, axis=0) - 1) * onehot, axis=1)
    slot = owner * CAP + rank
    weight_slots = jnp.zeros((chan, count_y * CAP), jnp.float32).at[:, slot].set(inverse_variance)
    target_slots = (
        jnp.zeros((chan, count_y * CAP), jnp.float32).at[:, slot].set(inverse_variance * innovation)
    )
    cell = cell_index[0]
    base = cell // (cols_here - 1) * cols_here + cell % (cols_here - 1)
    cells = jnp.stack([base, base + 1, base + cols_here, base + cols_here + 1])
    weights = corner_weights[:, 0, :]
    target_here = to_tiles(target_slots)
    rhs = diffuse(spread(target_here, cells, weights, diffusivity))
    control = jnp.zeros_like(rhs)
    residual = rhs
    direction = rhs
    norm_now = total(jnp.sum(residual * residual))
    for step in range(ITERS):
        state = diffuse(direction)
        values = sample(state, cells, weights)
        returned = lax.all_to_all(values, "gy", split_axis=1, concat_axis=1, tiled=True)
        misfit = to_tiles(weight_slots * returned)
        adjoint = spread(misfit, cells, weights, direction)
        image = direction + diffuse(adjoint)
        alpha = norm_now / total(jnp.sum(direction * image))
        control = control + alpha * direction
        residual = residual - alpha * image
        if step + 1 < ITERS:
            norm_next = total(jnp.sum(residual * residual))
            direction = residual + norm_next / norm_now * direction
            norm_now = norm_next
    return (control, residual)


def solution(mesh):
    return jax.shard_map(
        on_device,
        mesh=mesh,
        in_specs=(
            P(None, "gy", "gx"),
            P("gy", "gx"),
            P(None, ("gx", "gy")),
            P(None, ("gx", "gy")),
            P(("gx", "gy"), None),
            P(("gx", "gy"), None),
            P(None, ("gx", "gy"), None),
        ),
        out_specs=(P(None, "gy", "gx"), P(None, "gy", "gx")),
        check_vma=False,
    )
```

profile of v0, /device:TPU:1, one launch (start us, length us, event | category | flops | bytes accessed | tf_op | source)
XLA Modules:
  0.0 1019.5 jit_solution(9892910056060609160)
XLA Ops:
  4.3 14.7 %all-to-all-start = ((f32[64,1,200]{2,1,0:T(1,128)}), f32[64,1,200]{2,1,0:T(1,128)S(1)}, u32[]{:S(2)}, u32[]{:S(2)}) async-start(f32[64,1,200]{2,1,0:T(1,128)} %reshape.257), calls=%async_computation | async-start | bytes 131072 | tf_op jit(solution)/shard_map/all_to_all | solution.py:54
  19.8 9.1 all-to-all-done
  31.3 6.2 scatter_custom_fusion.1
  38.6 11.2 %collective-permute-start.1 = (f32[50,8,1]{2,1,0:T(8,128)S(1)}, f32[50,8,1]{2,1,0:T(8,128)S(1)}, u32[]{:S(2)}, u32[]{:S(2)}) collective-permute-start(f32[50,8,1]{2,1,0:T(8,128)S(1)} %get-tuple-element.159), channel_id=1, source_target_pairs={{64,0},{128,64},{192,128},{256,192},{320,256},{384,320},{448,384},... | collective-permute-start | bytes 4808 | tf_op jit(solution)/shard_map/ppermute | solution.py:20
  53.9 5.0 collective-permute-done
  59.3 3.5 collective-permute-start.2
  68.8 3.4 collective-permute-start.4
  76.9 8.3 collective-permute-start.6
  98.9 8.7 collective-permute-start.10
  113.3 3.4 collective-permute-start.12
  121.4 8.7 collective-permute-start.14
  143.8 8.7 collective-permute-start.18
  158.2 3.4 collective-permute-start.20
  166.3 8.7 collective-permute-start.22
  180.6 3.5 collective-permute-start.24
  188.7 8.7 collective-permute-start.26
  211.2 8.7 collective-permute-start.30
  233.6 8.7 collective-permute-start.34
  252.5 3.4 collective-permute-done.36
  256.3 9.0 collective-permute-start.38
  273.2 9.8 all-to-all-start.1
  284.1 8.9 all-to-all-done.1
  294.1 13.6 %all_to_all.51 = f32[64,1,200]{2,1,0:T(1,128)S(1)} all-to-all(f32[64,1,200]{2,1,0:T(1,128)S(1)} %reshape.261), channel_id=1, replica_groups=mesh['gx'=12,'gy'=64] {'gy'}, dimensions={0} | all-to-all | bytes 102400 | tf_op jit(solution)/shard_map/all_to_all | solution.py:54
  308.9 6.2 scatter_custom_fusion.3
  327.3 3.5 collective-permute-start.42
  341.4 4.0 collective-permute-done.44
  345.8 8.5 collective-permute-start.46
  364.5 3.4 collective-permute-done.48
  368.3 9.0 collective-permute-start.50
  391.0 8.7 collective-permute-start.54
  413.5 9.0 collective-permute-start.58
  426.7 108.6 %all-reduce = (f32[]{:T(128)}, f32[]{:T(128)}) all-reduce(f32[]{:T(128)} %get-tuple-element.4, f32[]{:T(128)} %get-tuple-element.3), channel_id=1, replica_groups=mesh['gx'=12,'gy'=64] {'gx','gy'}, use_global_device_ids=true, to_apply=%region_5.6 | all-reduce | flops 2 | bytes 16 | tf_op jit(solution)/shard_map/psum | solution.py:58
  537.4 105.3 %psum.30 = f32[]{:T(128)} all-reduce(f32[]{:T(128)} %multiply_reduce_fusion.1), channel_id=1, replica_groups=mesh['gx'=12,'gy'=64] {'gx','gy'}, use_global_device_ids=true, to_apply=%region_11.13 | all-reduce | flops 1 | bytes 8 | tf_op jit(solution)/shard_map/psum | solution.py:58
  652.1 3.7 collective-permute-done.60
  656.2 3.8 collective-permute-start.62
  673.7 8.7 collective-permute-start.66
  696.2 8.7 collective-permute-start.70
  718.6 8.7 collective-permute-start.74
  741.0 8.7 collective-permute-start.78
  757.0 18.8 %all_to_all.52 = f32[64,1,200]{2,1,0:T(1,128)S(1)} all-to-all(f32[64,1,200]{2,1,0:T(1,128)S(1)} %reshape.263), channel_id=1, replica_groups=mesh['gx'=12,'gy'=64] {'gy'}, dimensions={0} | all-to-all | bytes 102400 | tf_op jit(solution)/shard_map/all_to_all | solution.py:99
  776.9 13.6 %all_to_all.53 = f32[64,1,200]{2,1,0:T(1,128)S(1)} all-to-all(f32[64,1,200]{2,1,0:T(1,128)S(1)} %reshape.265), channel_id=1, replica_groups=mesh['gx'=12,'gy'=64] {'gy'}, dimensions={0} | all-to-all | bytes 102400 | tf_op jit(solution)/shard_map/all_to_all | solution.py:54
  791.7 6.2 scatter_custom_fusion.4
  827.3 8.6 collective-permute-start.86
  849.6 9.0 collective-permute-start.90
  868.8 3.4 collective-permute-done.92
  872.6 9.0 collective-permute-start.94
  895.4 9.0 collective-permute-start.98
  908.6 108.6 %psum.31 = f32[]{:T(128)} all-reduce(f32[]{:T(128)} %get-tuple-element.7), channel_id=1, replica_groups=mesh['gx'=12,'gy'=64] {'gx','gy'}, use_global_device_ids=true, to_apply=%region_14.16 | all-reduce | flops 1 | bytes 8 | tf_op jit(solution)/shard_map/psum | solution.py:58
  (317 shorter events, 341.0 us)
Async XLA Ops:
  4.3 24.6 %all-to-all-start = ((f32[64,1,200]{2,1,0:T(1,128)}), f32[64,1,200]{2,1,0:T(1,128)S(1)}, u32[]{:S(2)}, u32[]{:S(2)}) async-start(f32[64,1,200]{2,1,0:T(1,128)} %reshape.257), calls=%async_computation | async-start | bytes 131072 | tf_op jit(solution)/shard_map/all_to_all | solution.py:54
  38.6 15.3 %collective-permute-start.1 = (f32[50,8,1]{2,1,0:T(8,128)S(1)}, f32[50,8,1]{2,1,0:T(8,128)S(1)}, u32[]{:S(2)}, u32[]{:S(2)}) collective-permute-start(f32[50,8,1]{2,1,0:T(8,128)S(1)} %get-tuple-element.159), channel_id=1, source_target_pairs={{64,0},{128,64},{192,128},{256,192},{320,256},{384,320},{448,384},... | collective-permute-start | bytes 4808 | tf_op jit(solution)/shard_map/ppermute | solution.py:20
  49.8 9.0 collective-permute-start
  68.8 7.7 collective-permute-start.4
  76.9 10.3 %collective-permute-start.6 = (f32[50,1,130]{2,1,0:T(1,128)S(1)}, f32[50,1,130]{2,1,0:T(1,128)S(1)}, u32[]{:S(2)}, u32[]{:S(2)}) collective-permute-start(f32[50,1,130]{2,1,0:T(1,128)S(1)} %get-tuple-element.105), channel_id=1, source_target_pairs={{1,0},{2,1},{3,2},{4,3},{5,4},{6,5},{7,6},{8,7},{9,8},{10,9},{11,1... | collective-permute-start | bytes 78008 | tf_op jit(solution)/shard_map/ppermute | solution.py:20
  90.8 7.7 collective-permute-start.8
  98.9 10.6 %collective-permute-start.10 = (f32[50,1,130]{2,1,0:T(1,128)S(1)}, f32[50,1,130]{2,1,0:T(1,128)S(1)}, u32[]{:S(2)}, u32[]{:S(2)}) collective-permute-start(f32[50,1,130]{2,1,0:T(1,128)S(1)} %get-tuple-element.103), channel_id=1, source_target_pairs={{1,0},{2,1},{3,2},{4,3},{5,4},{6,5},{7,6},{8,7},{9,8},{10,9},{11,1... | collective-permute-start | bytes 78008 | tf_op jit(solution)/shard_map/ppermute | solution.py:20
  113.3 7.7 collective-permute-start.12
  121.4 10.6 %collective-permute-start.14 = (f32[50,1,130]{2,1,0:T(1,128)S(1)}, f32[50,1,130]{2,1,0:T(1,128)S(1)}, u32[]{:S(2)}, u32[]{:S(2)}) collective-permute-start(f32[50,1,130]{2,1,0:T(1,128)S(1)} %get-tuple-element.101), channel_id=1, source_target_pairs={{1,0},{2,1},{3,2},{4,3},{5,4},{6,5},{7,6},{8,7},{9,8},{10,9},{11,1... | collective-permute-start | bytes 78008 | tf_op jit(solution)/shard_map/ppermute | solution.py:20
  135.7 7.7 collective-permute-start.16
  143.8 10.6 %collective-permute-start.18 = (f32[50,1,130]{2,1,0:T(1,128)S(1)}, f32[50,1,130]{2,1,0:T(1,128)S(1)}, u32[]{:S(2)}, u32[]{:S(2)}) collective-permute-start(f32[50,1,130]{2,1,0:T(1,128)S(1)} %get-tuple-element.99), channel_id=1, source_target_pairs={{1,0},{2,1},{3,2},{4,3},{5,4},{6,5},{7,6},{8,7},{9,8},{10,9},{11,1... | collective-permute-start | bytes 78008 | tf_op jit(solution)/shard_map/ppermute | solution.py:20
  158.2 7.7 collective-permute-start.20
  166.3 10.6 %collective-permute-start.22 = (f32[50,1,130]{2,1,0:T(1,128)S(1)}, f32[50,1,130]{2,1,0:T(1,128)S(1)}, u32[]{:S(2)}, u32[]{:S(2)}) collective-permute-start(f32[50,1,130]{2,1,0:T(1,128)S(1)} %get-tuple-element.97), channel_id=1, source_target_pairs={{1,0},{2,1},{3,2},{4,3},{5,4},{6,5},{7,6},{8,7},{9,8},{10,9},{11,1... | collective-permute-start | bytes 78008 | tf_op jit(solution)/shard_map/ppermute | solution.py:20
  180.6 7.7 collective-permute-start.24
  188.7 10.6 %collective-permute-start.26 = (f32[50,1,130]{2,1,0:T(1,128)S(1)}, f32[50,1,130]{2,1,0:T(1,128)S(1)}, u32[]{:S(2)}, u32[]{:S(2)}) collective-permute-start(f32[50,1,130]{2,1,0:T(1,128)S(1)} %get-tuple-element.95), channel_id=1, source_target_pairs={{1,0},{2,1},{3,2},{4,3},{5,4},{6,5},{7,6},{8,7},{9,8},{10,9},{11,1... | collective-permute-start | bytes 78008 | tf_op jit(solution)/shard_map/ppermute | solution.py:20
  203.1 7.7 collective-permute-start.28
  211.2 10.7 %collective-permute-start.30 = (f32[50,1,130]{2,1,0:T(1,128)S(1)}, f32[50,1,130]{2,1,0:T(1,128)S(1)}, u32[]{:S(2)}, u32[]{:S(2)}) collective-permute-start(f32[50,1,130]{2,1,0:T(1,128)S(1)} %get-tuple-element.93), channel_id=1, source_target_pairs={{1,0},{2,1},{3,2},{4,3},{5,4},{6,5},{7,6},{8,7},{9,8},{10,9},{11,1... | collective-permute-start | bytes 78008 | tf_op jit(solution)/shard_map/ppermute | solution.py:20
  225.5 7.7 collective-permute-start.32
  233.6 10.6 %collective-permute-start.34 = (f32[50,1,130]{2,1,0:T(1,128)S(1)}, f32[50,1,130]{2,1,0:T(1,128)S(1)}, u32[]{:S(2)}, u32[]{:S(2)}) collective-permute-start(f32[50,1,130]{2,1,0:T(1,128)S(1)} %get-tuple-element.91), channel_id=1, source_target_pairs={{1,0},{2,1},{3,2},{4,3},{5,4},{6,5},{7,6},{8,7},{9,8},{10,9},{11,1... | collective-permute-start | bytes 78008 | tf_op jit(solution)/shard_map/ppermute | solution.py:20
  248.2 7.7 collective-permute-start.36
  256.3 10.9 %collective-permute-start.38 = (f32[50,1,130]{2,1,0:T(1,128)S(1)}, f32[50,1,130]{2,1,0:T(1,128)S(1)}, u32[]{:S(2)}, u32[]{:S(2)}) collective-permute-start(f32[50,1,130]{2,1,0:T(1,128)S(1)} %get-tuple-element.89), channel_id=1, source_target_pairs={{1,0},{2,1},{3,2},{4,3},{5,4},{6,5},{7,6},{8,7},{9,8},{10,9},{11,1... | collective-permute-start | bytes 78008 | tf_op jit(solution)/shard_map/ppermute | solution.py:20
  273.2 19.7 %all-to-all-start.1 = ((f32[64,1,200]{2,1,0:T(1,128)}), f32[64,1,200]{2,1,0:T(1,128)S(1)}, u32[]{:S(2)}, u32[]{:S(2)}) async-start(f32[64,1,200]{2,1,0:T(1,128)} %reshape.259), calls=%async_computation.1 | async-start | bytes 131072 | tf_op jit(solution)/shard_map/all_to_all | solution.py:99
  315.5 8.2 collective-permute-start.41
  317.9 9.0 collective-permute-start.40
  337.7 7.7 collective-permute-start.44
  345.8 10.4 %collective-permute-start.46 = (f32[50,1,130]{2,1,0:T(1,128)S(1)}, f32[50,1,130]{2,1,0:T(1,128)S(1)}, u32[]{:S(2)}, u32[]{:S(2)}) collective-permute-start(f32[50,1,130]{2,1,0:T(1,128)S(1)} %get-tuple-element.85), channel_id=1, source_target_pairs={{1,0},{2,1},{3,2},{4,3},{5,4},{6,5},{7,6},{8,7},{9,8},{10,9},{11,1... | collective-permute-start | bytes 78008 | tf_op jit(solution)/shard_map/ppermute | solution.py:20
  360.2 7.7 collective-permute-start.48
  368.3 10.9 %collective-permute-start.50 = (f32[50,1,130]{2,1,0:T(1,128)S(1)}, f32[50,1,130]{2,1,0:T(1,128)S(1)}, u32[]{:S(2)}, u32[]{:S(2)}) collective-permute-start(f32[50,1,130]{2,1,0:T(1,128)S(1)} %get-tuple-element.83), channel_id=1, source_target_pairs={{1,0},{2,1},{3,2},{4,3},{5,4},{6,5},{7,6},{8,7},{9,8},{10,9},{11,1... | collective-permute-start | bytes 78008 | tf_op jit(solution)/shard_map/ppermute | solution.py:20
  382.9 7.7 collective-permute-start.52
  391.0 10.6 %collective-permute-start.54 = (f32[50,1,130]{2,1,0:T(1,128)S(1)}, f32[50,1,130]{2,1,0:T(1,128)S(1)}, u32[]{:S(2)}, u32[]{:S(2)}) collective-permute-start(f32[50,1,130]{2,1,0:T(1,128)S(1)} %get-tuple-element.81), channel_id=1, source_target_pairs={{1,0},{2,1},{3,2},{4,3},{5,4},{6,5},{7,6},{8,7},{9,8},{10,9},{11,1... | collective-permute-start | bytes 78008 | tf_op jit(solution)/shard_map/ppermute | solution.py:20
  405.4 7.7 collective-permute-start.56
  413.5 10.9 %collective-permute-start.58 = (f32[50,1,130]{2,1,0:T(1,128)S(1)}, f32[50,1,130]{2,1,0:T(1,128)S(1)}, u32[]{:S(2)}, u32[]{:S(2)}) collective-permute-start(f32[50,1,130]{2,1,0:T(1,128)S(1)} %get-tuple-element.79), channel_id=1, source_target_pairs={{1,0},{2,1},{3,2},{4,3},{5,4},{6,5},{7,6},{8,7},{9,8},{10,9},{11,1... | collective-permute-start | bytes 78008 | tf_op jit(solution)/shard_map/ppermute | solution.py:20
  644.2 7.8 collective-permute-start.61
  647.1 8.7 collective-permute-start.60
  673.7 10.6 %collective-permute-start.66 = (f32[50,1,130]{2,1,0:T(1,128)S(1)}, f32[50,1,130]{2,1,0:T(1,128)S(1)}, u32[]{:S(2)}, u32[]{:S(2)}) collective-permute-start(f32[50,1,130]{2,1,0:T(1,128)S(1)} %get-tuple-element.75), channel_id=1, source_target_pairs={{1,0},{2,1},{3,2},{4,3},{5,4},{6,5},{7,6},{8,7},{9,8},{10,9},{11,1... | collective-permute-start | bytes 78008 | tf_op jit(solution)/shard_map/ppermute | solution.py:20
  696.2 10.6 %collective-permute-start.70 = (f32[50,1,130]{2,1,0:T(1,128)S(1)}, f32[50,1,130]{2,1,0:T(1,128)S(1)}, u32[]{:S(2)}, u32[]{:S(2)}) collective-permute-start(f32[50,1,130]{2,1,0:T(1,128)S(1)} %get-tuple-element.73), channel_id=1, source_target_pairs={{1,0},{2,1},{3,2},{4,3},{5,4},{6,5},{7,6},{8,7},{9,8},{10,9},{11,1... | collective-permute-start | bytes 78008 | tf_op jit(solution)/shard_map/ppermute | solution.py:20
  710.5 7.7 collective-permute-start.72
  718.6 10.6 %collective-permute-start.74 = (f32[50,1,130]{2,1,0:T(1,128)S(1)}, f32[50,1,130]{2,1,0:T(1,128)S(1)}, u32[]{:S(2)}, u32[]{:S(2)}) collective-permute-start(f32[50,1,130]{2,1,0:T(1,128)S(1)} %get-tuple-element.71), channel_id=1, source_target_pairs={{1,0},{2,1},{3,2},{4,3},{5,4},{6,5},{7,6},{8,7},{9,8},{10,9},{11,1... | collective-permute-start | bytes 78008 | tf_op jit(solution)/shard_map/ppermute | solution.py:20
  732.9 7.7 collective-permute-start.76
  741.0 10.8 %collective-permute-start.78 = (f32[50,1,130]{2,1,0:T(1,128)S(1)}, f32[50,1,130]{2,1,0:T(1,128)S(1)}, u32[]{:S(2)}, u32[]{:S(2)}) collective-permute-start(f32[50,1,130]{2,1,0:T(1,128)S(1)} %get-tuple-element.69), channel_id=1, source_target_pairs={{1,0},{2,1},{3,2},{4,3},{5,4},{6,5},{7,6},{8,7},{9,8},{10,9},{11,1... | collective-permute-start | bytes 78008 | tf_op jit(solution)/shard_map/ppermute | solution.py:20
  798.3 8.2 collective-permute-start.81
  800.2 9.2 collective-permute-start.80
  827.3 10.5 %collective-permute-start.86 = (f32[50,1,130]{2,1,0:T(1,128)S(1)}, f32[50,1,130]{2,1,0:T(1,128)S(1)}, u32[]{:S(2)}, u32[]{:S(2)}) collective-permute-start(f32[50,1,130]{2,1,0:T(1,128)S(1)} %get-tuple-element.65), channel_id=1, source_target_pairs={{1,0},{2,1},{3,2},{4,3},{5,4},{6,5},{7,6},{8,7},{9,8},{10,9},{11,1... | collective-permute-start | bytes 78008 | tf_op jit(solution)/shard_map/ppermute | solution.py:20
  841.5 7.7 collective-permute-start.88
  849.6 10.9 %collective-permute-start.90 = (f32[50,1,130]{2,1,0:T(1,128)S(1)}, f32[50,1,130]{2,1,0:T(1,128)S(1)}, u32[]{:S(2)}, u32[]{:S(2)}) collective-permute-start(f32[50,1,130]{2,1,0:T(1,128)S(1)} %get-tuple-element.63), channel_id=1, source_target_pairs={{1,0},{2,1},{3,2},{4,3},{5,4},{6,5},{7,6},{8,7},{9,8},{10,9},{11,1... | collective-permute-start | bytes 78008 | tf_op jit(solution)/shard_map/ppermute | solution.py:20
  872.6 10.9 %collective-permute-start.94 = (f32[50,1,130]{2,1,0:T(1,128)S(1)}, f32[50,1,130]{2,1,0:T(1,128)S(1)}, u32[]{:S(2)}, u32[]{:S(2)}) collective-permute-start(f32[50,1,130]{2,1,0:T(1,128)S(1)} %get-tuple-element.61), channel_id=1, source_target_pairs={{1,0},{2,1},{3,2},{4,3},{5,4},{6,5},{7,6},{8,7},{9,8},{10,9},{11,1... | collective-permute-start | bytes 78008 | tf_op jit(solution)/shard_map/ppermute | solution.py:20
  887.3 7.7 collective-permute-start.96
  895.4 10.9 %collective-permute-start.98 = (f32[50,1,130]{2,1,0:T(1,128)S(1)}, f32[50,1,130]{2,1,0:T(1,128)S(1)}, u32[]{:S(2)}, u32[]{:S(2)}) collective-permute-start(f32[50,1,130]{2,1,0:T(1,128)S(1)} %get-tuple-element.59), channel_id=1, source_target_pairs={{1,0},{2,1},{3,2},{4,3},{5,4},{6,5},{7,6},{8,7},{9,8},{10,9},{11,1... | collective-permute-start | bytes 78008 | tf_op jit(solution)/shard_map/ppermute | solution.py:20
  (60 other events, 297.5 us)
where the time goes:
time: 1030 us; the launch traced here: 1020 us
  starting transfers between devices  412 us (40%)
  blocking collectives  369 us (36%)
  waiting for transfers between devices  165 us (16%)
  other arithmetic  49.3 us (5%)
  local copies, waits for them, and re-layouts  17.7 us (2%)
    psum x3, blocking collectives, total(): return lax.psum(value, ('gx', 'gy'))  323 us
    ppermute x50, starting transfers between devices, extended(): lax.ppermute(lax.slice_in_dim(block, 0, width, axis=dim), axis, backward)  258 us
    ppermute x50, starting transfers between devices, extended(): lax.ppermute(lax.slice_in_dim(block, block.shape[dim] - width, None, axis...  129 us
    ppermute x50, waiting for transfers between devices, extended(): lax.ppermute(lax.slice_in_dim(block, block.shape[dim] - width, None, axis...  112 us
    ppermute x50, waiting for transfers between devices, extended(): lax.ppermute(lax.slice_in_dim(block, 0, width, axis=dim), axis, backward)  35.5 us
    all_to_all x2, blocking collectives, to_tiles(): return lax.all_to_all(buffer, 'gy', split_axis=1, concat_axis=1, tiled=True)  27.3 us
  transfers between devices with their start and end apart: 102, of which 77 were waited for; matrix products, arithmetic and copies ran while one was open for 0% of the time, Pallas kernels for 0%

commit v1 on v0

v1 whole, which is shorter than its diff:
```python
import functools

import jax
import jax.numpy as jnp
from jax import lax
from jax.experimental import pallas as pl
from jax.experimental.pallas import tpu as pltpu
from jax.sharding import PartitionSpec as P

CAP = 4
STEPS = 5
CHAN = 50
WIN = 32
LOW = 24
FULL = 56
COLS = 128
CY = 8
ROWS = 2 * CY
FAR = 2 * STEPS


def call(body, outs, flops, scratch=(), scalars=0):
    def run(*args):
        size = sum(a.size * a.dtype.itemsize for a in args) + sum(o.size * o.dtype.itemsize for o in outs)
        specs = [pl.BlockSpec(memory_space=pltpu.SMEM)] * scalars
        specs += [pl.BlockSpec(memory_space=pltpu.VMEM)] * (len(args) - scalars)
        return pl.pallas_call(
            body,
            out_shape=tuple(outs),
            in_specs=specs,
            out_specs=tuple(pl.BlockSpec(memory_space=pltpu.VMEM) for _ in outs),
            scratch_shapes=list(scratch),
            compiler_params=pltpu.CompilerParams(vmem_limit_bytes=16 * 1024 * 1024),
            cost_estimate=pl.CostEstimate(flops=flops, bytes_accessed=size, transcendentals=0),
        )(*args)

    return run


def f32(*shape):
    return jax.ShapeDtypeStruct(shape, jnp.float32)


def split(value):
    high = value.astype(jnp.bfloat16)
    return high, (value - high.astype(jnp.float32)).astype(jnp.bfloat16)


def dot(a, b, dims):
    return lax.dot_general(a, b, (dims, ((), ())), preferred_element_type=jnp.float32)


def records_body(own_ref, inv_ref, inno_ref, out_ref, pad_ref):
    count = own_ref.shape[1]
    tiles = out_ref.shape[0] // CAP
    chips = tiles // 2
    own = own_ref[...]
    owners = lax.broadcasted_iota(jnp.int32, (tiles, count), 0)
    onehot = jnp.where(owners == own, 1.0, 0.0)
    at = lax.broadcasted_iota(jnp.int32, (count, count), 0)
    to = lax.broadcasted_iota(jnp.int32, (count, count), 1)
    before = jnp.where(at < to, 1.0, 0.0).astype(jnp.bfloat16)
    earlier = dot(onehot.astype(jnp.bfloat16), before, ((1,), (0,)))
    rank = jnp.sum(onehot * earlier, axis=0, keepdims=True)
    chip_here = lax.broadcasted_iota(jnp.int32, (chips, count), 0) == (own >> 1)
    even = (own & 1) == 0
    picks = []
    for r in range(CAP):
        hit = jnp.where(chip_here & (rank == float(r)), 1.0, 0.0)
        picks.append(jnp.concatenate([jnp.where(even, hit, 0.0), jnp.where(even, 0.0, hit)], axis=1))
    pick = jnp.concatenate(picks, axis=0).astype(jnp.bfloat16)
    inv = inv_ref[...]
    pad_ref[...] = jnp.zeros_like(pad_ref)
    pad_ref[0:CHAN, :] = inv
    pad_ref[FULL : FULL + CHAN, :] = inv * inno_ref[...]
    zero = jnp.zeros((2 * WIN, count), jnp.float32)
    for core in range(2):
        at = LOW * core
        both = jnp.concatenate([pad_ref[at : at + WIN, :], pad_ref[FULL + at : FULL + at + WIN, :]], axis=0)
        block = jnp.concatenate(
            [jnp.concatenate([both, zero], axis=1), jnp.concatenate([zero, both], axis=1)], axis=0
        )
        first, rest = block.astype(jnp.bfloat16), block
        rest = rest - first.astype(jnp.float32)
        second, third = split(rest)
        total = dot(pick, first, ((1,), (1,)))
        total = total + dot(pick, second, ((1,), (1,)))
        total = total + dot(pick, third, ((1,), (1,)))
        for r in range(CAP):
            out_ref[pl.ds(core * CAP + r, chips, stride=2 * CAP), :] = total[r * chips : (r + 1) * chips]


def fields_body(core_ref, diff_ref, mask_ref, cell_ref, corner_ref, mine_ref, mate_ref, pad_ref):
    core = core_ref[0]
    slots = cell_ref.shape[1]
    masked = diff_ref[...] * mask_ref[...].astype(jnp.float32)[None]
    pad_ref[0 : CHAN * CY, :] = masked.reshape(CHAN * CY, COLS)
    pad_ref[CHAN * CY :, :] = jnp.zeros((FULL * CY - CHAN * CY, COLS), jnp.float32)
    for r in range(CY):
        at = LOW * CY * core + r
        mine_ref[r] = pad_ref[pl.ds(at, WIN, stride=CY), :]
        at = LOW * CY * (1 - core) + r
        mate_ref[r * WIN : (r + 1) * WIN, :] = pad_ref[pl.ds(at, WIN, stride=CY), :]
    base = CY * WIN
    table = jnp.concatenate(
        [cell_ref[...].astype(jnp.float32), corner_ref[...], jnp.zeros((3, slots), jnp.float32)], axis=0
    )
    for part in range(slots // COLS):
        mate_ref[base + 8 * part : base + 8 * part + 8, :] = table[:, part * COLS : (part + 1) * COLS]


def adjoint(misfits, high_ref, low_ref, store):
    for tile in range(2):
        high, low = split(misfits[tile])
        both = jnp.concatenate([high, low], axis=0)
        wide = dot(both, high_ref[tile], ((1,), (1,)))
        flat = wide[:WIN] + wide[WIN:] + dot(high, low_ref[tile], ((1,), (1,)))
        for r in range(CY):
            store(tile * CY + r, flat[:, r * COLS : (r + 1) * COLS])


def seed_body(core_ref, mine_ref, theirs_ref, cell_ref, corner_ref, rec_ref, *outs):
    d_ref, high_ref, low_ref, weight_ref, g_ref, up_ref, down_ref = outs
    core = core_ref[0]
    slots = cell_ref.shape[1]
    base = CY * WIN
    other = jnp.concatenate(
        [theirs_ref[base + 8 * part : base + 8 * part + 8, :] for part in range(slots // COLS)], axis=1
    )
    here = jnp.concatenate(
        [cell_ref[...].astype(jnp.float32), corner_ref[...], jnp.zeros((3, slots), jnp.float32)], axis=0
    )
    columns = lax.broadcasted_iota(jnp.int32, (COLS, slots), 0)
    slot_t = rec_ref[...].T
    targets = []
    for tile in range(2):
        first = core == tile
        table = jnp.where(first, here, other)
        cell = table[0:1].astype(jnp.int32)
        row = jnp.zeros_like(cell)
        for edge in range(1, CY - 1):
            row = row + jnp.where(cell >= edge * (COLS - 1), 1, 0)
        col = cell - row * (COLS - 1)
        at_col, at_next = col == columns, col + 1 == columns
        for r in range(CY):
            lower, upper = row == r, row == r - 1
            west = jnp.where(lower, table[1:2], 0.0) + jnp.where(upper, table[3:4], 0.0)
            east = jnp.where(lower, table[2:3], 0.0) + jnp.where(upper, table[4:5], 0.0)
            matrix = jnp.where(at_col, west, 0.0) + jnp.where(at_next, east, 0.0)
            high, low = split(matrix)
            high_ref[tile, r * COLS : (r + 1) * COLS, :] = high
            low_ref[tile, r * COLS : (r + 1) * COLS, :] = low
            d_ref[tile * CY + r] = jnp.where(first, mine_ref[r], theirs_ref[r * WIN : (r + 1) * WIN, :])
        weight_ref[tile] = slot_t[tile * 2 * WIN : tile * 2 * WIN + WIN]
        targets.append(slot_t[tile * 2 * WIN + WIN : (tile + 1) * 2 * WIN])

    def store(row, value):
        g_ref[row] = jnp.sqrt(d_ref[row]) * value

    adjoint(targets, high_ref, low_ref, store)
    up_ref[0:FAR] = g_ref[0:FAR]
    up_ref[FAR : 2 * FAR] = d_ref[0:FAR]
    down_ref[0:FAR] = g_ref[ROWS - FAR : ROWS]
    down_ref[FAR : 2 * FAR] = d_ref[ROWS - FAR : ROWS]


def places(halo):
    each = COLS // halo
    rows = range(1, ROWS + 2 * halo - 1)
    return [(row, n // each, n % each) for n, row in enumerate(rows)], -(-len(rows) // each)


def strips_body(halo, kinds, *refs):
    heres, (south_ref, north_ref, west_ref, east_ref) = refs[:kinds], refs[kinds:]
    spots, tiles = places(halo)
    lane = lax.broadcasted_iota(jnp.int32, (WIN, COLS), 1)
    for kind in range(kinds):
        for tile in range(tiles):
            west = jnp.zeros((WIN, COLS), jnp.float32)
            east = jnp.zeros((WIN, COLS), jnp.float32)
            for row, own_tile, q in spots:
                if own_tile != tile:
                    continue
                if row < halo:
                    line = south_ref[kind * halo + row]
                elif row < halo + ROWS:
                    line = heres[kind][row - halo]
                else:
                    line = north_ref[kind * halo + row - halo - ROWS]
                inside = (lane >= halo * q) & (lane < halo * q + halo)
                west = jnp.where(inside, pltpu.roll(line, halo * q, 1) if q else line, west)
                east = jnp.where(inside, pltpu.roll(line, (halo * q + halo) % COLS, 1), east)
            west_ref[kind * tiles + tile] = west
            east_ref[kind * tiles + tile] = east


def extend(dst, halo, offset, kind, here_ref, south_ref, north_ref, east_ref, west_ref):
    spots, tiles = places(halo)
    where_of = {row: (tile, q) for row, tile, q in spots}
    lane = lax.broadcasted_iota(jnp.int32, (WIN, COLS), 1)
    for row in range(ROWS + 2 * halo):
        if row < halo:
            line = south_ref[kind * halo + row]
        elif row < halo + ROWS:
            line = here_ref[row - halo]
        else:
            line = north_ref[kind * halo + row - halo - ROWS]
        dst[offset + row, :, 0:COLS] = line
        beyond = jnp.zeros((WIN, COLS), jnp.float32)
        if row in where_of:
            tile, q = where_of[row]
            right, left = east_ref[kind * tiles + tile], west_ref[kind * tiles + tile]
            right = pltpu.roll(right, COLS - halo * q, 1) if q else right
            left = pltpu.roll(left, COLS - halo - halo * q, 1)
            beyond = jnp.where(lane < halo, right, jnp.where(lane >= COLS - halo, left, 0.0))
        dst[offset + row, :, COLS:] = beyond


def sweep(src, dst, d_ref, low, high):
    lane = lax.broadcasted_iota(jnp.int32, (WIN, COLS), 1)
    last, first = lane == COLS - 1, lane == 0

    def body(row, carry):
        before, now = carry
        after = src[row + 1]
        a, b = now[:, :COLS], now[:, COLS:]
        east_a, east_b = pltpu.roll(a, COLS - 1, 1), pltpu.roll(b, COLS - 1, 1)
        west_a, west_b = pltpu.roll(a, 1, 1), pltpu.roll(b, 1, 1)
        beside_a = jnp.where(last, east_b, east_a) + jnp.where(first, west_b, west_a)
        beside_b = jnp.where(last, east_a, east_b) + jnp.where(first, west_a, west_b)
        beside = jnp.concatenate([beside_a, beside_b], axis=1)
        dst[row] = now + d_ref[row] * (before + after + beside - 4.0 * now)
        return now, after

    lax.fori_loop(low, high, body, (src[low - 1], src[low]), unroll=2)


def unscale(value, d):
    return jnp.where(d > 0.0, value * lax.rsqrt(jnp.where(d > 0.0, d, 1.0)), 0.0)


def largest(value):
    top = jnp.max(jnp.max(jnp.abs(value), axis=1, keepdims=True), axis=0, keepdims=True)
    return jnp.maximum(top, 1e-30)


def whole_sum(value):
    return jnp.sum(jnp.sum(value, axis=1, keepdims=True), axis=0, keepdims=True)


def pair_body(later, *refs):
    refs = list(refs)
    core_ref = refs.pop(0)
    here_ref, south_ref, north_ref, east_ref, west_ref = refs[:5]
    refs = refs[5:]
    if later:
        wide_d, high_ref, low_ref, weight_ref, q_in, u_in = refs[:6]
        q_ref, up_ref, down_ref, g_ref, stats_ref, first_ref, second_ref = refs[6:]
    else:
        d_ref, high_ref, low_ref, weight_ref = refs[:4]
        q_ref, u_ref, wide_d, up_ref, down_ref, g_ref, first_ref, second_ref = refs[4:]
        extend(wide_d, FAR, 0, 1, d_ref, south_ref, north_ref, east_ref, west_ref)
    extend(first_ref, FAR, 0, 0, here_ref, south_ref, north_ref, east_ref, west_ref)
    src, dst = first_ref, second_ref
    total = ROWS + 2 * FAR
    halo = STEPS if later else FAR
    rows = []
    for step in range(1, FAR + 1):
        sweep(src, dst, wide_d, step, total - step)
        src, dst = dst, src
        if step == STEPS:
            for r in range(ROWS):
                value = unscale(src[FAR + r, :, 0:COLS], wide_d[FAR + r, :, 0:COLS])
                q_ref[r] = q_in[r] + value if later else value
    for r in range(ROWS):
        value = unscale(src[FAR + r, :, 0:COLS], wide_d[FAR + r, :, 0:COLS])
        if later:
            value = value + u_in[r]
        else:
            u_ref[r] = value
        rows.append(value)
    misfits, samples = [], []
    for tile in range(2):
        flat = jnp.concatenate(rows[tile * CY : (tile + 1) * CY], axis=1)
        high, low = split(flat)
        both = dot(jnp.concatenate([high, low], axis=0), high_ref[tile], ((1,), (0,)))
        value = both[:WIN] + both[WIN:] + dot(high, low_ref[tile], ((1,), (0,)))
        samples.append(value)
        misfits.append(weight_ref[tile] * value)

    def store(row, value):
        g_ref[row] = jnp.sqrt(wide_d[FAR + row, :, 0:COLS]) * value

    adjoint(misfits, high_ref, low_ref, store)
    up_ref[...] = g_ref[0:halo]
    down_ref[...] = g_ref[ROWS - halo : ROWS]
    if later:
        sub = lax.broadcasted_iota(jnp.int32, (WIN, 1), 0)
        keep = jnp.where((sub < LOW) | (core_ref[0] == 1), 1.0, 0.0)
        top0 = jnp.zeros((WIN, COLS), jnp.float32)
        top1 = jnp.zeros((WIN, COLS), jnp.float32)
        for r in range(ROWS):
            top0 = jnp.maximum(top0, jnp.abs(q_in[r]))
            top1 = jnp.maximum(top1, jnp.abs(q_ref[r]))
        t0, t1 = largest(top0), largest(top1)
        v1 = jnp.maximum(largest(samples[0]), largest(samples[1]))
        i0, i1, iv = 1.0 / t0, 1.0 / t1, 1.0 / v1
        sums = [jnp.zeros((WIN, COLS), jnp.float32) for _ in range(3)]
        for r in range(ROWS):
            a, b = q_in[r] * i0, q_ref[r] * i1
            sums = [sums[0] + a * a, sums[1] + a * b, sums[2] + b * b]
        values = [whole_sum(s * keep) for s in sums]
        quad = sum(weight_ref[tile] * (samples[tile] * iv) * (samples[tile] * iv) for tile in range(2))
        values += [whole_sum(quad * keep), t0, t1, v1]
        stats_ref[...] = jnp.broadcast_to(as_row(values), stats_ref.shape)


def as_row(values):
    lane = lax.broadcasted_iota(jnp.int32, (1, COLS), 1)
    row = jnp.zeros((1, COLS), jnp.float32)
    for n, value in enumerate(values):
        row = jnp.where(lane == n, value, row)
    return row


def merged(block):
    part = [block[:, n : n + 1] for n in range(7)]
    tops = [jnp.max(part[n], axis=0, keepdims=True) for n in (4, 5, 6)]
    r0, r1, rv = (part[4 + n] / tops[n] for n in range(3))
    values = [part[0] * r0 * r0, part[1] * r0 * r1, part[2] * r1 * r1, part[3] * rv * rv]
    return [jnp.sum(value, axis=0, keepdims=True) for value in values] + tops


def merge_body(in_ref, out_ref):
    out_ref[...] = jnp.broadcast_to(as_row(merged(in_ref[...])), out_ref.shape)


def last_body(core_ref, here_ref, south_ref, north_ref, east_ref, west_ref, wide_d, q0_ref, q1_ref, *outs):
    mine_ref, mate_ref, first_ref, second_ref, near_d, q2_ref = outs
    core = core_ref[0]
    total = ROWS + 2 * STEPS
    extend(first_ref, STEPS, 0, 0, here_ref, south_ref, north_ref, east_ref, west_ref)
    for row in range(total):
        near_d[row] = wide_d[row + FAR - STEPS]
    src, dst = first_ref, second_ref
    for step in range(1, STEPS + 1):
        sweep(src, dst, near_d, step, total - step)
        src, dst = dst, src
    for r in range(ROWS):
        d = near_d[STEPS + r, :, 0:COLS]
        q2_ref[r] = q1_ref[r] + unscale(src[STEPS + r, :, 0:COLS], d)
    for n, q in enumerate((q0_ref, q1_ref, q2_ref)):
        mine_ref[n * CY : (n + 1) * CY] = q[pl.ds(core * CY, CY)]
        mate_ref[n * CY : (n + 1) * CY] = q[pl.ds((1 - core) * CY, CY)]


def final_body(core_ref, mine_ref, theirs_ref, stats_ref, control_ref, residual_ref, c_ref, r_ref):
    core = core_ref[0]
    m00, m01, m11, s11, t0, t1, v1 = merged(stats_ref[...])
    ratio = t1 / t0
    scaled = m00 / m01
    alpha0 = scaled / ratio
    norm1 = m00 - 2.0 * scaled * m01 + scaled * scaled * m11
    beta = norm1 / m00
    lift = 1.0 + beta
    relative = v1 / t1
    curve = lift * lift * ratio * m01 - 2.0 * lift * scaled * ratio * m11
    curve = curve + scaled * scaled * (m11 + relative * relative * s11)
    alpha1 = norm1 / curve
    one = alpha0 + alpha1 * lift
    two = alpha1 * alpha0
    for ref, owner in ((mine_ref, core), (theirs_ref, 1 - core)):
        for r in range(CY):
            q0, q1, q2 = ref[r], ref[CY + r], ref[2 * CY + r]
            at = LOW * CY * owner + r
            c_ref[pl.ds(at, WIN, stride=CY), :] = one * q0 - two * q1
            r_ref[pl.ds(at, WIN, stride=CY), :] = q0 - one * q1 + two * q2
    control_ref[...] = c_ref[0 : CHAN * CY, :].reshape(CHAN, CY, COLS)
    residual_ref[...] = r_ref[0 : CHAN * CY, :].reshape(CHAN, CY, COLS)


def on_device(
    diffusivity, land_mask, innovation, inverse_variance, owner_ids, cell_index, corner_weights
):
    count_x, count_y = lax.axis_size("gx"), lax.axis_size("gy")
    slots = count_y * CAP
    core = (lax.axis_index("gy") % 2).astype(jnp.int32).reshape(1)
    corners = corner_weights.reshape(4, slots)
    count = owner_ids.shape[0]

    def along_y(value, by):
        pairs = [(i, i + by) for i in range(count_y) if 0 <= i + by < count_y]
        return lax.ppermute(value, "gy", pairs)

    def along_x(value, by):
        return lax.ppermute(value, "gx", [(i, (i + by) % count_x) for i in range(count_x)])

    def across(value):
        return lax.ppermute(value, "gy", [(i, i ^ 1) for i in range(count_y)])

    def exchange(heres, up, down, halo):
        kinds = len(heres)
        tiles = places(halo)[1]
        south, north = along_y(down, 2), along_y(up, -2)
        pack = call(functools.partial(strips_body, halo, kinds), [f32(kinds * tiles, WIN, COLS)] * 2, 10**6)
        west, east = pack(*heres, south, north)
        return south, north, along_x(west, -1), along_x(east, 1)

    field = f32(ROWS, WIN, COLS)
    (chunks,) = call(
        records_body, [f32(slots, COLS)], 10**7, [pltpu.VMEM((2 * FULL, count), jnp.float32)]
    )(owner_ids.reshape(1, count), inverse_variance, innovation)
    mine, mate = call(
        fields_body,
        [f32(CY, WIN, COLS), f32(CY * WIN + 8 * (slots // COLS), COLS)],
        10**6,
        [pltpu.VMEM((FULL * CY, COLS), jnp.float32)],
        1,
    )(core, diffusivity, land_mask, cell_index, corners)
    theirs = across(mate)
    received = lax.all_to_all(chunks, "gy", split_axis=0, concat_axis=0, tiled=True)
    matrix = jax.ShapeDtypeStruct((2, CY * COLS, slots), jnp.bfloat16)
    both = f32(2 * FAR, WIN, COLS)
    d, high, low, weights, g, up, down = call(
        seed_body, [field, matrix, matrix, f32(2, WIN, slots), field, both, both], 10**8, (), 1
    )(core, mine, theirs, cell_index, corners, received)
    wide = (ROWS + 2 * FAR, WIN, 2 * COLS)
    space = [pltpu.VMEM(wide, jnp.float32)] * 2
    south, north, east, west = exchange([g, d], up, down, FAR)
    q0, u0, wide_d, up, down, g = call(
        functools.partial(pair_body, False),
        [field, field, f32(*wide), f32(FAR, WIN, COLS), f32(FAR, WIN, COLS), field],
        2 * 10**8,
        space,
        1,
    )(core, g, south, north, east, west, d, high, low, weights)
    south, north, east, west = exchange([g], up, down, FAR)
    q1, up, down, g, stats = call(
        functools.partial(pair_body, True),
        [field, f32(STEPS, WIN, COLS), f32(STEPS, WIN, COLS), field, f32(count_y, COLS)],
        2 * 10**8,
        space,
        1,
    )(core, g, south, north, east, west, wide_d, high, low, weights, q0, u0)
    stats = lax.all_to_all(stats, "gy", split_axis=0, concat_axis=0, tiled=True)
    (stats,) = call(merge_body, [f32(count_x, COLS)], 10**5)(stats)
    stats = lax.all_to_all(stats, "gx", split_axis=0, concat_axis=0, tiled=True)
    south, north, east, west = exchange([g], up, down, STEPS)
    near = (ROWS + 2 * STEPS, WIN, 2 * COLS)
    mine, mate = call(
        last_body,
        [f32(3 * CY, WIN, COLS)] * 2,
        10**8,
        [pltpu.VMEM(near, jnp.float32)] * 3 + [pltpu.VMEM((ROWS, WIN, COLS), jnp.float32)],
        1,
    )(core, g, south, north, east, west, wide_d, q0, q1)
    theirs = across(mate)
    out = f32(CHAN, CY, COLS)
    return call(
        final_body, [out, out], 10**6, [pltpu.VMEM((FULL * CY, COLS), jnp.float32)] * 2, 1
    )(core, mine, theirs, stats)


def solution(mesh):
    return jax.shard_map(
        on_device,
        mesh=mesh,
        in_specs=(
            P(None, "gy", "gx"),
            P("gy", "gx"),
            P(None, ("gx", "gy")),
            P(None, ("gx", "gy")),
            P(("gx", "gy"), None),
            P(("gx", "gy"), None),
            P(None, ("gx", "gy"), None),
        ),
        out_specs=(P(None, "gy", "gx"), P(None, "gy", "gx")),
        check_vma=False,
    )
```

time: 1030 us -> 174 us (0.17)
  starting transfers between devices: 412 us -> 62.4 us
  blocking collectives: 369 us -> 31.1 us
  waiting for transfers between devices: 165 us -> 32.4 us
  other arithmetic: 49.3 us -> 0 us
  Pallas kernels: 0 us -> 40.6 us
  local copies, waits for them, and re-layouts: 17.7 us -> 5.82 us
    ppermute x100 -> x14, starting transfers between devices: 387 us -> 47.9 us  [the longest x6 23.7 us: along_x(): lax.ppermute(value, 'gx', [(i, (i + by) % count_x) for i in range(count_x)])]
    psum x3 -> x0, blocking collectives: 323 us -> none  [total(): return lax.psum(value, ('gx', 'gy'))]
    ppermute x100 -> x14, waiting for transfers between devices: 147 us -> 28.4 us  [the longest x6 17.8 us: along_y(): return lax.ppermute(value, 'gy', pairs)]
    pallas_call x0 -> x11, Pallas kernels: none -> 40.6 us  [run(): pl.pallas_call(body, out_shape=tuple(outs), in_specs=specs, out_specs=tup...]
    scatter-add x3 -> x0, other arithmetic: 18.6 us -> none  [spread(): flat = flat.at[:, cells.reshape(-1)].add(terms)]
    all_to_all x3 -> x2, blocking collectives: 46.1 us -> 31.1 us  [the longest x1 19.7 us: on_device(): stats = lax.all_to_all(stats, 'gy', split_axis=0, concat_axis=0, tiled=True)]
    all_to_all x2 -> x1, waiting for transfers between devices: 18 us -> 3.95 us  [on_device(): lax.all_to_all(chunks, 'gy', split_axis=0, concat_axis=0, tiled=True)]
    mul x33 -> x0, other arithmetic: 12.2 us -> none  [the longest x25 9.88 us: diffuse_short(): scaled = sroot * field]
  transfers between devices with their start and end apart: 102 -> 15, of which waited for: 77 -> 11; matrix products, arithmetic and copies ran while one was open for 0% -> 0% of each run, Pallas kernels for 0% -> 0%
where the time goes in v1:
time: 174 us; the launch traced here: 173 us
  starting transfers between devices  62.4 us (36%)
  Pallas kernels  40.6 us (23%)
  waiting for transfers between devices  32.4 us (19%)
  blocking collectives  31.1 us (18%)
  local copies, waits for them, and re-layouts  5.82 us (3%)
    pallas_call x11, Pallas kernels, run(): pl.pallas_call(body, out_shape=tuple(outs), in_specs=specs, out_specs=tup...  40.6 us
    ppermute x6, starting transfers between devices, along_x(): lax.ppermute(value, 'gx', [(i, (i + by) % count_x) for i in range(count_x)])  23.7 us
    all_to_all x1, blocking collectives, on_device(): stats = lax.all_to_all(stats, 'gy', split_axis=0, concat_axis=0, tiled=True)  19.7 us
    ppermute x6, waiting for transfers between devices, along_y(): return lax.ppermute(value, 'gy', pairs)  17.8 us
    all_to_all x1, starting transfers between devices, on_device(): lax.all_to_all(chunks, 'gy', split_axis=0, concat_axis=0, tiled=True)  14.6 us
    ppermute x2, starting transfers between devices, across(): return lax.ppermute(value, 'gy', [(i, i ^ 1) for i in range(count_y)])  12.1 us
    ppermute x6, starting transfers between devices, along_y(): return lax.ppermute(value, 'gy', pairs)  12 us
    all_to_all x1, blocking collectives, on_device(): stats = lax.all_to_all(stats, 'gx', split_axis=0, concat_axis=0, tiled=True)  11.5 us
  transfers between devices with their start and end apart: 15, of which 11 were waited for; matrix products, arithmetic and copies ran while one was open for 0% of the time, Pallas kernels for 0%

profile of v1, /device:TPU:1, one launch (start us, length us, event | category | flops | bytes accessed | tf_op | source)
XLA Modules:
  0.0 173.2 jit_solution(929803475319991436)
XLA Ops:
  0.6 0.7 copy-done.1
  1.4 0.7 copy-done.2
  2.1 0.7 copy-done.6
  2.8 1.0 shard_map.87
  3.8 14.6 %all-to-all-start = ((f32[64,4,128]{2,1,0:T(4,128)}), f32[64,4,128]{2,1,0:T(4,128)S(1)}, u32[]{:S(2)}, u32[]{:S(2)}) async-start(f32[64,4,128]{2,1,0:T(4,128)} %bitcast.2), calls=%async_computation | async-start | bytes 262144 | tf_op jit(solution)/shard_map/all_to_all | solution.py:421
  18.4 0.7 copy.16
  19.1 0.9 copy-done
  20.0 0.7 copy-done.3
  20.7 0.7 copy-done.5
  21.4 0.1 shard_map.86
  21.5 2.5 %collective-permute-start = (f32[272,128]{1,0:T(8,128)S(1)}, f32[272,128]{1,0:T(8,128)S(1)}, u32[]{:S(2)}, u32[]{:S(2)}) collective-permute-start(f32[272,128]{1,0:T(8,128)S(1)} %get-tuple-element.31), channel_id=1, source_target_pairs={{0,1},{1,0},{2,3},{3,2},{4,5},{5,4},{6,7},{7,6},{8,9},{9,8},{10,11... | collective-permute-start | bytes 417800 | tf_op jit(solution)/shard_map/ppermute | solution.py:399
  24.0 1.0 collective-permute-done.theirs_ref
  24.9 3.9 %all-to-all-done = f32[64,4,128]{2,1,0:T(4,128)S(1)} async-done(((f32[64,4,128]{2,1,0:T(4,128)}), f32[64,4,128]{2,1,0:T(4,128)S(1)}, u32[]{:S(2)}, u32[]{:S(2)}) %all-to-all-start) | async-done | bytes 131104 | tf_op jit(solution)/shard_map/all_to_all | solution.py:421
  28.9 0.7 copy-done.4
  29.6 0.9 shard_map.88
  30.5 2.9 %collective-permute-start.1 = (f32[20,32,128]{2,1,0:T(8,128)S(1)}, f32[20,32,128]{2,1,0:T(8,128)S(1)}, u32[]{:S(2)}, u32[]{:S(2)}) collective-permute-start(f32[20,32,128]{2,1,0:T(8,128)S(1)} %get-tuple-element.33), channel_id=1, source_target_pairs={{0,2},{1,3},{2,4},{3,5},{4,6},{5,7},{6,8},{7,9},{8,10},{9,11},{10,... | collective-permute-start | bytes 983048 | tf_op jit(solution)/shard_map/ppermute | solution.py:393
  33.5 1.3 collective-permute-start.2
  34.8 5.4 %collective-permute-done.1.refs_2_ = f32[20,32,128]{2,1,0:T(8,128)S(1)} collective-permute-done((f32[20,32,128]{2,1,0:T(8,128)S(1)}, f32[20,32,128]{2,1,0:T(8,128)S(1)}, u32[]{:S(2)}, u32[]{:S(2)}) %collective-permute-start.1) | collective-permute-done | bytes 327712 | tf_op jit(solution)/shard_map/ppermute | solution.py:393
  40.1 3.8 %collective-permute-done.2.refs_3_ = f32[20,32,128]{2,1,0:T(8,128)S(1)} collective-permute-done((f32[20,32,128]{2,1,0:T(8,128)S(1)}, f32[20,32,128]{2,1,0:T(8,128)S(1)}, u32[]{:S(2)}, u32[]{:S(2)}) %collective-permute-start.2) | collective-permute-done | bytes 327712 | tf_op jit(solution)/shard_map/ppermute | solution.py:393
  44.0 0.6 shard_map.89
  44.6 11.2 %collective-permute-start.3 = (f32[6,32,128]{2,1,0:T(8,128)S(1)}, f32[6,32,128]{2,1,0:T(8,128)S(1)}, u32[]{:S(2)}, u32[]{:S(2)}) collective-permute-start(f32[6,32,128]{2,1,0:T(8,128)S(1)} %get-tuple-element.36), channel_id=1, source_target_pairs={{0,704},{64,0},{128,64},{192,128},{256,192},{320,256},{384,320},{4... | collective-permute-start | bytes 294920 | tf_op jit(solution)/shard_map/ppermute | solution.py:396
  55.8 1.9 %collective-permute-start.4 = (f32[6,32,128]{2,1,0:T(8,128)S(1)}, f32[6,32,128]{2,1,0:T(8,128)S(1)}, u32[]{:S(2)}, u32[]{:S(2)}) collective-permute-start(f32[6,32,128]{2,1,0:T(8,128)S(1)} %get-tuple-element.37), channel_id=1, source_target_pairs={{0,64},{64,128},{128,192},{192,256},{256,320},{320,384},{384,448},... | collective-permute-start | bytes 294920 | tf_op jit(solution)/shard_map/ppermute | solution.py:396
  57.8 0.0 collective-permute-done.3.refs_4_
  57.8 4.6 %collective-permute-done.4.refs_5_ = f32[6,32,128]{2,1,0:T(8,128)S(1)} collective-permute-done((f32[6,32,128]{2,1,0:T(8,128)S(1)}, f32[6,32,128]{2,1,0:T(8,128)S(1)}, u32[]{:S(2)}, u32[]{:S(2)}) %collective-permute-start.4) | collective-permute-done | bytes 98336 | tf_op jit(solution)/shard_map/ppermute | solution.py:396
  62.4 15.2 %shard_map.90 = (f32[16,32,128]{2,1,0:T(8,128)S(1)}, f32[16,32,128]{2,1,0:T(8,128)S(1)}, f32[36,32,256]{2,1,0:T(8,128)S(1)}, f32[10,32,128]{2,1,0:T(8,128)S(1)},...) custom-call(s32[1]{0:T(128)} %bitcast.core_ref.refs_0_, f32[16,32,128]{2,1,0:T(8,128)S(1)} %get-tuple-element.32.refs_0_.refs_1_, ...), custom_call_target="tpu_custom_call" | custom-call | flops 200000000 | bytes 5832708 | tf_op jit(solution)/shard_map/pallas_call | solution.py:27
  77.6 2.4 %collective-permute-start.5 = (f32[10,32,128]{2,1,0:T(8,128)S(1)}, f32[10,32,128]{2,1,0:T(8,128)S(1)}, u32[]{:S(2)}, u32[]{:S(2)}) collective-permute-start(f32[10,32,128]{2,1,0:T(8,128)S(1)} %get-tuple-element.42), channel_id=1, source_target_pairs={{0,2},{1,3},{2,4},{3,5},{4,6},{5,7},{6,8},{7,9},{8,10},{9,11},{10,... | collective-permute-start | bytes 491528 | tf_op jit(solution)/shard_map/ppermute | solution.py:393
  80.0 1.3 collective-permute-start.6
  81.3 0.9 collective-permute-done.5.refs_1_.refs_2_
  82.3 3.8 %collective-permute-done.6.refs_2_.refs_3_ = f32[10,32,128]{2,1,0:T(8,128)S(1)} collective-permute-done((f32[10,32,128]{2,1,0:T(8,128)S(1)}, f32[10,32,128]{2,1,0:T(8,128)S(1)}, u32[]{:S(2)}, u32[]{:S(2)}) %collective-permute-start.6) | collective-permute-done | bytes 163872 | tf_op jit(solution)/shard_map/ppermute | solution.py:393
  86.1 0.3 shard_map.91
  86.4 1.9 %collective-permute-start.7 = (f32[3,32,128]{2,1,0:T(8,128)S(1)}, f32[3,32,128]{2,1,0:T(8,128)S(1)}, u32[]{:S(2)}, u32[]{:S(2)}) collective-permute-start(f32[3,32,128]{2,1,0:T(8,128)S(1)} %get-tuple-element.44), channel_id=1, source_target_pairs={{0,704},{64,0},{128,64},{192,128},{256,192},{320,256},{384,320},{4... | collective-permute-start | bytes 147464 | tf_op jit(solution)/shard_map/ppermute | solution.py:396
  88.4 3.4 %collective-permute-start.8 = (f32[3,32,128]{2,1,0:T(8,128)S(1)}, f32[3,32,128]{2,1,0:T(8,128)S(1)}, u32[]{:S(2)}, u32[]{:S(2)}) collective-permute-start(f32[3,32,128]{2,1,0:T(8,128)S(1)} %get-tuple-element.45), channel_id=1, source_target_pairs={{0,64},{64,128},{128,192},{192,256},{256,320},{320,384},{384,448},... | collective-permute-start | bytes 147464 | tf_op jit(solution)/shard_map/ppermute | solution.py:396
  91.7 2.7 %collective-permute-done.8.refs_5_ = f32[3,32,128]{2,1,0:T(8,128)S(1)} collective-permute-done((f32[3,32,128]{2,1,0:T(8,128)S(1)}, f32[3,32,128]{2,1,0:T(8,128)S(1)}, u32[]{:S(2)}, u32[]{:S(2)}) %collective-permute-start.8) | collective-permute-done | bytes 49184 | tf_op jit(solution)/shard_map/ppermute | solution.py:396
  94.4 14.9 %shard_map.92 = (f32[16,32,128]{2,1,0:T(8,128)S(1)}, f32[5,32,128]{2,1,0:T(8,128)S(1)}, f32[5,32,128]{2,1,0:T(8,128)S(1)}, f32[16,32,128]{2,1,0:T(8,128)S(1)}, f32[64,128]{1,0:T(8,128)S(1)}) custom-call(s32[1]{0:T(128)} %bitcast.core_ref.refs_0_, f32[16,32,128]{2,1,0:T(8,128)S(1)} %get-tuple-element.41.refs_0_.refs_1_, ...), custom_call_target="tpu_custom_call" | custom-call | flops 200000000 | bytes 5275652 | tf_op jit(solution)/shard_map/pallas_call | solution.py:27
  109.3 2.8 %collective-permute-start.9 = (f32[5,32,128]{2,1,0:T(8,128)S(1)}, f32[5,32,128]{2,1,0:T(8,128)S(1)}, u32[]{:S(2)}, u32[]{:S(2)}) collective-permute-start(f32[5,32,128]{2,1,0:T(8,128)S(1)} %get-tuple-element.50), channel_id=1, source_target_pairs={{0,2},{1,3},{2,4},{3,5},{4,6},{5,7},{6,8},{7,9},{8,10},{9,11},{10,... | collective-permute-start | bytes 245768 | tf_op jit(solution)/shard_map/ppermute | solution.py:393
  112.1 1.3 collective-permute-start.10
  113.4 0.2 collective-permute-done.9.refs_1_.south_ref
  113.6 3.7 %collective-permute-done.10.refs_2_.north_ref = f32[5,32,128]{2,1,0:T(8,128)S(1)} collective-permute-done((f32[5,32,128]{2,1,0:T(8,128)S(1)}, f32[5,32,128]{2,1,0:T(8,128)S(1)}, u32[]{:S(2)}, u32[]{:S(2)}) %collective-permute-start.10) | collective-permute-done | bytes 81952 | tf_op jit(solution)/shard_map/ppermute | solution.py:393
  117.3 0.3 shard_map.93
  117.6 1.9 %collective-permute-start.11 = (f32[1,32,128]{2,1,0:T(8,128)S(1)}, f32[1,32,128]{2,1,0:T(8,128)S(1)}, u32[]{:S(2)}, u32[]{:S(2)}) collective-permute-start(f32[1,32,128]{2,1,0:T(8,128)S(1)} %get-tuple-element.52), channel_id=1, source_target_pairs={{0,704},{64,0},{128,64},{192,128},{256,192},{320,256},{384,320},{4... | collective-permute-start | bytes 49160 | tf_op jit(solution)/shard_map/ppermute | solution.py:396
  119.5 3.4 %collective-permute-start.12 = (f32[1,32,128]{2,1,0:T(8,128)S(1)}, f32[1,32,128]{2,1,0:T(8,128)S(1)}, u32[]{:S(2)}, u32[]{:S(2)}) collective-permute-start(f32[1,32,128]{2,1,0:T(8,128)S(1)} %get-tuple-element.53), channel_id=1, source_target_pairs={{0,64},{64,128},{128,192},{192,256},{256,320},{320,384},{384,448},... | collective-permute-start | bytes 49160 | tf_op jit(solution)/shard_map/ppermute | solution.py:396
  122.9 2.3 %collective-permute-done.12.west_ref = f32[1,32,128]{2,1,0:T(8,128)S(1)} collective-permute-done((f32[1,32,128]{2,1,0:T(8,128)S(1)}, f32[1,32,128]{2,1,0:T(8,128)S(1)}, u32[]{:S(2)}, u32[]{:S(2)}) %collective-permute-start.12) | collective-permute-done | bytes 16416 | tf_op jit(solution)/shard_map/ppermute | solution.py:396
  125.2 5.7 %shard_map.94 = (f32[24,32,128]{2,1,0:T(8,128)S(1)}, f32[24,32,128]{2,1,0:T(8,128)S(1)}) custom-call(s32[1]{0:T(128)} %bitcast.core_ref.refs_0_, f32[16,32,128]{2,1,0:T(8,128)S(1)} %get-tuple-element.49.refs_0_.here_ref, f32[5,32,128]{2,1,0:T(8,128)S(1)} %collective-permute-done.9.refs_1_.south_ref, ...), custom_call_target="tpu_custom_call" | custom-call | flops 100000000 | bytes 2949124 | tf_op jit(solution)/shard_map/pallas_call | solution.py:27
  130.9 9.6 %collective-permute-start.13 = (f32[24,32,128]{2,1,0:T(8,128)S(1)}, f32[24,32,128]{2,1,0:T(8,128)S(1)}, u32[]{:S(2)}, u32[]{:S(2)}) collective-permute-start(f32[24,32,128]{2,1,0:T(8,128)S(1)} %get-tuple-element.56), channel_id=1, source_target_pairs={{0,1},{1,0},{2,3},{3,2},{4,5},{5,4},{6,7},{7,6},{8,9},{9,8},{10,11... | collective-permute-start | bytes 1179656 | tf_op jit(solution)/shard_map/ppermute | solution.py:399
  140.6 19.7 %all_to_all.33 = f32[64,1,128]{2,1,0:T(1,128)S(1)} all-to-all(f32[64,1,128]{2,1,0:T(1,128)S(1)} %bitcast.21), channel_id=1, replica_groups=mesh['gx'=12,'gy'=64] {'gy'}, dimensions={0} | all-to-all | bytes 65536 | tf_op jit(solution)/shard_map/all_to_all | solution.py:445
  160.2 0.2 shard_map.95
  160.5 11.5 %all_to_all.34 = f32[12,1,128]{2,1,0:T(1,128)S(1)} all-to-all(f32[12,1,128]{2,1,0:T(1,128)S(1)} %copy.10), channel_id=1, replica_groups=mesh['gx'=12,'gy'=64] {'gx'}, dimensions={0} | all-to-all | bytes 12288 | tf_op jit(solution)/shard_map/all_to_all | solution.py:447
  171.9 1.2 shard_map.96
  (12 shorter events, 0.0 us)
Async XLA Ops:
  0.6 0.7 copy-start.1
  1.4 0.7 copy-start.2
  2.1 0.7 copy-start.6
  3.8 25.1 %all-to-all-start = ((f32[64,4,128]{2,1,0:T(4,128)}), f32[64,4,128]{2,1,0:T(4,128)S(1)}, u32[]{:S(2)}, u32[]{:S(2)}) async-start(f32[64,4,128]{2,1,0:T(4,128)} %bitcast.2), calls=%async_computation | async-start | bytes 262144 | tf_op jit(solution)/shard_map/all_to_all | solution.py:421
  19.1 0.9 copy-start
  20.0 0.7 copy-start.3
  20.7 0.7 copy-start.5
  21.5 3.5 %collective-permute-start = (f32[272,128]{1,0:T(8,128)S(1)}, f32[272,128]{1,0:T(8,128)S(1)}, u32[]{:S(2)}, u32[]{:S(2)}) collective-permute-start(f32[272,128]{1,0:T(8,128)S(1)} %get-tuple-element.31), channel_id=1, source_target_pairs={{0,1},{1,0},{2,3},{3,2},{4,5},{5,4},{6,7},{7,6},{8,9},{9,8},{10,11... | collective-permute-start | bytes 417800 | tf_op jit(solution)/shard_map/ppermute | solution.py:399
  28.9 0.7 copy-start.4
  30.5 9.6 %collective-permute-start.1 = (f32[20,32,128]{2,1,0:T(8,128)S(1)}, f32[20,32,128]{2,1,0:T(8,128)S(1)}, u32[]{:S(2)}, u32[]{:S(2)}) collective-permute-start(f32[20,32,128]{2,1,0:T(8,128)S(1)} %get-tuple-element.33), channel_id=1, source_target_pairs={{0,2},{1,3},{2,4},{3,5},{4,6},{5,7},{6,8},{7,9},{8,10},{9,11},{10,... | collective-permute-start | bytes 983048 | tf_op jit(solution)/shard_map/ppermute | solution.py:393
  33.5 10.5 %collective-permute-start.2 = (f32[20,32,128]{2,1,0:T(8,128)S(1)}, f32[20,32,128]{2,1,0:T(8,128)S(1)}, u32[]{:S(2)}, u32[]{:S(2)}) collective-permute-start(f32[20,32,128]{2,1,0:T(8,128)S(1)} %get-tuple-element.34), channel_id=1, source_target_pairs={{2,0},{3,1},{4,2},{5,3},{6,4},{7,5},{8,6},{9,7},{10,8},{11,9},{12,... | collective-permute-start | bytes 983048 | tf_op jit(solution)/shard_map/ppermute | solution.py:393
  44.6 13.2 %collective-permute-start.3 = (f32[6,32,128]{2,1,0:T(8,128)S(1)}, f32[6,32,128]{2,1,0:T(8,128)S(1)}, u32[]{:S(2)}, u32[]{:S(2)}) collective-permute-start(f32[6,32,128]{2,1,0:T(8,128)S(1)} %get-tuple-element.36), channel_id=1, source_target_pairs={{0,704},{64,0},{128,64},{192,128},{256,192},{320,256},{384,320},{4... | collective-permute-start | bytes 294920 | tf_op jit(solution)/shard_map/ppermute | solution.py:396
  55.8 6.6 %collective-permute-start.4 = (f32[6,32,128]{2,1,0:T(8,128)S(1)}, f32[6,32,128]{2,1,0:T(8,128)S(1)}, u32[]{:S(2)}, u32[]{:S(2)}) collective-permute-start(f32[6,32,128]{2,1,0:T(8,128)S(1)} %get-tuple-element.37), channel_id=1, source_target_pairs={{0,64},{64,128},{128,192},{192,256},{256,320},{320,384},{384,448},... | collective-permute-start | bytes 294920 | tf_op jit(solution)/shard_map/ppermute | solution.py:396
  77.6 4.7 %collective-permute-start.5 = (f32[10,32,128]{2,1,0:T(8,128)S(1)}, f32[10,32,128]{2,1,0:T(8,128)S(1)}, u32[]{:S(2)}, u32[]{:S(2)}) collective-permute-start(f32[10,32,128]{2,1,0:T(8,128)S(1)} %get-tuple-element.42), channel_id=1, source_target_pairs={{0,2},{1,3},{2,4},{3,5},{4,6},{5,7},{6,8},{7,9},{8,10},{9,11},{10,... | collective-permute-start | bytes 491528 | tf_op jit(solution)/shard_map/ppermute | solution.py:393
  80.0 6.1 %collective-permute-start.6 = (f32[10,32,128]{2,1,0:T(8,128)S(1)}, f32[10,32,128]{2,1,0:T(8,128)S(1)}, u32[]{:S(2)}, u32[]{:S(2)}) collective-permute-start(f32[10,32,128]{2,1,0:T(8,128)S(1)} %get-tuple-element.43), channel_id=1, source_target_pairs={{2,0},{3,1},{4,2},{5,3},{6,4},{7,5},{8,6},{9,7},{10,8},{11,9},{12,... | collective-permute-start | bytes 491528 | tf_op jit(solution)/shard_map/ppermute | solution.py:393
  86.4 5.3 %collective-permute-start.7 = (f32[3,32,128]{2,1,0:T(8,128)S(1)}, f32[3,32,128]{2,1,0:T(8,128)S(1)}, u32[]{:S(2)}, u32[]{:S(2)}) collective-permute-start(f32[3,32,128]{2,1,0:T(8,128)S(1)} %get-tuple-element.44), channel_id=1, source_target_pairs={{0,704},{64,0},{128,64},{192,128},{256,192},{320,256},{384,320},{4... | collective-permute-start | bytes 147464 | tf_op jit(solution)/shard_map/ppermute | solution.py:396
  88.4 6.0 %collective-permute-start.8 = (f32[3,32,128]{2,1,0:T(8,128)S(1)}, f32[3,32,128]{2,1,0:T(8,128)S(1)}, u32[]{:S(2)}, u32[]{:S(2)}) collective-permute-start(f32[3,32,128]{2,1,0:T(8,128)S(1)} %get-tuple-element.45), channel_id=1, source_target_pairs={{0,64},{64,128},{128,192},{192,256},{256,320},{320,384},{384,448},... | collective-permute-start | bytes 147464 | tf_op jit(solution)/shard_map/ppermute | solution.py:396
  109.3 4.3 %collective-permute-start.9 = (f32[5,32,128]{2,1,0:T(8,128)S(1)}, f32[5,32,128]{2,1,0:T(8,128)S(1)}, u32[]{:S(2)}, u32[]{:S(2)}) collective-permute-start(f32[5,32,128]{2,1,0:T(8,128)S(1)} %get-tuple-element.50), channel_id=1, source_target_pairs={{0,2},{1,3},{2,4},{3,5},{4,6},{5,7},{6,8},{7,9},{8,10},{9,11},{10,... | collective-permute-start | bytes 245768 | tf_op jit(solution)/shard_map/ppermute | solution.py:393
  112.1 5.2 %collective-permute-start.10 = (f32[5,32,128]{2,1,0:T(8,128)S(1)}, f32[5,32,128]{2,1,0:T(8,128)S(1)}, u32[]{:S(2)}, u32[]{:S(2)}) collective-permute-start(f32[5,32,128]{2,1,0:T(8,128)S(1)} %get-tuple-element.51), channel_id=1, source_target_pairs={{2,0},{3,1},{4,2},{5,3},{6,4},{7,5},{8,6},{9,7},{10,8},{11,9},{12,... | collective-permute-start | bytes 245768 | tf_op jit(solution)/shard_map/ppermute | solution.py:393
  117.6 5.3 %collective-permute-start.11 = (f32[1,32,128]{2,1,0:T(8,128)S(1)}, f32[1,32,128]{2,1,0:T(8,128)S(1)}, u32[]{:S(2)}, u32[]{:S(2)}) collective-permute-start(f32[1,32,128]{2,1,0:T(8,128)S(1)} %get-tuple-element.52), channel_id=1, source_target_pairs={{0,704},{64,0},{128,64},{192,128},{256,192},{320,256},{384,320},{4... | collective-permute-start | bytes 49160 | tf_op jit(solution)/shard_map/ppermute | solution.py:396
  119.5 5.7 %collective-permute-start.12 = (f32[1,32,128]{2,1,0:T(8,128)S(1)}, f32[1,32,128]{2,1,0:T(8,128)S(1)}, u32[]{:S(2)}, u32[]{:S(2)}) collective-permute-start(f32[1,32,128]{2,1,0:T(8,128)S(1)} %get-tuple-element.53), channel_id=1, source_target_pairs={{0,64},{64,128},{128,192},{192,256},{256,320},{320,384},{384,448},... | collective-permute-start | bytes 49160 | tf_op jit(solution)/shard_map/ppermute | solution.py:396
  130.9 41.0 %collective-permute-start.13 = (f32[24,32,128]{2,1,0:T(8,128)S(1)}, f32[24,32,128]{2,1,0:T(8,128)S(1)}, u32[]{:S(2)}, u32[]{:S(2)}) collective-permute-start(f32[24,32,128]{2,1,0:T(8,128)S(1)} %get-tuple-element.56), channel_id=1, source_target_pairs={{0,1},{1,0},{2,3},{3,2},{4,5},{5,4},{6,7},{7,6},{8,9},{9,8},{10,11... | collective-permute-start | bytes 1179656 | tf_op jit(solution)/shard_map/ppermute | solution.py:399

commit v2 on v1

--- a/solution.py
+++ b/solution.py
@@ -19,11 +19,11 @@
 FAR = 2 * STEPS
 
 
-def call(body, outs, flops, scratch=(), scalars=0):
+def call(body, outs, flops, scratch=(), scalars=0, source=pltpu.VMEM):
     def run(*args):
         size = sum(a.size * a.dtype.itemsize for a in args) + sum(o.size * o.dtype.itemsize for o in outs)
         specs = [pl.BlockSpec(memory_space=pltpu.SMEM)] * scalars
-        specs += [pl.BlockSpec(memory_space=pltpu.VMEM)] * (len(args) - scalars)
+        specs += [pl.BlockSpec(memory_space=source)] * (len(args) - scalars)
         return pl.pallas_call(
             body,
             out_shape=tuple(outs),
@@ -50,7 +50,35 @@
     return lax.dot_general(a, b, (dims, ((), ())), preferred_element_type=jnp.float32)
 
 
-def records_body(own_ref, inv_ref, inno_ref, out_ref, pad_ref):
+def first_body(core_ref, *refs):
+    ins, (chunk_ref, mine_ref, mate_ref, table_ref), space = refs[:7], refs[7:11], refs[11:]
+    held, pad_ref, field_ref, sems = space[:7], space[7], space[8], space[9]
+    copies = [pltpu.make_async_copy(ins[n], held[n], sems.at[n]) for n in range(7)]
+    for copy in copies:
+        copy.start()
+    own_ref, inv_ref, inno_ref, diff_ref, mask_ref, cell_ref, corner_ref = held
+    for copy in copies:
+        copy.wait()
+    route(own_ref, inv_ref, inno_ref, chunk_ref, pad_ref)
+    core = core_ref[0]
+    slots = cell_ref.shape[1]
+    masked = diff_ref[...] * mask_ref[...].astype(jnp.float32)[None]
+    field_ref[0 : CHAN * CY, :] = masked.reshape(CHAN * CY, COLS)
+    field_ref[CHAN * CY :, :] = jnp.zeros((FULL * CY - CHAN * CY, COLS), jnp.float32)
+    for r in range(CY):
+        at = LOW * CY * core + r
+        mine_ref[r] = field_ref[pl.ds(at, WIN, stride=CY), :]
+        at = LOW * CY * (1 - core) + r
+        mate_ref[r * WIN : (r + 1) * WIN, :] = field_ref[pl.ds(at, WIN, stride=CY), :]
+    base = CY * WIN
+    rows = [cell_ref[...].astype(jnp.float32)] + [corner_ref[n] for n in range(4)]
+    table = jnp.concatenate(rows + [jnp.zeros((3, slots), jnp.float32)], axis=0)
+    table_ref[...] = table
+    for part in range(slots // COLS):
+        mate_ref[base + 8 * part : base + 8 * part + 8, :] = table[:, part * COLS : (part + 1) * COLS]
+
+
+def route(own_ref, inv_ref, inno_ref, out_ref, pad_ref):
     count = own_ref.shape[1]
     tiles = out_ref.shape[0] // CAP
     chips = tiles // 2
@@ -90,25 +118,6 @@
             out_ref[pl.ds(core * CAP + r, chips, stride=2 * CAP), :] = total[r * chips : (r + 1) * chips]
 
 
-def fields_body(core_ref, diff_ref, mask_ref, cell_ref, corner_ref, mine_ref, mate_ref, pad_ref):
-    core = core_ref[0]
-    slots = cell_ref.shape[1]
-    masked = diff_ref[...] * mask_ref[...].astype(jnp.float32)[None]
-    pad_ref[0 : CHAN * CY, :] = masked.reshape(CHAN * CY, COLS)
-    pad_ref[CHAN * CY :, :] = jnp.zeros((FULL * CY - CHAN * CY, COLS), jnp.float32)
-    for r in range(CY):
-        at = LOW * CY * core + r
-        mine_ref[r] = pad_ref[pl.ds(at, WIN, stride=CY), :]
-        at = LOW * CY * (1 - core) + r
-        mate_ref[r * WIN : (r + 1) * WIN, :] = pad_ref[pl.ds(at, WIN, stride=CY), :]
-    base = CY * WIN
-    table = jnp.concatenate(
-        [cell_ref[...].astype(jnp.float32), corner_ref[...], jnp.zeros((3, slots), jnp.float32)], axis=0
-    )
-    for part in range(slots // COLS):
-        mate_ref[base + 8 * part : base + 8 * part + 8, :] = table[:, part * COLS : (part + 1) * COLS]
-
-
 def adjoint(misfits, high_ref, low_ref, store):
     for tile in range(2):
         high, low = split(misfits[tile])
@@ -119,17 +128,15 @@
             store(tile * CY + r, flat[:, r * COLS : (r + 1) * COLS])
 
 
-def seed_body(core_ref, mine_ref, theirs_ref, cell_ref, corner_ref, rec_ref, *outs):
+def seed_body(core_ref, mine_ref, theirs_ref, table_ref, rec_ref, *outs):
     d_ref, high_ref, low_ref, weight_ref, g_ref, up_ref, down_ref = outs
     core = core_ref[0]
-    slots = cell_ref.shape[1]
+    slots = table_ref.shape[1]
     base = CY * WIN
     other = jnp.concatenate(
         [theirs_ref[base + 8 * part : base + 8 * part + 8, :] for part in range(slots // COLS)], axis=1
     )
-    here = jnp.concatenate(
-        [cell_ref[...].astype(jnp.float32), corner_ref[...], jnp.zeros((3, slots), jnp.float32)], axis=0
-    )
+    here = table_ref[...]
     columns = lax.broadcasted_iota(jnp.int32, (COLS, slots), 0)
     slot_t = rec_ref[...].T
     targets = []
@@ -232,7 +239,9 @@
         dst[row] = now + d_ref[row] * (before + after + beside - 4.0 * now)
         return now, after
 
-    lax.fori_loop(low, high, body, (src[low - 1], src[low]), unroll=2)
+    carry = (src[low - 1], src[low])
+    for row in range(low, high):
+        carry = body(row, carry)
 
 
 def unscale(value, d):
@@ -385,7 +394,6 @@
     count_x, count_y = lax.axis_size("gx"), lax.axis_size("gy")
     slots = count_y * CAP
     core = (lax.axis_index("gy") % 2).astype(jnp.int32).reshape(1)
-    corners = corner_weights.reshape(4, slots)
     count = owner_ids.shape[0]
 
     def along_y(value, by):
@@ -398,32 +406,36 @@
     def across(value):
         return lax.ppermute(value, "gy", [(i, i ^ 1) for i in range(count_y)])
 
-    def exchange(heres, up, down, halo):
+    def exchange(heres, up, down, halo, *after):
         kinds = len(heres)
         tiles = places(halo)[1]
         south, north = along_y(down, 2), along_y(up, -2)
         pack = call(functools.partial(strips_body, halo, kinds), [f32(kinds * tiles, WIN, COLS)] * 2, 10**6)
         west, east = pack(*heres, south, north)
-        return south, north, along_x(west, -1), along_x(east, 1)
+        west, east, *after = lax.optimization_barrier((west, east, *after))
+        return south, north, along_x(west, -1), along_x(east, 1), *after
 
     field = f32(ROWS, WIN, COLS)
-    (chunks,) = call(
-        records_body, [f32(slots, COLS)], 10**7, [pltpu.VMEM((2 * FULL, count), jnp.float32)]
-    )(owner_ids.reshape(1, count), inverse_variance, innovation)
-    mine, mate = call(
-        fields_body,
-        [f32(CY, WIN, COLS), f32(CY * WIN + 8 * (slots // COLS), COLS)],
-        10**6,
-        [pltpu.VMEM((FULL * CY, COLS), jnp.float32)],
+    ins = [
+        owner_ids.reshape(1, count), inverse_variance, innovation, diffusivity, land_mask, cell_index, corner_weights
+    ]
+    space = [pltpu.VMEM(x.shape, x.dtype) for x in ins]
+    space += [pltpu.VMEM((2 * FULL, count), jnp.float32), pltpu.VMEM((FULL * CY, COLS), jnp.float32)]
+    chunks, mine, mate, table = call(
+        first_body,
+        [f32(slots, COLS), f32(CY, WIN, COLS), f32(CY * WIN + 8 * (slots // COLS), COLS), f32(8, slots)],
+        10**7,
+        space + [pltpu.SemaphoreType.DMA((len(ins),))],
         1,
-    )(core, diffusivity, land_mask, cell_index, corners)
+        pltpu.HBM,
+    )(core, *(pltpu.with_memory_space_constraint(x, pltpu.HBM) for x in ins))
     theirs = across(mate)
     received = lax.all_to_all(chunks, "gy", split_axis=0, concat_axis=0, tiled=True)
     matrix = jax.ShapeDtypeStruct((2, CY * COLS, slots), jnp.bfloat16)
     both = f32(2 * FAR, WIN, COLS)
     d, high, low, weights, g, up, down = call(
         seed_body, [field, matrix, matrix, f32(2, WIN, slots), field, both, both], 10**8, (), 1
-    )(core, mine, theirs, cell_index, corners, received)
+    )(core, mine, theirs, table, received)
     wide = (ROWS + 2 * FAR, WIN, 2 * COLS)
     space = [pltpu.VMEM(wide, jnp.float32)] * 2
     south, north, east, west = exchange([g, d], up, down, FAR)
@@ -444,8 +456,8 @@
     )(core, g, south, north, east, west, wide_d, high, low, weights, q0, u0)
     stats = lax.all_to_all(stats, "gy", split_axis=0, concat_axis=0, tiled=True)
     (stats,) = call(merge_body, [f32(count_x, COLS)], 10**5)(stats)
+    south, north, east, west, stats = exchange([g], up, down, STEPS, stats)
     stats = lax.all_to_all(stats, "gx", split_axis=0, concat_axis=0, tiled=True)
-    south, north, east, west = exchange([g], up, down, STEPS)
     near = (ROWS + 2 * STEPS, WIN, 2 * COLS)
     mine, mate = call(
         last_body,
@@ -454,6 +466,7 @@
         [pltpu.VMEM(near, jnp.float32)] * 3 + [pltpu.VMEM((ROWS, WIN, COLS), jnp.float32)],
         1,
     )(core, g, south, north, east, west, wide_d, q0, q1)
+    mate, stats = lax.optimization_barrier((mate, stats))
     theirs = across(mate)
     out = f32(CHAN, CY, COLS)
     return call(

time: 174 us -> 145 us (0.83)
  Pallas kernels: 40.6 us -> 19.1 us
  blocking collectives: 31.1 us -> 25.5 us
  local copies, waits for them, and re-layouts: 5.82 us -> 0.6 us
  waiting for transfers between devices: 32.4 us -> 37.2 us
    pallas_call x11 -> x10, Pallas kernels: 40.6 us -> 19.1 us  [run(): pl.pallas_call(body, out_shape=tuple(outs), in_specs=specs, out_specs=tup...]
    all_to_all x1 -> x0, blocking collectives: 11.5 us -> none  [on_device(): stats = lax.all_to_all(stats, 'gx', split_axis=0, concat_axis=0, tiled=True)]
    all_to_all x0 -> x1, waiting for transfers between devices: none -> 6.81 us  [on_device(): stats = lax.all_to_all(stats, 'gx', split_axis=0, concat_axis=0, tiled=True)]
    all_to_all x1, blocking collectives: 19.7 us -> 25.5 us  [on_device(): stats = lax.all_to_all(stats, 'gy', split_axis=0, concat_axis=0, tiled=True)]
    unnamed x16 -> x1, local copies, waits for them, and re-layouts: 5.81 us -> 0.01 us
    ppermute x2, starting transfers between devices: 12.1 us -> 6.75 us  [across(): return lax.ppermute(value, 'gy', [(i, i ^ 1) for i in range(count_y)])]
    ppermute x6, waiting for transfers between devices: 17.8 us -> 13.9 us  [along_y(): return lax.ppermute(value, 'gy', pairs)]
    all_to_all x0 -> x1, starting transfers between devices: none -> 3.71 us  [on_device(): stats = lax.all_to_all(stats, 'gx', split_axis=0, concat_axis=0, tiled=True)]
  transfers between devices with their start and end apart: 15 -> 16, of which waited for: 11 -> 10; matrix products, arithmetic and copies ran while one was open for 0% -> 0% of each run, Pallas kernels for 0% -> 2%
where the time goes in v2:
time: 145 us; the launch traced here: 144 us
  starting transfers between devices  60.9 us (42%)
  waiting for transfers between devices  37.2 us (26%)
  blocking collectives  25.5 us (18%)
  Pallas kernels  19.1 us (13%)
    all_to_all x1, blocking collectives, on_device(): stats = lax.all_to_all(stats, 'gy', split_axis=0, concat_axis=0, tiled=True)  25.5 us
    ppermute x6, starting transfers between devices, along_x(): lax.ppermute(value, 'gx', [(i, (i + by) % count_x) for i in range(count_x)])  23.9 us
    pallas_call x10, Pallas kernels, run(): pl.pallas_call(body, out_shape=tuple(outs), in_specs=specs, out_specs=tup...  19.1 us
    all_to_all x1, starting transfers between devices, on_device(): lax.all_to_all(chunks, 'gy', split_axis=0, concat_axis=0, tiled=True)  14.6 us
    ppermute x6, waiting for transfers between devices, along_y(): return lax.ppermute(value, 'gy', pairs)  13.9 us
    ppermute x6, starting transfers between devices, along_y(): return lax.ppermute(value, 'gy', pairs)  12 us
    ppermute x6, waiting for transfers between devices, along_x(): lax.ppermute(value, 'gx', [(i, (i + by) % count_x) for i in range(count_x)])  7.13 us
    all_to_all x1, waiting for transfers between devices, on_device(): lax.all_to_all(chunks, 'gy', split_axis=0, concat_axis=0, tiled=True)  7.02 us
  transfers between devices with their start and end apart: 16, of which 10 were waited for; matrix products, arithmetic and copies ran while one was open for 0% of the time, Pallas kernels for 2%

profile of v2, /device:TPU:1, one launch (start us, length us, event | category | flops | bytes accessed | tf_op | source)
XLA Modules:
  0.0 144.2 jit_solution(11490261668691627696)
XLA Ops:
  0.6 2.1 %shard_map.86 = (f32[256,128]{1,0:T(8,128)}, f32[8,32,128]{2,1,0:T(8,128)S(1)}, f32[272,128]{1,0:T(8,128)S(1)}, f32[8,256]{1,0:T(8,128)S(1)}) custom-call(s32[1]{0:T(128)} %bitcast.core_ref.refs_0_, s32[1,128]{1,0:T(1,128)} %bitcast.17, f32[50,128]{1,0:T(8,128)} %refs_1_.1, f32[50,128]{1,0:T(8,128)} %refs_2_.1, f32[50,8,128]{2,1,0:T(8,128)} %refs_3_.1, ...), custom_call_target="tpu_custom_call" | custom-call | flops 10000000 | bytes 675332 | tf_op jit(solution)/shard_map/pallas_call | solution.py:27
  2.8 14.6 %all-to-all-start = ((f32[64,4,128]{2,1,0:T(4,128)}), f32[64,4,128]{2,1,0:T(4,128)S(1)}, u32[]{:S(2)}, u32[]{:S(2)}) async-start(f32[64,4,128]{2,1,0:T(4,128)} %bitcast.2), calls=%async_computation | async-start | bytes 262144 | tf_op jit(solution)/shard_map/all_to_all | solution.py:433
  17.3 2.5 %collective-permute-start = (f32[272,128]{1,0:T(8,128)S(1)}, f32[272,128]{1,0:T(8,128)S(1)}, u32[]{:S(2)}, u32[]{:S(2)}) collective-permute-start(f32[272,128]{1,0:T(8,128)S(1)} %get-tuple-element.38), channel_id=1, source_target_pairs={{0,1},{1,0},{2,3},{3,2},{4,5},{5,4},{6,7},{7,6},{8,9},{9,8},{10,11... | collective-permute-start | bytes 417800 | tf_op jit(solution)/shard_map/ppermute | solution.py:407
  19.8 1.0 collective-permute-done.theirs_ref
  20.8 7.0 %all-to-all-done = f32[64,4,128]{2,1,0:T(4,128)S(1)} async-done(((f32[64,4,128]{2,1,0:T(4,128)}), f32[64,4,128]{2,1,0:T(4,128)S(1)}, u32[]{:S(2)}, u32[]{:S(2)}) %all-to-all-start) | async-done | bytes 131104 | tf_op jit(solution)/shard_map/all_to_all | solution.py:433
  27.8 0.9 shard_map.87
  28.8 2.9 %collective-permute-start.1 = (f32[20,32,128]{2,1,0:T(8,128)S(1)}, f32[20,32,128]{2,1,0:T(8,128)S(1)}, u32[]{:S(2)}, u32[]{:S(2)}) collective-permute-start(f32[20,32,128]{2,1,0:T(8,128)S(1)} %get-tuple-element.42), channel_id=1, source_target_pairs={{0,2},{1,3},{2,4},{3,5},{4,6},{5,7},{6,8},{7,9},{8,10},{9,11},{10,... | collective-permute-start | bytes 983048 | tf_op jit(solution)/shard_map/ppermute | solution.py:401
  31.7 1.3 collective-permute-start.2
  33.0 5.4 %collective-permute-done.1.refs_2_ = f32[20,32,128]{2,1,0:T(8,128)S(1)} collective-permute-done((f32[20,32,128]{2,1,0:T(8,128)S(1)}, f32[20,32,128]{2,1,0:T(8,128)S(1)}, u32[]{:S(2)}, u32[]{:S(2)}) %collective-permute-start.1) | collective-permute-done | bytes 327712 | tf_op jit(solution)/shard_map/ppermute | solution.py:401
  38.4 3.8 %collective-permute-done.2.refs_3_ = f32[20,32,128]{2,1,0:T(8,128)S(1)} collective-permute-done((f32[20,32,128]{2,1,0:T(8,128)S(1)}, f32[20,32,128]{2,1,0:T(8,128)S(1)}, u32[]{:S(2)}, u32[]{:S(2)}) %collective-permute-start.2) | collective-permute-done | bytes 327712 | tf_op jit(solution)/shard_map/ppermute | solution.py:401
  42.2 0.6 shard_map.88
  42.8 11.3 %collective-permute-start.3 = (f32[6,32,128]{2,1,0:T(8,128)S(1)}, f32[6,32,128]{2,1,0:T(8,128)S(1)}, u32[]{:S(2)}, u32[]{:S(2)}) collective-permute-start(f32[6,32,128]{2,1,0:T(8,128)S(1)} %get-tuple-element.45), channel_id=1, source_target_pairs={{0,704},{64,0},{128,64},{192,128},{256,192},{320,256},{384,320},{4... | collective-permute-start | bytes 294920 | tf_op jit(solution)/shard_map/ppermute | solution.py:404
  54.1 1.9 %collective-permute-start.4 = (f32[6,32,128]{2,1,0:T(8,128)S(1)}, f32[6,32,128]{2,1,0:T(8,128)S(1)}, u32[]{:S(2)}, u32[]{:S(2)}) collective-permute-start(f32[6,32,128]{2,1,0:T(8,128)S(1)} %get-tuple-element.46), channel_id=1, source_target_pairs={{0,64},{64,128},{128,192},{192,256},{256,320},{320,384},{384,448},... | collective-permute-start | bytes 294920 | tf_op jit(solution)/shard_map/ppermute | solution.py:404
  56.0 0.0 collective-permute-done.3.refs_4_
  56.0 4.6 %collective-permute-done.4.refs_5_ = f32[6,32,128]{2,1,0:T(8,128)S(1)} collective-permute-done((f32[6,32,128]{2,1,0:T(8,128)S(1)}, f32[6,32,128]{2,1,0:T(8,128)S(1)}, u32[]{:S(2)}, u32[]{:S(2)}) %collective-permute-start.4) | collective-permute-done | bytes 98336 | tf_op jit(solution)/shard_map/ppermute | solution.py:404
  60.6 5.8 %shard_map.89 = (f32[16,32,128]{2,1,0:T(8,128)S(1)}, f32[16,32,128]{2,1,0:T(8,128)S(1)}, f32[36,32,256]{2,1,0:T(8,128)S(1)}, f32[10,32,128]{2,1,0:T(8,128)S(1)},...) custom-call(s32[1]{0:T(128)} %bitcast.core_ref.refs_0_, f32[16,32,128]{2,1,0:T(8,128)S(1)} %get-tuple-element.41.refs_0_.refs_1_, ...), custom_call_target="tpu_custom_call" | custom-call | flops 200000000 | bytes 5832708 | tf_op jit(solution)/shard_map/pallas_call | solution.py:27
  66.5 2.4 %collective-permute-start.5 = (f32[10,32,128]{2,1,0:T(8,128)S(1)}, f32[10,32,128]{2,1,0:T(8,128)S(1)}, u32[]{:S(2)}, u32[]{:S(2)}) collective-permute-start(f32[10,32,128]{2,1,0:T(8,128)S(1)} %get-tuple-element.51), channel_id=1, source_target_pairs={{0,2},{1,3},{2,4},{3,5},{4,6},{5,7},{6,8},{7,9},{8,10},{9,11},{10,... | collective-permute-start | bytes 491528 | tf_op jit(solution)/shard_map/ppermute | solution.py:401
  68.9 1.3 collective-permute-start.6
  70.2 0.9 collective-permute-done.5.refs_1_.refs_2_
  71.1 3.8 %collective-permute-done.6.refs_2_.refs_3_ = f32[10,32,128]{2,1,0:T(8,128)S(1)} collective-permute-done((f32[10,32,128]{2,1,0:T(8,128)S(1)}, f32[10,32,128]{2,1,0:T(8,128)S(1)}, u32[]{:S(2)}, u32[]{:S(2)}) %collective-permute-start.6) | collective-permute-done | bytes 163872 | tf_op jit(solution)/shard_map/ppermute | solution.py:401
  74.9 0.3 shard_map.90
  75.3 1.9 %collective-permute-start.7 = (f32[3,32,128]{2,1,0:T(8,128)S(1)}, f32[3,32,128]{2,1,0:T(8,128)S(1)}, u32[]{:S(2)}, u32[]{:S(2)}) collective-permute-start(f32[3,32,128]{2,1,0:T(8,128)S(1)} %get-tuple-element.53), channel_id=1, source_target_pairs={{0,704},{64,0},{128,64},{192,128},{256,192},{320,256},{384,320},{4... | collective-permute-start | bytes 147464 | tf_op jit(solution)/shard_map/ppermute | solution.py:404
  77.2 3.5 %collective-permute-start.8 = (f32[3,32,128]{2,1,0:T(8,128)S(1)}, f32[3,32,128]{2,1,0:T(8,128)S(1)}, u32[]{:S(2)}, u32[]{:S(2)}) collective-permute-start(f32[3,32,128]{2,1,0:T(8,128)S(1)} %get-tuple-element.54), channel_id=1, source_target_pairs={{0,64},{64,128},{128,192},{192,256},{256,320},{320,384},{384,448},... | collective-permute-start | bytes 147464 | tf_op jit(solution)/shard_map/ppermute | solution.py:404
  80.8 0.0 collective-permute-done.7.refs_4_
  80.8 2.5 %collective-permute-done.8.refs_5_ = f32[3,32,128]{2,1,0:T(8,128)S(1)} collective-permute-done((f32[3,32,128]{2,1,0:T(8,128)S(1)}, f32[3,32,128]{2,1,0:T(8,128)S(1)}, u32[]{:S(2)}, u32[]{:S(2)}) %collective-permute-start.8) | collective-permute-done | bytes 49184 | tf_op jit(solution)/shard_map/ppermute | solution.py:404
  83.2 5.6 %shard_map.91 = (f32[16,32,128]{2,1,0:T(8,128)S(1)}, f32[5,32,128]{2,1,0:T(8,128)S(1)}, f32[5,32,128]{2,1,0:T(8,128)S(1)}, f32[16,32,128]{2,1,0:T(8,128)S(1)}, f32[64,128]{1,0:T(8,128)S(1)}) custom-call(s32[1]{0:T(128)} %bitcast.core_ref.refs_0_, f32[16,32,128]{2,1,0:T(8,128)S(1)} %get-tuple-element.50.refs_0_.refs_1_, ...), custom_call_target="tpu_custom_call" | custom-call | flops 200000000 | bytes 5275652 | tf_op jit(solution)/shard_map/pallas_call | solution.py:27
  88.9 2.8 %collective-permute-start.9 = (f32[5,32,128]{2,1,0:T(8,128)S(1)}, f32[5,32,128]{2,1,0:T(8,128)S(1)}, u32[]{:S(2)}, u32[]{:S(2)}) collective-permute-start(f32[5,32,128]{2,1,0:T(8,128)S(1)} %get-tuple-element.59), channel_id=1, source_target_pairs={{0,2},{1,3},{2,4},{3,5},{4,6},{5,7},{6,8},{7,9},{8,10},{9,11},{10,... | collective-permute-start | bytes 245768 | tf_op jit(solution)/shard_map/ppermute | solution.py:401
  91.6 1.3 collective-permute-start.10
  92.9 25.5 %all_to_all.34 = f32[64,1,128]{2,1,0:T(1,128)S(1)} all-to-all(f32[64,1,128]{2,1,0:T(1,128)S(1)} %bitcast.16), channel_id=1, replica_groups=mesh['gx'=12,'gy'=64] {'gy'}, dimensions={0} | all-to-all | bytes 65536 | tf_op jit(solution)/shard_map/all_to_all | solution.py:457
  118.4 0.2 shard_map.93
  118.7 0.0 collective-permute-done.9.refs_1_.south_ref
  118.7 0.0 collective-permute-done.10.refs_2_.north_ref
  118.7 0.3 shard_map.92
  118.9 1.9 %collective-permute-start.11 = (f32[1,32,128]{2,1,0:T(8,128)S(1)}, f32[1,32,128]{2,1,0:T(8,128)S(1)}, u32[]{:S(2)}, u32[]{:S(2)}) collective-permute-start(f32[1,32,128]{2,1,0:T(8,128)S(1)} %get-tuple-element.64), channel_id=1, source_target_pairs={{0,704},{64,0},{128,64},{192,128},{256,192},{320,256},{384,320},{4... | collective-permute-start | bytes 49160 | tf_op jit(solution)/shard_map/ppermute | solution.py:404
  120.9 3.4 %collective-permute-start.12 = (f32[1,32,128]{2,1,0:T(8,128)S(1)}, f32[1,32,128]{2,1,0:T(8,128)S(1)}, u32[]{:S(2)}, u32[]{:S(2)}) collective-permute-start(f32[1,32,128]{2,1,0:T(8,128)S(1)} %get-tuple-element.65), channel_id=1, source_target_pairs={{0,64},{64,128},{128,192},{192,256},{256,320},{320,384},{384,448},... | collective-permute-start | bytes 49160 | tf_op jit(solution)/shard_map/ppermute | solution.py:404
  124.2 0.6 copy.10
  124.8 3.7 %all-to-all-start.2 = ((f32[12,1,128]{2,1,0:T(1,128)}), f32[12,1,128]{2,1,0:T(1,128)S(1)}, u32[]{:S(2)}, u32[]{:S(2)}) async-start(f32[12,1,128]{2,1,0:T(1,128)} %copy.10), calls=%async_computation.2 | async-start | bytes 12288 | tf_op jit(solution)/shard_map/all_to_all | solution.py:460
  128.6 0.0 collective-permute-done.11.east_ref
  128.6 0.0 collective-permute-done.12.west_ref
  128.6 2.0 %shard_map.94 = (f32[24,32,128]{2,1,0:T(8,128)S(1)}, f32[24,32,128]{2,1,0:T(8,128)S(1)}) custom-call(s32[1]{0:T(128)} %bitcast.core_ref.refs_0_, f32[16,32,128]{2,1,0:T(8,128)S(1)} %get-tuple-element.58.refs_0_.here_ref, f32[5,32,128]{2,1,0:T(8,128)S(1)} %collective-permute-done.9.refs_1_.south_ref, ...), custom_call_target="tpu_custom_call" | custom-call | flops 100000000 | bytes 2949124 | tf_op jit(solution)/shard_map/pallas_call | solution.py:27
  130.6 6.8 %all-to-all-done.2 = f32[12,1,128]{2,1,0:T(1,128)S(1)} async-done(((f32[12,1,128]{2,1,0:T(1,128)}), f32[12,1,128]{2,1,0:T(1,128)S(1)}, u32[]{:S(2)}, u32[]{:S(2)}) %all-to-all-start.2) | async-done | bytes 6176 | tf_op jit(solution)/shard_map/all_to_all | solution.py:460
  137.4 4.3 %collective-permute-start.13 = (f32[24,32,128]{2,1,0:T(8,128)S(1)}, f32[24,32,128]{2,1,0:T(8,128)S(1)}, u32[]{:S(2)}, u32[]{:S(2)}) collective-permute-start(f32[24,32,128]{2,1,0:T(8,128)S(1)} %get-tuple-element.70), channel_id=1, source_target_pairs={{0,1},{1,0},{2,3},{3,2},{4,5},{5,4},{6,7},{7,6},{8,9},{9,8},{10,11... | collective-permute-start | bytes 1179656 | tf_op jit(solution)/shard_map/ppermute | solution.py:407
  141.7 1.3 collective-permute-done.13.theirs_ref
  143.0 1.2 shard_map.95
  (1 shorter events, 0.0 us)
Async XLA Ops:
  2.8 25.1 %all-to-all-start = ((f32[64,4,128]{2,1,0:T(4,128)}), f32[64,4,128]{2,1,0:T(4,128)S(1)}, u32[]{:S(2)}, u32[]{:S(2)}) async-start(f32[64,4,128]{2,1,0:T(4,128)} %bitcast.2), calls=%async_computation | async-start | bytes 262144 | tf_op jit(solution)/shard_map/all_to_all | solution.py:433
  17.3 3.5 %collective-permute-start = (f32[272,128]{1,0:T(8,128)S(1)}, f32[272,128]{1,0:T(8,128)S(1)}, u32[]{:S(2)}, u32[]{:S(2)}) collective-permute-start(f32[272,128]{1,0:T(8,128)S(1)} %get-tuple-element.38), channel_id=1, source_target_pairs={{0,1},{1,0},{2,3},{3,2},{4,5},{5,4},{6,7},{7,6},{8,9},{9,8},{10,11... | collective-permute-start | bytes 417800 | tf_op jit(solution)/shard_map/ppermute | solution.py:407
  28.8 9.6 %collective-permute-start.1 = (f32[20,32,128]{2,1,0:T(8,128)S(1)}, f32[20,32,128]{2,1,0:T(8,128)S(1)}, u32[]{:S(2)}, u32[]{:S(2)}) collective-permute-start(f32[20,32,128]{2,1,0:T(8,128)S(1)} %get-tuple-element.42), channel_id=1, source_target_pairs={{0,2},{1,3},{2,4},{3,5},{4,6},{5,7},{6,8},{7,9},{8,10},{9,11},{10,... | collective-permute-start | bytes 983048 | tf_op jit(solution)/shard_map/ppermute | solution.py:401
  31.7 10.5 %collective-permute-start.2 = (f32[20,32,128]{2,1,0:T(8,128)S(1)}, f32[20,32,128]{2,1,0:T(8,128)S(1)}, u32[]{:S(2)}, u32[]{:S(2)}) collective-permute-start(f32[20,32,128]{2,1,0:T(8,128)S(1)} %get-tuple-element.43), channel_id=1, source_target_pairs={{2,0},{3,1},{4,2},{5,3},{6,4},{7,5},{8,6},{9,7},{10,8},{11,9},{12,... | collective-permute-start | bytes 983048 | tf_op jit(solution)/shard_map/ppermute | solution.py:401
  42.8 13.2 %collective-permute-start.3 = (f32[6,32,128]{2,1,0:T(8,128)S(1)}, f32[6,32,128]{2,1,0:T(8,128)S(1)}, u32[]{:S(2)}, u32[]{:S(2)}) collective-permute-start(f32[6,32,128]{2,1,0:T(8,128)S(1)} %get-tuple-element.45), channel_id=1, source_target_pairs={{0,704},{64,0},{128,64},{192,128},{256,192},{320,256},{384,320},{4... | collective-permute-start | bytes 294920 | tf_op jit(solution)/shard_map/ppermute | solution.py:404
  54.1 6.6 %collective-permute-start.4 = (f32[6,32,128]{2,1,0:T(8,128)S(1)}, f32[6,32,128]{2,1,0:T(8,128)S(1)}, u32[]{:S(2)}, u32[]{:S(2)}) collective-permute-start(f32[6,32,128]{2,1,0:T(8,128)S(1)} %get-tuple-element.46), channel_id=1, source_target_pairs={{0,64},{64,128},{128,192},{192,256},{256,320},{320,384},{384,448},... | collective-permute-start | bytes 294920 | tf_op jit(solution)/shard_map/ppermute | solution.py:404
  66.5 4.6 %collective-permute-start.5 = (f32[10,32,128]{2,1,0:T(8,128)S(1)}, f32[10,32,128]{2,1,0:T(8,128)S(1)}, u32[]{:S(2)}, u32[]{:S(2)}) collective-permute-start(f32[10,32,128]{2,1,0:T(8,128)S(1)} %get-tuple-element.51), channel_id=1, source_target_pairs={{0,2},{1,3},{2,4},{3,5},{4,6},{5,7},{6,8},{7,9},{8,10},{9,11},{10,... | collective-permute-start | bytes 491528 | tf_op jit(solution)/shard_map/ppermute | solution.py:401
  68.9 6.1 %collective-permute-start.6 = (f32[10,32,128]{2,1,0:T(8,128)S(1)}, f32[10,32,128]{2,1,0:T(8,128)S(1)}, u32[]{:S(2)}, u32[]{:S(2)}) collective-permute-start(f32[10,32,128]{2,1,0:T(8,128)S(1)} %get-tuple-element.52), channel_id=1, source_target_pairs={{2,0},{3,1},{4,2},{5,3},{6,4},{7,5},{8,6},{9,7},{10,8},{11,9},{12,... | collective-permute-start | bytes 491528 | tf_op jit(solution)/shard_map/ppermute | solution.py:401
  75.3 5.5 %collective-permute-start.7 = (f32[3,32,128]{2,1,0:T(8,128)S(1)}, f32[3,32,128]{2,1,0:T(8,128)S(1)}, u32[]{:S(2)}, u32[]{:S(2)}) collective-permute-start(f32[3,32,128]{2,1,0:T(8,128)S(1)} %get-tuple-element.53), channel_id=1, source_target_pairs={{0,704},{64,0},{128,64},{192,128},{256,192},{320,256},{384,320},{4... | collective-permute-start | bytes 147464 | tf_op jit(solution)/shard_map/ppermute | solution.py:404
  77.2 6.0 %collective-permute-start.8 = (f32[3,32,128]{2,1,0:T(8,128)S(1)}, f32[3,32,128]{2,1,0:T(8,128)S(1)}, u32[]{:S(2)}, u32[]{:S(2)}) collective-permute-start(f32[3,32,128]{2,1,0:T(8,128)S(1)} %get-tuple-element.54), channel_id=1, source_target_pairs={{0,64},{64,128},{128,192},{192,256},{256,320},{320,384},{384,448},... | collective-permute-start | bytes 147464 | tf_op jit(solution)/shard_map/ppermute | solution.py:404
  88.9 29.8 %collective-permute-start.9 = (f32[5,32,128]{2,1,0:T(8,128)S(1)}, f32[5,32,128]{2,1,0:T(8,128)S(1)}, u32[]{:S(2)}, u32[]{:S(2)}) collective-permute-start(f32[5,32,128]{2,1,0:T(8,128)S(1)} %get-tuple-element.59), channel_id=1, source_target_pairs={{0,2},{1,3},{2,4},{3,5},{4,6},{5,7},{6,8},{7,9},{8,10},{9,11},{10,... | collective-permute-start | bytes 245768 | tf_op jit(solution)/shard_map/ppermute | solution.py:401
  91.6 27.0 %collective-permute-start.10 = (f32[5,32,128]{2,1,0:T(8,128)S(1)}, f32[5,32,128]{2,1,0:T(8,128)S(1)}, u32[]{:S(2)}, u32[]{:S(2)}) collective-permute-start(f32[5,32,128]{2,1,0:T(8,128)S(1)} %get-tuple-element.60), channel_id=1, source_target_pairs={{2,0},{3,1},{4,2},{5,3},{6,4},{7,5},{8,6},{9,7},{10,8},{11,9},{12,... | collective-permute-start | bytes 245768 | tf_op jit(solution)/shard_map/ppermute | solution.py:401
  118.9 9.6 %collective-permute-start.11 = (f32[1,32,128]{2,1,0:T(8,128)S(1)}, f32[1,32,128]{2,1,0:T(8,128)S(1)}, u32[]{:S(2)}, u32[]{:S(2)}) collective-permute-start(f32[1,32,128]{2,1,0:T(8,128)S(1)} %get-tuple-element.64), channel_id=1, source_target_pairs={{0,704},{64,0},{128,64},{192,128},{256,192},{320,256},{384,320},{4... | collective-permute-start | bytes 49160 | tf_op jit(solution)/shard_map/ppermute | solution.py:404
  120.9 7.7 %collective-permute-start.12 = (f32[1,32,128]{2,1,0:T(8,128)S(1)}, f32[1,32,128]{2,1,0:T(8,128)S(1)}, u32[]{:S(2)}, u32[]{:S(2)}) collective-permute-start(f32[1,32,128]{2,1,0:T(8,128)S(1)} %get-tuple-element.65), channel_id=1, source_target_pairs={{0,64},{64,128},{128,192},{192,256},{256,320},{320,384},{384,448},... | collective-permute-start | bytes 49160 | tf_op jit(solution)/shard_map/ppermute | solution.py:404
  124.8 12.6 %all-to-all-start.2 = ((f32[12,1,128]{2,1,0:T(1,128)}), f32[12,1,128]{2,1,0:T(1,128)S(1)}, u32[]{:S(2)}, u32[]{:S(2)}) async-start(f32[12,1,128]{2,1,0:T(1,128)} %copy.10), calls=%async_computation.2 | async-start | bytes 12288 | tf_op jit(solution)/shard_map/all_to_all | solution.py:460
  137.4 5.6 %collective-permute-start.13 = (f32[24,32,128]{2,1,0:T(8,128)S(1)}, f32[24,32,128]{2,1,0:T(8,128)S(1)}, u32[]{:S(2)}, u32[]{:S(2)}) collective-permute-start(f32[24,32,128]{2,1,0:T(8,128)S(1)} %get-tuple-element.70), channel_id=1, source_target_pairs={{0,1},{1,0},{2,3},{3,2},{4,5},{5,4},{6,7},{7,6},{8,9},{9,8},{10,11... | collective-permute-start | bytes 1179656 | tf_op jit(solution)/shard_map/ppermute | solution.py:407

commit v3 on v2

--- a/solution.py
+++ b/solution.py
@@ -321,7 +321,7 @@
         values = [whole_sum(s * keep) for s in sums]
         quad = sum(weight_ref[tile] * (samples[tile] * iv) * (samples[tile] * iv) for tile in range(2))
         values += [whole_sum(quad * keep), t0, t1, v1]
-        stats_ref[...] = jnp.broadcast_to(as_row(values), stats_ref.shape)
+        stats_ref[...] = jnp.broadcast_to(as_row(values)[None], stats_ref.shape)
 
 
 def as_row(values):
@@ -341,7 +341,7 @@
 
 
 def merge_body(in_ref, out_ref):
-    out_ref[...] = jnp.broadcast_to(as_row(merged(in_ref[...])), out_ref.shape)
+    out_ref[...] = jnp.broadcast_to(as_row(merged(in_ref[:, 0, :]))[None], out_ref.shape)
 
 
 def last_body(core_ref, here_ref, south_ref, north_ref, east_ref, west_ref, wide_d, q0_ref, q1_ref, *outs):
@@ -365,7 +365,7 @@
 
 def final_body(core_ref, mine_ref, theirs_ref, stats_ref, control_ref, residual_ref, c_ref, r_ref):
     core = core_ref[0]
-    m00, m01, m11, s11, t0, t1, v1 = merged(stats_ref[...])
+    m00, m01, m11, s11, t0, t1, v1 = merged(stats_ref[:, 0, :])
     ratio = t1 / t0
     scaled = m00 / m01
     alpha0 = scaled / ratio
@@ -449,13 +449,13 @@
     south, north, east, west = exchange([g], up, down, FAR)
     q1, up, down, g, stats = call(
         functools.partial(pair_body, True),
-        [field, f32(STEPS, WIN, COLS), f32(STEPS, WIN, COLS), field, f32(count_y, COLS)],
+        [field, f32(STEPS, WIN, COLS), f32(STEPS, WIN, COLS), field, f32(count_y, 2, COLS)],
         2 * 10**8,
         space,
         1,
     )(core, g, south, north, east, west, wide_d, high, low, weights, q0, u0)
     stats = lax.all_to_all(stats, "gy", split_axis=0, concat_axis=0, tiled=True)
-    (stats,) = call(merge_body, [f32(count_x, COLS)], 10**5)(stats)
+    (stats,) = call(merge_body, [f32(count_x, 2, COLS)], 10**5)(stats)
     south, north, east, west, stats = exchange([g], up, down, STEPS, stats)
     stats = lax.all_to_all(stats, "gx", split_axis=0, concat_axis=0, tiled=True)
     near = (ROWS + 2 * STEPS, WIN, 2 * COLS)

time: 145 us -> 139 us (0.959)
  blocking collectives: 25.5 us -> 0 us
  starting transfers between devices: 60.9 us -> 76.9 us
  waiting for transfers between devices: 37.2 us -> 39.3 us
    all_to_all x1 -> x0, blocking collectives: 25.5 us -> none  [on_device(): stats = lax.all_to_all(stats, 'gy', split_axis=0, concat_axis=0, tiled=True)]
    all_to_all x0 -> x1, starting transfers between devices: none -> 14.7 us  [on_device(): stats = lax.all_to_all(stats, 'gy', split_axis=0, concat_axis=0, tiled=True)]
    all_to_all x1, waiting for transfers between devices: 6.81 us -> 0.01 us  [on_device(): stats = lax.all_to_all(stats, 'gx', split_axis=0, concat_axis=0, tiled=True)]
    ppermute x6, waiting for transfers between devices: 13.9 us -> 18.1 us  [along_y(): return lax.ppermute(value, 'gy', pairs)]
    ppermute x6, waiting for transfers between devices: 7.13 us -> 11.1 us  [along_x(): lax.ppermute(value, 'gx', [(i, (i + by) % count_x) for i in range(count_x)])]
  transfers between devices with their start and end apart: 16 -> 17, of which waited for: 10 -> 13; matrix products, arithmetic and copies ran while one was open for 0% -> 0% of each run, Pallas kernels for 2% -> 2%
where the time goes in v3:
time: 139 us; the launch traced here: 137 us
  starting transfers between devices  76.9 us (55%)
  waiting for transfers between devices  39.3 us (28%)
  Pallas kernels  20 us (14%)
    ppermute x6, starting transfers between devices, along_x(): lax.ppermute(value, 'gx', [(i, (i + by) % count_x) for i in range(count_x)])  25 us
    pallas_call x10, Pallas kernels, run(): pl.pallas_call(body, out_shape=tuple(outs), in_specs=specs, out_specs=tup...  20 us
    ppermute x6, waiting for transfers between devices, along_y(): return lax.ppermute(value, 'gy', pairs)  18.1 us
    all_to_all x1, starting transfers between devices, on_device(): stats = lax.all_to_all(stats, 'gy', split_axis=0, concat_axis=0, tiled=True)  14.7 us
    all_to_all x1, starting transfers between devices, on_device(): lax.all_to_all(chunks, 'gy', split_axis=0, concat_axis=0, tiled=True)  14.6 us
    ppermute x6, starting transfers between devices, along_y(): return lax.ppermute(value, 'gy', pairs)  12.5 us
    ppermute x6, waiting for transfers between devices, along_x(): lax.ppermute(value, 'gx', [(i, (i + by) % count_x) for i in range(count_x)])  11.1 us
    all_to_all x1, waiting for transfers between devices, on_device(): lax.all_to_all(chunks, 'gy', split_axis=0, concat_axis=0, tiled=True)  7.02 us
  transfers between devices with their start and end apart: 17, of which 13 were waited for; matrix products, arithmetic and copies ran while one was open for 0% of the time, Pallas kernels for 2%

profile of v3, /device:TPU:1, one launch (start us, length us, event | category | flops | bytes accessed | tf_op | source)
XLA Modules:
  0.0 137.1 jit_solution(13527396922831948034)
XLA Ops:
  0.6 2.1 %shard_map.86 = (f32[256,128]{1,0:T(8,128)}, f32[8,32,128]{2,1,0:T(8,128)S(1)}, f32[272,128]{1,0:T(8,128)S(1)}, f32[8,256]{1,0:T(8,128)S(1)}) custom-call(s32[1]{0:T(128)} %bitcast.core_ref.refs_0_, s32[1,128]{1,0:T(1,128)} %bitcast.5, f32[50,128]{1,0:T(8,128)} %refs_1_.1, f32[50,128]{1,0:T(8,128)} %refs_2_.1, f32[50,8,128]{2,1,0:T(8,128)} %refs_3_.1, ...), custom_call_target="tpu_custom_call" | custom-call | flops 10000000 | bytes 675332 | tf_op jit(solution)/shard_map/pallas_call | solution.py:27
  2.8 14.6 %all-to-all-start = ((f32[64,4,128]{2,1,0:T(4,128)}), f32[64,4,128]{2,1,0:T(4,128)S(1)}, u32[]{:S(2)}, u32[]{:S(2)}) async-start(f32[64,4,128]{2,1,0:T(4,128)} %bitcast.2), calls=%async_computation | async-start | bytes 262144 | tf_op jit(solution)/shard_map/all_to_all | solution.py:433
  17.3 2.5 %collective-permute-start = (f32[272,128]{1,0:T(8,128)S(1)}, f32[272,128]{1,0:T(8,128)S(1)}, u32[]{:S(2)}, u32[]{:S(2)}) collective-permute-start(f32[272,128]{1,0:T(8,128)S(1)} %get-tuple-element.38), channel_id=1, source_target_pairs={{0,1},{1,0},{2,3},{3,2},{4,5},{5,4},{6,7},{7,6},{8,9},{9,8},{10,11... | collective-permute-start | bytes 417800 | tf_op jit(solution)/shard_map/ppermute | solution.py:407
  19.8 1.0 collective-permute-done.theirs_ref
  20.8 7.0 %all-to-all-done = f32[64,4,128]{2,1,0:T(4,128)S(1)} async-done(((f32[64,4,128]{2,1,0:T(4,128)}), f32[64,4,128]{2,1,0:T(4,128)S(1)}, u32[]{:S(2)}, u32[]{:S(2)}) %all-to-all-start) | async-done | bytes 131104 | tf_op jit(solution)/shard_map/all_to_all | solution.py:433
  27.8 0.9 shard_map.87
  28.8 2.9 %collective-permute-start.1 = (f32[20,32,128]{2,1,0:T(8,128)S(1)}, f32[20,32,128]{2,1,0:T(8,128)S(1)}, u32[]{:S(2)}, u32[]{:S(2)}) collective-permute-start(f32[20,32,128]{2,1,0:T(8,128)S(1)} %get-tuple-element.42), channel_id=1, source_target_pairs={{0,2},{1,3},{2,4},{3,5},{4,6},{5,7},{6,8},{7,9},{8,10},{9,11},{10,... | collective-permute-start | bytes 983048 | tf_op jit(solution)/shard_map/ppermute | solution.py:401
  31.7 1.3 collective-permute-start.2
  33.0 5.4 %collective-permute-done.1.refs_2_ = f32[20,32,128]{2,1,0:T(8,128)S(1)} collective-permute-done((f32[20,32,128]{2,1,0:T(8,128)S(1)}, f32[20,32,128]{2,1,0:T(8,128)S(1)}, u32[]{:S(2)}, u32[]{:S(2)}) %collective-permute-start.1) | collective-permute-done | bytes 327712 | tf_op jit(solution)/shard_map/ppermute | solution.py:401
  38.4 3.8 %collective-permute-done.2.refs_3_ = f32[20,32,128]{2,1,0:T(8,128)S(1)} collective-permute-done((f32[20,32,128]{2,1,0:T(8,128)S(1)}, f32[20,32,128]{2,1,0:T(8,128)S(1)}, u32[]{:S(2)}, u32[]{:S(2)}) %collective-permute-start.2) | collective-permute-done | bytes 327712 | tf_op jit(solution)/shard_map/ppermute | solution.py:401
  42.2 0.6 shard_map.88
  42.8 11.3 %collective-permute-start.3 = (f32[6,32,128]{2,1,0:T(8,128)S(1)}, f32[6,32,128]{2,1,0:T(8,128)S(1)}, u32[]{:S(2)}, u32[]{:S(2)}) collective-permute-start(f32[6,32,128]{2,1,0:T(8,128)S(1)} %get-tuple-element.45), channel_id=1, source_target_pairs={{0,704},{64,0},{128,64},{192,128},{256,192},{320,256},{384,320},{4... | collective-permute-start | bytes 294920 | tf_op jit(solution)/shard_map/ppermute | solution.py:404
  54.1 1.9 %collective-permute-start.4 = (f32[6,32,128]{2,1,0:T(8,128)S(1)}, f32[6,32,128]{2,1,0:T(8,128)S(1)}, u32[]{:S(2)}, u32[]{:S(2)}) collective-permute-start(f32[6,32,128]{2,1,0:T(8,128)S(1)} %get-tuple-element.46), channel_id=1, source_target_pairs={{0,64},{64,128},{128,192},{192,256},{256,320},{320,384},{384,448},... | collective-permute-start | bytes 294920 | tf_op jit(solution)/shard_map/ppermute | solution.py:404
  56.0 0.0 collective-permute-done.3.refs_4_
  56.0 4.6 %collective-permute-done.4.refs_5_ = f32[6,32,128]{2,1,0:T(8,128)S(1)} collective-permute-done((f32[6,32,128]{2,1,0:T(8,128)S(1)}, f32[6,32,128]{2,1,0:T(8,128)S(1)}, u32[]{:S(2)}, u32[]{:S(2)}) %collective-permute-start.4) | collective-permute-done | bytes 98336 | tf_op jit(solution)/shard_map/ppermute | solution.py:404
  60.6 5.8 %shard_map.89 = (f32[16,32,128]{2,1,0:T(8,128)S(1)}, f32[16,32,128]{2,1,0:T(8,128)S(1)}, f32[36,32,256]{2,1,0:T(8,128)S(1)}, f32[10,32,128]{2,1,0:T(8,128)S(1)},...) custom-call(s32[1]{0:T(128)} %bitcast.core_ref.refs_0_, f32[16,32,128]{2,1,0:T(8,128)S(1)} %get-tuple-element.41.refs_0_.refs_1_, ...), custom_call_target="tpu_custom_call" | custom-call | flops 200000000 | bytes 5832708 | tf_op jit(solution)/shard_map/pallas_call | solution.py:27
  66.5 2.4 %collective-permute-start.5 = (f32[10,32,128]{2,1,0:T(8,128)S(1)}, f32[10,32,128]{2,1,0:T(8,128)S(1)}, u32[]{:S(2)}, u32[]{:S(2)}) collective-permute-start(f32[10,32,128]{2,1,0:T(8,128)S(1)} %get-tuple-element.51), channel_id=1, source_target_pairs={{0,2},{1,3},{2,4},{3,5},{4,6},{5,7},{6,8},{7,9},{8,10},{9,11},{10,... | collective-permute-start | bytes 491528 | tf_op jit(solution)/shard_map/ppermute | solution.py:401
  68.9 1.3 collective-permute-start.6
  70.2 0.9 collective-permute-done.5.refs_1_.refs_2_
  71.1 3.8 %collective-permute-done.6.refs_2_.refs_3_ = f32[10,32,128]{2,1,0:T(8,128)S(1)} collective-permute-done((f32[10,32,128]{2,1,0:T(8,128)S(1)}, f32[10,32,128]{2,1,0:T(8,128)S(1)}, u32[]{:S(2)}, u32[]{:S(2)}) %collective-permute-start.6) | collective-permute-done | bytes 163872 | tf_op jit(solution)/shard_map/ppermute | solution.py:401
  74.9 0.3 shard_map.90
  75.3 1.9 %collective-permute-start.7 = (f32[3,32,128]{2,1,0:T(8,128)S(1)}, f32[3,32,128]{2,1,0:T(8,128)S(1)}, u32[]{:S(2)}, u32[]{:S(2)}) collective-permute-start(f32[3,32,128]{2,1,0:T(8,128)S(1)} %get-tuple-element.53), channel_id=1, source_target_pairs={{0,704},{64,0},{128,64},{192,128},{256,192},{320,256},{384,320},{4... | collective-permute-start | bytes 147464 | tf_op jit(solution)/shard_map/ppermute | solution.py:404
  77.2 3.5 %collective-permute-start.8 = (f32[3,32,128]{2,1,0:T(8,128)S(1)}, f32[3,32,128]{2,1,0:T(8,128)S(1)}, u32[]{:S(2)}, u32[]{:S(2)}) collective-permute-start(f32[3,32,128]{2,1,0:T(8,128)S(1)} %get-tuple-element.54), channel_id=1, source_target_pairs={{0,64},{64,128},{128,192},{192,256},{256,320},{320,384},{384,448},... | collective-permute-start | bytes 147464 | tf_op jit(solution)/shard_map/ppermute | solution.py:404
  80.8 0.0 collective-permute-done.7.refs_4_
  80.8 2.5 %collective-permute-done.8.refs_5_ = f32[3,32,128]{2,1,0:T(8,128)S(1)} collective-permute-done((f32[3,32,128]{2,1,0:T(8,128)S(1)}, f32[3,32,128]{2,1,0:T(8,128)S(1)}, u32[]{:S(2)}, u32[]{:S(2)}) %collective-permute-start.8) | collective-permute-done | bytes 49184 | tf_op jit(solution)/shard_map/ppermute | solution.py:404
  83.2 5.9 %shard_map.91 = (f32[16,32,128]{2,1,0:T(8,128)S(1)}, f32[5,32,128]{2,1,0:T(8,128)S(1)}, f32[5,32,128]{2,1,0:T(8,128)S(1)}, f32[16,32,128]{2,1,0:T(8,128)S(1)}, f32[64,2,128]{2,1,0:T(2,128)}) custom-call(s32[1]{0:T(128)} %bitcast.core_ref.refs_0_, f32[16,32,128]{2,1,0:T(8,128)S(1)} %get-tuple-element.50.refs_0_.refs_1_, ...), custom_call_target="tpu_custom_call" | custom-call | flops 200000000 | bytes 5308420 | tf_op jit(solution)/shard_map/pallas_call | solution.py:27
  89.1 14.7 %all-to-all-start.1 = ((f32[64,2,128]{2,1,0:T(2,128)}), f32[64,2,128]{2,1,0:T(2,128)S(1)}, u32[]{:S(2)}, u32[]{:S(2)}) async-start(f32[64,2,128]{2,1,0:T(2,128)} %get-tuple-element.63), calls=%async_computation.1 | async-start | bytes 131072 | tf_op jit(solution)/shard_map/all_to_all | solution.py:457
  103.8 3.3 %collective-permute-start.9 = (f32[5,32,128]{2,1,0:T(8,128)S(1)}, f32[5,32,128]{2,1,0:T(8,128)S(1)}, u32[]{:S(2)}, u32[]{:S(2)}) collective-permute-start(f32[5,32,128]{2,1,0:T(8,128)S(1)} %get-tuple-element.59), channel_id=1, source_target_pairs={{0,2},{1,3},{2,4},{3,5},{4,6},{5,7},{6,8},{7,9},{8,10},{9,11},{10,... | collective-permute-start | bytes 245768 | tf_op jit(solution)/shard_map/ppermute | solution.py:401
  107.1 1.3 collective-permute-start.10
  108.4 0.5 collective-permute-done.9.refs_1_.south_ref
  108.9 3.7 %collective-permute-done.10.refs_2_.north_ref = f32[5,32,128]{2,1,0:T(8,128)S(1)} collective-permute-done((f32[5,32,128]{2,1,0:T(8,128)S(1)}, f32[5,32,128]{2,1,0:T(8,128)S(1)}, u32[]{:S(2)}, u32[]{:S(2)}) %collective-permute-start.10) | collective-permute-done | bytes 81952 | tf_op jit(solution)/shard_map/ppermute | solution.py:401
  112.6 0.3 shard_map.92
  112.8 0.7 all-to-all-done.1.in_ref
  113.6 0.8 shard_map.93
  114.4 3.5 %all-to-all-start.2 = ((f32[12,2,128]{2,1,0:T(2,128)}), f32[12,2,128]{2,1,0:T(2,128)S(1)}, u32[]{:S(2)}, u32[]{:S(2)}) async-start(f32[12,2,128]{2,1,0:T(2,128)} %shard_map.93), calls=%async_computation.2 | async-start | bytes 24576 | tf_op jit(solution)/shard_map/all_to_all | solution.py:460
  117.9 4.5 %collective-permute-start.11 = (f32[1,32,128]{2,1,0:T(8,128)S(1)}, f32[1,32,128]{2,1,0:T(8,128)S(1)}, u32[]{:S(2)}, u32[]{:S(2)}) collective-permute-start(f32[1,32,128]{2,1,0:T(8,128)S(1)} %get-tuple-element.64), channel_id=1, source_target_pairs={{0,704},{64,0},{128,64},{192,128},{256,192},{320,256},{384,320},{4... | collective-permute-start | bytes 49160 | tf_op jit(solution)/shard_map/ppermute | solution.py:404
  122.4 1.9 %collective-permute-start.12 = (f32[1,32,128]{2,1,0:T(8,128)S(1)}, f32[1,32,128]{2,1,0:T(8,128)S(1)}, u32[]{:S(2)}, u32[]{:S(2)}) collective-permute-start(f32[1,32,128]{2,1,0:T(8,128)S(1)} %get-tuple-element.65), channel_id=1, source_target_pairs={{0,64},{64,128},{128,192},{192,256},{256,320},{320,384},{384,448},... | collective-permute-start | bytes 49160 | tf_op jit(solution)/shard_map/ppermute | solution.py:404
  124.3 0.0 collective-permute-done.11.east_ref
  124.3 4.0 %collective-permute-done.12.west_ref = f32[1,32,128]{2,1,0:T(8,128)S(1)} collective-permute-done((f32[1,32,128]{2,1,0:T(8,128)S(1)}, f32[1,32,128]{2,1,0:T(8,128)S(1)}, u32[]{:S(2)}, u32[]{:S(2)}) %collective-permute-start.12) | collective-permute-done | bytes 16416 | tf_op jit(solution)/shard_map/ppermute | solution.py:404
  128.3 2.0 %shard_map.94 = (f32[24,32,128]{2,1,0:T(8,128)S(1)}, f32[24,32,128]{2,1,0:T(8,128)S(1)}) custom-call(s32[1]{0:T(128)} %bitcast.core_ref.refs_0_, f32[16,32,128]{2,1,0:T(8,128)S(1)} %get-tuple-element.58.refs_0_.here_ref, f32[5,32,128]{2,1,0:T(8,128)S(1)} %collective-permute-done.9.refs_1_.south_ref, ...), custom_call_target="tpu_custom_call" | custom-call | flops 100000000 | bytes 2949124 | tf_op jit(solution)/shard_map/pallas_call | solution.py:27
  130.3 0.0 all-to-all-done.2.stats_ref
  130.3 4.2 %collective-permute-start.13 = (f32[24,32,128]{2,1,0:T(8,128)S(1)}, f32[24,32,128]{2,1,0:T(8,128)S(1)}, u32[]{:S(2)}, u32[]{:S(2)}) collective-permute-start(f32[24,32,128]{2,1,0:T(8,128)S(1)} %get-tuple-element.70), channel_id=1, source_target_pairs={{0,1},{1,0},{2,3},{3,2},{4,5},{5,4},{6,7},{7,6},{8,9},{9,8},{10,11... | collective-permute-start | bytes 1179656 | tf_op jit(solution)/shard_map/ppermute | solution.py:407
  134.5 1.3 collective-permute-done.13.theirs_ref
  135.8 1.2 shard_map.95
Async XLA Ops:
  2.8 25.1 %all-to-all-start = ((f32[64,4,128]{2,1,0:T(4,128)}), f32[64,4,128]{2,1,0:T(4,128)S(1)}, u32[]{:S(2)}, u32[]{:S(2)}) async-start(f32[64,4,128]{2,1,0:T(4,128)} %bitcast.2), calls=%async_computation | async-start | bytes 262144 | tf_op jit(solution)/shard_map/all_to_all | solution.py:433
  17.3 3.5 %collective-permute-start = (f32[272,128]{1,0:T(8,128)S(1)}, f32[272,128]{1,0:T(8,128)S(1)}, u32[]{:S(2)}, u32[]{:S(2)}) collective-permute-start(f32[272,128]{1,0:T(8,128)S(1)} %get-tuple-element.38), channel_id=1, source_target_pairs={{0,1},{1,0},{2,3},{3,2},{4,5},{5,4},{6,7},{7,6},{8,9},{9,8},{10,11... | collective-permute-start | bytes 417800 | tf_op jit(solution)/shard_map/ppermute | solution.py:407
  28.8 9.6 %collective-permute-start.1 = (f32[20,32,128]{2,1,0:T(8,128)S(1)}, f32[20,32,128]{2,1,0:T(8,128)S(1)}, u32[]{:S(2)}, u32[]{:S(2)}) collective-permute-start(f32[20,32,128]{2,1,0:T(8,128)S(1)} %get-tuple-element.42), channel_id=1, source_target_pairs={{0,2},{1,3},{2,4},{3,5},{4,6},{5,7},{6,8},{7,9},{8,10},{9,11},{10,... | collective-permute-start | bytes 983048 | tf_op jit(solution)/shard_map/ppermute | solution.py:401
  31.7 10.5 %collective-permute-start.2 = (f32[20,32,128]{2,1,0:T(8,128)S(1)}, f32[20,32,128]{2,1,0:T(8,128)S(1)}, u32[]{:S(2)}, u32[]{:S(2)}) collective-permute-start(f32[20,32,128]{2,1,0:T(8,128)S(1)} %get-tuple-element.43), channel_id=1, source_target_pairs={{2,0},{3,1},{4,2},{5,3},{6,4},{7,5},{8,6},{9,7},{10,8},{11,9},{12,... | collective-permute-start | bytes 983048 | tf_op jit(solution)/shard_map/ppermute | solution.py:401
  42.8 13.2 %collective-permute-start.3 = (f32[6,32,128]{2,1,0:T(8,128)S(1)}, f32[6,32,128]{2,1,0:T(8,128)S(1)}, u32[]{:S(2)}, u32[]{:S(2)}) collective-permute-start(f32[6,32,128]{2,1,0:T(8,128)S(1)} %get-tuple-element.45), channel_id=1, source_target_pairs={{0,704},{64,0},{128,64},{192,128},{256,192},{320,256},{384,320},{4... | collective-permute-start | bytes 294920 | tf_op jit(solution)/shard_map/ppermute | solution.py:404
  54.1 6.6 %collective-permute-start.4 = (f32[6,32,128]{2,1,0:T(8,128)S(1)}, f32[6,32,128]{2,1,0:T(8,128)S(1)}, u32[]{:S(2)}, u32[]{:S(2)}) collective-permute-start(f32[6,32,128]{2,1,0:T(8,128)S(1)} %get-tuple-element.46), channel_id=1, source_target_pairs={{0,64},{64,128},{128,192},{192,256},{256,320},{320,384},{384,448},... | collective-permute-start | bytes 294920 | tf_op jit(solution)/shard_map/ppermute | solution.py:404
  66.5 4.6 %collective-permute-start.5 = (f32[10,32,128]{2,1,0:T(8,128)S(1)}, f32[10,32,128]{2,1,0:T(8,128)S(1)}, u32[]{:S(2)}, u32[]{:S(2)}) collective-permute-start(f32[10,32,128]{2,1,0:T(8,128)S(1)} %get-tuple-element.51), channel_id=1, source_target_pairs={{0,2},{1,3},{2,4},{3,5},{4,6},{5,7},{6,8},{7,9},{8,10},{9,11},{10,... | collective-permute-start | bytes 491528 | tf_op jit(solution)/shard_map/ppermute | solution.py:401
  68.9 6.1 %collective-permute-start.6 = (f32[10,32,128]{2,1,0:T(8,128)S(1)}, f32[10,32,128]{2,1,0:T(8,128)S(1)}, u32[]{:S(2)}, u32[]{:S(2)}) collective-permute-start(f32[10,32,128]{2,1,0:T(8,128)S(1)} %get-tuple-element.52), channel_id=1, source_target_pairs={{2,0},{3,1},{4,2},{5,3},{6,4},{7,5},{8,6},{9,7},{10,8},{11,9},{12,... | collective-permute-start | bytes 491528 | tf_op jit(solution)/shard_map/ppermute | solution.py:401
  75.3 5.5 %collective-permute-start.7 = (f32[3,32,128]{2,1,0:T(8,128)S(1)}, f32[3,32,128]{2,1,0:T(8,128)S(1)}, u32[]{:S(2)}, u32[]{:S(2)}) collective-permute-start(f32[3,32,128]{2,1,0:T(8,128)S(1)} %get-tuple-element.53), channel_id=1, source_target_pairs={{0,704},{64,0},{128,64},{192,128},{256,192},{320,256},{384,320},{4... | collective-permute-start | bytes 147464 | tf_op jit(solution)/shard_map/ppermute | solution.py:404
  77.2 6.0 %collective-permute-start.8 = (f32[3,32,128]{2,1,0:T(8,128)S(1)}, f32[3,32,128]{2,1,0:T(8,128)S(1)}, u32[]{:S(2)}, u32[]{:S(2)}) collective-permute-start(f32[3,32,128]{2,1,0:T(8,128)S(1)} %get-tuple-element.54), channel_id=1, source_target_pairs={{0,64},{64,128},{128,192},{192,256},{256,320},{320,384},{384,448},... | collective-permute-start | bytes 147464 | tf_op jit(solution)/shard_map/ppermute | solution.py:404
  89.1 24.4 %all-to-all-start.1 = ((f32[64,2,128]{2,1,0:T(2,128)}), f32[64,2,128]{2,1,0:T(2,128)S(1)}, u32[]{:S(2)}, u32[]{:S(2)}) async-start(f32[64,2,128]{2,1,0:T(2,128)} %get-tuple-element.63), calls=%async_computation.1 | async-start | bytes 131072 | tf_op jit(solution)/shard_map/all_to_all | solution.py:457
  103.8 5.1 %collective-permute-start.9 = (f32[5,32,128]{2,1,0:T(8,128)S(1)}, f32[5,32,128]{2,1,0:T(8,128)S(1)}, u32[]{:S(2)}, u32[]{:S(2)}) collective-permute-start(f32[5,32,128]{2,1,0:T(8,128)S(1)} %get-tuple-element.59), channel_id=1, source_target_pairs={{0,2},{1,3},{2,4},{3,5},{4,6},{5,7},{6,8},{7,9},{8,10},{9,11},{10,... | collective-permute-start | bytes 245768 | tf_op jit(solution)/shard_map/ppermute | solution.py:401
  107.1 5.5 %collective-permute-start.10 = (f32[5,32,128]{2,1,0:T(8,128)S(1)}, f32[5,32,128]{2,1,0:T(8,128)S(1)}, u32[]{:S(2)}, u32[]{:S(2)}) collective-permute-start(f32[5,32,128]{2,1,0:T(8,128)S(1)} %get-tuple-element.60), channel_id=1, source_target_pairs={{2,0},{3,1},{4,2},{5,3},{6,4},{7,5},{8,6},{9,7},{10,8},{11,9},{12,... | collective-permute-start | bytes 245768 | tf_op jit(solution)/shard_map/ppermute | solution.py:401
  114.4 15.9 %all-to-all-start.2 = ((f32[12,2,128]{2,1,0:T(2,128)}), f32[12,2,128]{2,1,0:T(2,128)S(1)}, u32[]{:S(2)}, u32[]{:S(2)}) async-start(f32[12,2,128]{2,1,0:T(2,128)} %shard_map.93), calls=%async_computation.2 | async-start | bytes 24576 | tf_op jit(solution)/shard_map/all_to_all | solution.py:460
  117.9 6.4 %collective-permute-start.11 = (f32[1,32,128]{2,1,0:T(8,128)S(1)}, f32[1,32,128]{2,1,0:T(8,128)S(1)}, u32[]{:S(2)}, u32[]{:S(2)}) collective-permute-start(f32[1,32,128]{2,1,0:T(8,128)S(1)} %get-tuple-element.64), channel_id=1, source_target_pairs={{0,704},{64,0},{128,64},{192,128},{256,192},{320,256},{384,320},{4... | collective-permute-start | bytes 49160 | tf_op jit(solution)/shard_map/ppermute | solution.py:404
  122.4 5.9 %collective-permute-start.12 = (f32[1,32,128]{2,1,0:T(8,128)S(1)}, f32[1,32,128]{2,1,0:T(8,128)S(1)}, u32[]{:S(2)}, u32[]{:S(2)}) collective-permute-start(f32[1,32,128]{2,1,0:T(8,128)S(1)} %get-tuple-element.65), channel_id=1, source_target_pairs={{0,64},{64,128},{128,192},{192,256},{256,320},{320,384},{384,448},... | collective-permute-start | bytes 49160 | tf_op jit(solution)/shard_map/ppermute | solution.py:404
  130.3 5.5 %collective-permute-start.13 = (f32[24,32,128]{2,1,0:T(8,128)S(1)}, f32[24,32,128]{2,1,0:T(8,128)S(1)}, u32[]{:S(2)}, u32[]{:S(2)}) collective-permute-start(f32[24,32,128]{2,1,0:T(8,128)S(1)} %get-tuple-element.70), channel_id=1, source_target_pairs={{0,1},{1,0},{2,3},{3,2},{4,5},{5,4},{6,7},{7,6},{8,9},{9,8},{10,11... | collective-permute-start | bytes 1179656 | tf_op jit(solution)/shard_map/ppermute | solution.py:407

commit v4 on v3

--- a/solution.py
+++ b/solution.py
@@ -406,14 +406,13 @@
     def across(value):
         return lax.ppermute(value, "gy", [(i, i ^ 1) for i in range(count_y)])
 
-    def exchange(heres, up, down, halo, *after):
+    def exchange(heres, up, down, halo):
         kinds = len(heres)
         tiles = places(halo)[1]
         south, north = along_y(down, 2), along_y(up, -2)
         pack = call(functools.partial(strips_body, halo, kinds), [f32(kinds * tiles, WIN, COLS)] * 2, 10**6)
         west, east = pack(*heres, south, north)
-        west, east, *after = lax.optimization_barrier((west, east, *after))
-        return south, north, along_x(west, -1), along_x(east, 1), *after
+        return south, north, along_x(west, -1), along_x(east, 1)
 
     field = f32(ROWS, WIN, COLS)
     ins = [
@@ -449,14 +448,14 @@
     south, north, east, west = exchange([g], up, down, FAR)
     q1, up, down, g, stats = call(
         functools.partial(pair_body, True),
-        [field, f32(STEPS, WIN, COLS), f32(STEPS, WIN, COLS), field, f32(count_y, 2, COLS)],
+        [field, f32(STEPS, WIN, COLS), f32(STEPS, WIN, COLS), field, f32(count_y, 1, COLS)],
         2 * 10**8,
         space,
         1,
     )(core, g, south, north, east, west, wide_d, high, low, weights, q0, u0)
     stats = lax.all_to_all(stats, "gy", split_axis=0, concat_axis=0, tiled=True)
-    (stats,) = call(merge_body, [f32(count_x, 2, COLS)], 10**5)(stats)
-    south, north, east, west, stats = exchange([g], up, down, STEPS, stats)
+    (stats,) = call(merge_body, [f32(count_x, 1, COLS)], 10**5)(stats)
+    south, north, east, west = exchange([g], up, down, STEPS)
     stats = lax.all_to_all(stats, "gx", split_axis=0, concat_axis=0, tiled=True)
     near = (ROWS + 2 * STEPS, WIN, 2 * COLS)
     mine, mate = call(

time: 139 us -> 139 us (level)
  waiting for transfers between devices: 39.3 us -> 40.7 us
    all_to_all x1, waiting for transfers between devices: 0.01 us -> 6.72 us  [on_device(): stats = lax.all_to_all(stats, 'gx', split_axis=0, concat_axis=0, tiled=True)]
    ppermute x6, waiting for transfers between devices: 18.1 us -> 13.9 us  [along_y(): return lax.ppermute(value, 'gy', pairs)]
    ppermute x6, waiting for transfers between devices: 11.1 us -> 7.13 us  [along_x(): lax.ppermute(value, 'gx', [(i, (i + by) % count_x) for i in range(count_x)])]
    all_to_all x1, waiting for transfers between devices: 0.74 us -> 3.63 us  [on_device(): stats = lax.all_to_all(stats, 'gy', split_axis=0, concat_axis=0, tiled=True)]
    all_to_all x1, starting transfers between devices: 14.7 us -> 16.4 us  [on_device(): stats = lax.all_to_all(stats, 'gy', split_axis=0, concat_axis=0, tiled=True)]
  transfers between devices with their start and end apart: 17 -> 17, of which waited for: 13 -> 11; matrix products, arithmetic and copies ran while one was open for 0% -> 0% of each run, Pallas kernels for 2% -> 2%
where the time goes in v4:
time: 139 us; the launch traced here: 138 us
  starting transfers between devices  76.6 us (55%)
  waiting for transfers between devices  40.7 us (29%)
  Pallas kernels  20 us (14%)
    ppermute x6, starting transfers between devices, along_x(): lax.ppermute(value, 'gx', [(i, (i + by) % count_x) for i in range(count_x)])  23.9 us
    pallas_call x10, Pallas kernels, run(): pl.pallas_call(body, out_shape=tuple(outs), in_specs=specs, out_specs=tup...  20 us
    all_to_all x1, starting transfers between devices, on_device(): stats = lax.all_to_all(stats, 'gy', split_axis=0, concat_axis=0, tiled=True)  16.4 us
    all_to_all x1, starting transfers between devices, on_device(): lax.all_to_all(chunks, 'gy', split_axis=0, concat_axis=0, tiled=True)  14.6 us
    ppermute x6, waiting for transfers between devices, along_y(): return lax.ppermute(value, 'gy', pairs)  13.9 us
    ppermute x6, starting transfers between devices, along_y(): return lax.ppermute(value, 'gy', pairs)  12 us
    ppermute x6, waiting for transfers between devices, along_x(): lax.ppermute(value, 'gx', [(i, (i + by) % count_x) for i in range(count_x)])  7.13 us
    all_to_all x1, waiting for transfers between devices, on_device(): lax.all_to_all(chunks, 'gy', split_axis=0, concat_axis=0, tiled=True)  7.02 us
  transfers between devices with their start and end apart: 17, of which 11 were waited for; matrix products, arithmetic and copies ran while one was open for 0% of the time, Pallas kernels for 2%

profile of v4, /device:TPU:1, one launch (start us, length us, event | category | flops | bytes accessed | tf_op | source)
XLA Modules:
  0.0 138.2 jit_solution(15840048583739989285)
XLA Ops:
  0.6 2.1 %shard_map.86 = (f32[256,128]{1,0:T(8,128)}, f32[8,32,128]{2,1,0:T(8,128)S(1)}, f32[272,128]{1,0:T(8,128)S(1)}, f32[8,256]{1,0:T(8,128)S(1)}) custom-call(s32[1]{0:T(128)} %bitcast.core_ref.refs_0_, s32[1,128]{1,0:T(1,128)} %bitcast.5, f32[50,128]{1,0:T(8,128)} %refs_1_.1, f32[50,128]{1,0:T(8,128)} %refs_2_.1, f32[50,8,128]{2,1,0:T(8,128)} %refs_3_.1, ...), custom_call_target="tpu_custom_call" | custom-call | flops 10000000 | bytes 675332 | tf_op jit(solution)/shard_map/pallas_call | solution.py:27
  2.8 14.6 %all-to-all-start = ((f32[64,4,128]{2,1,0:T(4,128)}), f32[64,4,128]{2,1,0:T(4,128)S(1)}, u32[]{:S(2)}, u32[]{:S(2)}) async-start(f32[64,4,128]{2,1,0:T(4,128)} %bitcast.2), calls=%async_computation | async-start | bytes 262144 | tf_op jit(solution)/shard_map/all_to_all | solution.py:432
  17.3 2.5 %collective-permute-start = (f32[272,128]{1,0:T(8,128)S(1)}, f32[272,128]{1,0:T(8,128)S(1)}, u32[]{:S(2)}, u32[]{:S(2)}) collective-permute-start(f32[272,128]{1,0:T(8,128)S(1)} %get-tuple-element.35), channel_id=1, source_target_pairs={{0,1},{1,0},{2,3},{3,2},{4,5},{5,4},{6,7},{7,6},{8,9},{9,8},{10,11... | collective-permute-start | bytes 417800 | tf_op jit(solution)/shard_map/ppermute | solution.py:407
  19.8 1.0 collective-permute-done.theirs_ref
  20.8 7.0 %all-to-all-done = f32[64,4,128]{2,1,0:T(4,128)S(1)} async-done(((f32[64,4,128]{2,1,0:T(4,128)}), f32[64,4,128]{2,1,0:T(4,128)S(1)}, u32[]{:S(2)}, u32[]{:S(2)}) %all-to-all-start) | async-done | bytes 131104 | tf_op jit(solution)/shard_map/all_to_all | solution.py:432
  27.8 0.9 shard_map.87
  28.8 2.9 %collective-permute-start.1 = (f32[20,32,128]{2,1,0:T(8,128)S(1)}, f32[20,32,128]{2,1,0:T(8,128)S(1)}, u32[]{:S(2)}, u32[]{:S(2)}) collective-permute-start(f32[20,32,128]{2,1,0:T(8,128)S(1)} %get-tuple-element.39), channel_id=1, source_target_pairs={{0,2},{1,3},{2,4},{3,5},{4,6},{5,7},{6,8},{7,9},{8,10},{9,11},{10,... | collective-permute-start | bytes 983048 | tf_op jit(solution)/shard_map/ppermute | solution.py:401
  31.7 1.3 collective-permute-start.2
  33.0 5.4 %collective-permute-done.1.refs_2_ = f32[20,32,128]{2,1,0:T(8,128)S(1)} collective-permute-done((f32[20,32,128]{2,1,0:T(8,128)S(1)}, f32[20,32,128]{2,1,0:T(8,128)S(1)}, u32[]{:S(2)}, u32[]{:S(2)}) %collective-permute-start.1) | collective-permute-done | bytes 327712 | tf_op jit(solution)/shard_map/ppermute | solution.py:401
  38.4 3.8 %collective-permute-done.2.refs_3_ = f32[20,32,128]{2,1,0:T(8,128)S(1)} collective-permute-done((f32[20,32,128]{2,1,0:T(8,128)S(1)}, f32[20,32,128]{2,1,0:T(8,128)S(1)}, u32[]{:S(2)}, u32[]{:S(2)}) %collective-permute-start.2) | collective-permute-done | bytes 327712 | tf_op jit(solution)/shard_map/ppermute | solution.py:401
  42.2 0.6 shard_map.88
  42.8 11.3 %collective-permute-start.3 = (f32[6,32,128]{2,1,0:T(8,128)S(1)}, f32[6,32,128]{2,1,0:T(8,128)S(1)}, u32[]{:S(2)}, u32[]{:S(2)}) collective-permute-start(f32[6,32,128]{2,1,0:T(8,128)S(1)} %get-tuple-element.42), channel_id=1, source_target_pairs={{0,704},{64,0},{128,64},{192,128},{256,192},{320,256},{384,320},{4... | collective-permute-start | bytes 294920 | tf_op jit(solution)/shard_map/ppermute | solution.py:404
  54.1 1.9 %collective-permute-start.4 = (f32[6,32,128]{2,1,0:T(8,128)S(1)}, f32[6,32,128]{2,1,0:T(8,128)S(1)}, u32[]{:S(2)}, u32[]{:S(2)}) collective-permute-start(f32[6,32,128]{2,1,0:T(8,128)S(1)} %get-tuple-element.43), channel_id=1, source_target_pairs={{0,64},{64,128},{128,192},{192,256},{256,320},{320,384},{384,448},... | collective-permute-start | bytes 294920 | tf_op jit(solution)/shard_map/ppermute | solution.py:404
  56.0 0.0 collective-permute-done.3.refs_4_
  56.0 4.6 %collective-permute-done.4.refs_5_ = f32[6,32,128]{2,1,0:T(8,128)S(1)} collective-permute-done((f32[6,32,128]{2,1,0:T(8,128)S(1)}, f32[6,32,128]{2,1,0:T(8,128)S(1)}, u32[]{:S(2)}, u32[]{:S(2)}) %collective-permute-start.4) | collective-permute-done | bytes 98336 | tf_op jit(solution)/shard_map/ppermute | solution.py:404
  60.6 5.8 %shard_map.89 = (f32[16,32,128]{2,1,0:T(8,128)S(1)}, f32[16,32,128]{2,1,0:T(8,128)S(1)}, f32[36,32,256]{2,1,0:T(8,128)S(1)}, f32[10,32,128]{2,1,0:T(8,128)S(1)},...) custom-call(s32[1]{0:T(128)} %bitcast.core_ref.refs_0_, f32[16,32,128]{2,1,0:T(8,128)S(1)} %get-tuple-element.38.refs_0_.refs_1_, ...), custom_call_target="tpu_custom_call" | custom-call | flops 200000000 | bytes 5832708 | tf_op jit(solution)/shard_map/pallas_call | solution.py:27
  66.5 2.4 %collective-permute-start.5 = (f32[10,32,128]{2,1,0:T(8,128)S(1)}, f32[10,32,128]{2,1,0:T(8,128)S(1)}, u32[]{:S(2)}, u32[]{:S(2)}) collective-permute-start(f32[10,32,128]{2,1,0:T(8,128)S(1)} %get-tuple-element.48), channel_id=1, source_target_pairs={{0,2},{1,3},{2,4},{3,5},{4,6},{5,7},{6,8},{7,9},{8,10},{9,11},{10,... | collective-permute-start | bytes 491528 | tf_op jit(solution)/shard_map/ppermute | solution.py:401
  68.9 1.3 collective-permute-start.6
  70.2 0.9 collective-permute-done.5.refs_1_.refs_2_
  71.1 3.8 %collective-permute-done.6.refs_2_.refs_3_ = f32[10,32,128]{2,1,0:T(8,128)S(1)} collective-permute-done((f32[10,32,128]{2,1,0:T(8,128)S(1)}, f32[10,32,128]{2,1,0:T(8,128)S(1)}, u32[]{:S(2)}, u32[]{:S(2)}) %collective-permute-start.6) | collective-permute-done | bytes 163872 | tf_op jit(solution)/shard_map/ppermute | solution.py:401
  74.9 0.3 shard_map.90
  75.3 1.9 %collective-permute-start.7 = (f32[3,32,128]{2,1,0:T(8,128)S(1)}, f32[3,32,128]{2,1,0:T(8,128)S(1)}, u32[]{:S(2)}, u32[]{:S(2)}) collective-permute-start(f32[3,32,128]{2,1,0:T(8,128)S(1)} %get-tuple-element.50), channel_id=1, source_target_pairs={{0,704},{64,0},{128,64},{192,128},{256,192},{320,256},{384,320},{4... | collective-permute-start | bytes 147464 | tf_op jit(solution)/shard_map/ppermute | solution.py:404
  77.2 3.5 %collective-permute-start.8 = (f32[3,32,128]{2,1,0:T(8,128)S(1)}, f32[3,32,128]{2,1,0:T(8,128)S(1)}, u32[]{:S(2)}, u32[]{:S(2)}) collective-permute-start(f32[3,32,128]{2,1,0:T(8,128)S(1)} %get-tuple-element.51), channel_id=1, source_target_pairs={{0,64},{64,128},{128,192},{192,256},{256,320},{320,384},{384,448},... | collective-permute-start | bytes 147464 | tf_op jit(solution)/shard_map/ppermute | solution.py:404
  80.8 0.0 collective-permute-done.7.refs_4_
  80.8 2.5 %collective-permute-done.8.refs_5_ = f32[3,32,128]{2,1,0:T(8,128)S(1)} collective-permute-done((f32[3,32,128]{2,1,0:T(8,128)S(1)}, f32[3,32,128]{2,1,0:T(8,128)S(1)}, u32[]{:S(2)}, u32[]{:S(2)}) %collective-permute-start.8) | collective-permute-done | bytes 49184 | tf_op jit(solution)/shard_map/ppermute | solution.py:404
  83.2 5.9 %shard_map.91 = (f32[16,32,128]{2,1,0:T(8,128)S(1)}, f32[5,32,128]{2,1,0:T(8,128)S(1)}, f32[5,32,128]{2,1,0:T(8,128)S(1)}, f32[16,32,128]{2,1,0:T(8,128)S(1)}, f32[64,1,128]{2,1,0:T(1,128)}) custom-call(s32[1]{0:T(128)} %bitcast.core_ref.refs_0_, f32[16,32,128]{2,1,0:T(8,128)S(1)} %get-tuple-element.47.refs_0_.refs_1_, ...), custom_call_target="tpu_custom_call" | custom-call | flops 200000000 | bytes 5275652 | tf_op jit(solution)/shard_map/pallas_call | solution.py:27
  89.1 2.8 %collective-permute-start.9 = (f32[5,32,128]{2,1,0:T(8,128)S(1)}, f32[5,32,128]{2,1,0:T(8,128)S(1)}, u32[]{:S(2)}, u32[]{:S(2)}) collective-permute-start(f32[5,32,128]{2,1,0:T(8,128)S(1)} %get-tuple-element.56), channel_id=1, source_target_pairs={{0,2},{1,3},{2,4},{3,5},{4,6},{5,7},{6,8},{7,9},{8,10},{9,11},{10,... | collective-permute-start | bytes 245768 | tf_op jit(solution)/shard_map/ppermute | solution.py:401
  91.9 1.3 collective-permute-start.10
  93.2 16.4 %all-to-all-start.1 = ((f32[64,1,128]{2,1,0:T(1,128)}), f32[64,1,128]{2,1,0:T(1,128)S(1)}, u32[]{:S(2)}, u32[]{:S(2)}) async-start(f32[64,1,128]{2,1,0:T(1,128)} %get-tuple-element.63), calls=%async_computation.1 | async-start | bytes 65536 | tf_op jit(solution)/shard_map/all_to_all | solution.py:456
  109.6 0.0 collective-permute-done.9.refs_1_.south_ref
  109.7 0.0 collective-permute-done.10.refs_2_.north_ref
  109.7 0.3 shard_map.92
  109.9 1.9 %collective-permute-start.11 = (f32[1,32,128]{2,1,0:T(8,128)S(1)}, f32[1,32,128]{2,1,0:T(8,128)S(1)}, u32[]{:S(2)}, u32[]{:S(2)}) collective-permute-start(f32[1,32,128]{2,1,0:T(8,128)S(1)} %get-tuple-element.58), channel_id=1, source_target_pairs={{0,704},{64,0},{128,64},{192,128},{256,192},{320,256},{384,320},{4... | collective-permute-start | bytes 49160 | tf_op jit(solution)/shard_map/ppermute | solution.py:404
  111.9 3.4 %collective-permute-start.12 = (f32[1,32,128]{2,1,0:T(8,128)S(1)}, f32[1,32,128]{2,1,0:T(8,128)S(1)}, u32[]{:S(2)}, u32[]{:S(2)}) collective-permute-start(f32[1,32,128]{2,1,0:T(8,128)S(1)} %get-tuple-element.59), channel_id=1, source_target_pairs={{0,64},{64,128},{128,192},{192,256},{256,320},{320,384},{384,448},... | collective-permute-start | bytes 49160 | tf_op jit(solution)/shard_map/ppermute | solution.py:404
  115.2 3.6 %all-to-all-done.1.in_ref = f32[64,1,128]{2,1,0:T(1,128)S(1)} async-done(((f32[64,1,128]{2,1,0:T(1,128)}), f32[64,1,128]{2,1,0:T(1,128)S(1)}, u32[]{:S(2)}, u32[]{:S(2)}) %all-to-all-start.1) | async-done | bytes 32800 | tf_op jit(solution)/shard_map/all_to_all | solution.py:456
  118.9 0.8 shard_map.94
  119.7 3.5 %all-to-all-start.2 = ((f32[12,1,128]{2,1,0:T(1,128)}), f32[12,1,128]{2,1,0:T(1,128)S(1)}, u32[]{:S(2)}, u32[]{:S(2)}) async-start(f32[12,1,128]{2,1,0:T(1,128)} %shard_map.94), calls=%async_computation.2 | async-start | bytes 12288 | tf_op jit(solution)/shard_map/all_to_all | solution.py:459
  123.1 0.0 collective-permute-done.11.east_ref
  123.2 0.0 collective-permute-done.12.west_ref
  123.2 2.0 %shard_map.93 = (f32[24,32,128]{2,1,0:T(8,128)S(1)}, f32[24,32,128]{2,1,0:T(8,128)S(1)}) custom-call(s32[1]{0:T(128)} %bitcast.core_ref.refs_0_, f32[16,32,128]{2,1,0:T(8,128)S(1)} %get-tuple-element.55.refs_0_.here_ref, f32[5,32,128]{2,1,0:T(8,128)S(1)} %collective-permute-done.9.refs_1_.south_ref, ...), custom_call_target="tpu_custom_call" | custom-call | flops 100000000 | bytes 2949124 | tf_op jit(solution)/shard_map/pallas_call | solution.py:27
  125.2 6.7 %all-to-all-done.2.stats_ref = f32[12,1,128]{2,1,0:T(1,128)S(1)} async-done(((f32[12,1,128]{2,1,0:T(1,128)}), f32[12,1,128]{2,1,0:T(1,128)S(1)}, u32[]{:S(2)}, u32[]{:S(2)}) %all-to-all-start.2) | async-done | bytes 6176 | tf_op jit(solution)/shard_map/all_to_all | solution.py:459
  131.9 3.7 %collective-permute-start.13 = (f32[24,32,128]{2,1,0:T(8,128)S(1)}, f32[24,32,128]{2,1,0:T(8,128)S(1)}, u32[]{:S(2)}, u32[]{:S(2)}) collective-permute-start(f32[24,32,128]{2,1,0:T(8,128)S(1)} %get-tuple-element.64), channel_id=1, source_target_pairs={{0,1},{1,0},{2,3},{3,2},{4,5},{5,4},{6,7},{7,6},{8,9},{9,8},{10,11... | collective-permute-start | bytes 1179656 | tf_op jit(solution)/shard_map/ppermute | solution.py:407
  135.6 1.3 collective-permute-done.13.theirs_ref
  136.9 1.2 shard_map.95
Async XLA Ops:
  2.8 25.1 %all-to-all-start = ((f32[64,4,128]{2,1,0:T(4,128)}), f32[64,4,128]{2,1,0:T(4,128)S(1)}, u32[]{:S(2)}, u32[]{:S(2)}) async-start(f32[64,4,128]{2,1,0:T(4,128)} %bitcast.2), calls=%async_computation | async-start | bytes 262144 | tf_op jit(solution)/shard_map/all_to_all | solution.py:432
  17.3 3.5 %collective-permute-start = (f32[272,128]{1,0:T(8,128)S(1)}, f32[272,128]{1,0:T(8,128)S(1)}, u32[]{:S(2)}, u32[]{:S(2)}) collective-permute-start(f32[272,128]{1,0:T(8,128)S(1)} %get-tuple-element.35), channel_id=1, source_target_pairs={{0,1},{1,0},{2,3},{3,2},{4,5},{5,4},{6,7},{7,6},{8,9},{9,8},{10,11... | collective-permute-start | bytes 417800 | tf_op jit(solution)/shard_map/ppermute | solution.py:407
  28.8 9.6 %collective-permute-start.1 = (f32[20,32,128]{2,1,0:T(8,128)S(1)}, f32[20,32,128]{2,1,0:T(8,128)S(1)}, u32[]{:S(2)}, u32[]{:S(2)}) collective-permute-start(f32[20,32,128]{2,1,0:T(8,128)S(1)} %get-tuple-element.39), channel_id=1, source_target_pairs={{0,2},{1,3},{2,4},{3,5},{4,6},{5,7},{6,8},{7,9},{8,10},{9,11},{10,... | collective-permute-start | bytes 983048 | tf_op jit(solution)/shard_map/ppermute | solution.py:401
  31.7 10.5 %collective-permute-start.2 = (f32[20,32,128]{2,1,0:T(8,128)S(1)}, f32[20,32,128]{2,1,0:T(8,128)S(1)}, u32[]{:S(2)}, u32[]{:S(2)}) collective-permute-start(f32[20,32,128]{2,1,0:T(8,128)S(1)} %get-tuple-element.40), channel_id=1, source_target_pairs={{2,0},{3,1},{4,2},{5,3},{6,4},{7,5},{8,6},{9,7},{10,8},{11,9},{12,... | collective-permute-start | bytes 983048 | tf_op jit(solution)/shard_map/ppermute | solution.py:401
  42.8 13.2 %collective-permute-start.3 = (f32[6,32,128]{2,1,0:T(8,128)S(1)}, f32[6,32,128]{2,1,0:T(8,128)S(1)}, u32[]{:S(2)}, u32[]{:S(2)}) collective-permute-start(f32[6,32,128]{2,1,0:T(8,128)S(1)} %get-tuple-element.42), channel_id=1, source_target_pairs={{0,704},{64,0},{128,64},{192,128},{256,192},{320,256},{384,320},{4... | collective-permute-start | bytes 294920 | tf_op jit(solution)/shard_map/ppermute | solution.py:404
  54.1 6.6 %collective-permute-start.4 = (f32[6,32,128]{2,1,0:T(8,128)S(1)}, f32[6,32,128]{2,1,0:T(8,128)S(1)}, u32[]{:S(2)}, u32[]{:S(2)}) collective-permute-start(f32[6,32,128]{2,1,0:T(8,128)S(1)} %get-tuple-element.43), channel_id=1, source_target_pairs={{0,64},{64,128},{128,192},{192,256},{256,320},{320,384},{384,448},... | collective-permute-start | bytes 294920 | tf_op jit(solution)/shard_map/ppermute | solution.py:404
  66.5 4.6 %collective-permute-start.5 = (f32[10,32,128]{2,1,0:T(8,128)S(1)}, f32[10,32,128]{2,1,0:T(8,128)S(1)}, u32[]{:S(2)}, u32[]{:S(2)}) collective-permute-start(f32[10,32,128]{2,1,0:T(8,128)S(1)} %get-tuple-element.48), channel_id=1, source_target_pairs={{0,2},{1,3},{2,4},{3,5},{4,6},{5,7},{6,8},{7,9},{8,10},{9,11},{10,... | collective-permute-start | bytes 491528 | tf_op jit(solution)/shard_map/ppermute | solution.py:401
  68.9 6.1 %collective-permute-start.6 = (f32[10,32,128]{2,1,0:T(8,128)S(1)}, f32[10,32,128]{2,1,0:T(8,128)S(1)}, u32[]{:S(2)}, u32[]{:S(2)}) collective-permute-start(f32[10,32,128]{2,1,0:T(8,128)S(1)} %get-tuple-element.49), channel_id=1, source_target_pairs={{2,0},{3,1},{4,2},{5,3},{6,4},{7,5},{8,6},{9,7},{10,8},{11,9},{12,... | collective-permute-start | bytes 491528 | tf_op jit(solution)/shard_map/ppermute | solution.py:401
  75.3 5.5 %collective-permute-start.7 = (f32[3,32,128]{2,1,0:T(8,128)S(1)}, f32[3,32,128]{2,1,0:T(8,128)S(1)}, u32[]{:S(2)}, u32[]{:S(2)}) collective-permute-start(f32[3,32,128]{2,1,0:T(8,128)S(1)} %get-tuple-element.50), channel_id=1, source_target_pairs={{0,704},{64,0},{128,64},{192,128},{256,192},{320,256},{384,320},{4... | collective-permute-start | bytes 147464 | tf_op jit(solution)/shard_map/ppermute | solution.py:404
  77.2 6.0 %collective-permute-start.8 = (f32[3,32,128]{2,1,0:T(8,128)S(1)}, f32[3,32,128]{2,1,0:T(8,128)S(1)}, u32[]{:S(2)}, u32[]{:S(2)}) collective-permute-start(f32[3,32,128]{2,1,0:T(8,128)S(1)} %get-tuple-element.51), channel_id=1, source_target_pairs={{0,64},{64,128},{128,192},{192,256},{256,320},{320,384},{384,448},... | collective-permute-start | bytes 147464 | tf_op jit(solution)/shard_map/ppermute | solution.py:404
  89.1 20.5 %collective-permute-start.9 = (f32[5,32,128]{2,1,0:T(8,128)S(1)}, f32[5,32,128]{2,1,0:T(8,128)S(1)}, u32[]{:S(2)}, u32[]{:S(2)}) collective-permute-start(f32[5,32,128]{2,1,0:T(8,128)S(1)} %get-tuple-element.56), channel_id=1, source_target_pairs={{0,2},{1,3},{2,4},{3,5},{4,6},{5,7},{6,8},{7,9},{8,10},{9,11},{10,... | collective-permute-start | bytes 245768 | tf_op jit(solution)/shard_map/ppermute | solution.py:401
  91.9 17.8 %collective-permute-start.10 = (f32[5,32,128]{2,1,0:T(8,128)S(1)}, f32[5,32,128]{2,1,0:T(8,128)S(1)}, u32[]{:S(2)}, u32[]{:S(2)}) collective-permute-start(f32[5,32,128]{2,1,0:T(8,128)S(1)} %get-tuple-element.57), channel_id=1, source_target_pairs={{2,0},{3,1},{4,2},{5,3},{6,4},{7,5},{8,6},{9,7},{10,8},{11,9},{12,... | collective-permute-start | bytes 245768 | tf_op jit(solution)/shard_map/ppermute | solution.py:401
  93.2 25.7 %all-to-all-start.1 = ((f32[64,1,128]{2,1,0:T(1,128)}), f32[64,1,128]{2,1,0:T(1,128)S(1)}, u32[]{:S(2)}, u32[]{:S(2)}) async-start(f32[64,1,128]{2,1,0:T(1,128)} %get-tuple-element.63), calls=%async_computation.1 | async-start | bytes 65536 | tf_op jit(solution)/shard_map/all_to_all | solution.py:456
  109.9 13.2 %collective-permute-start.11 = (f32[1,32,128]{2,1,0:T(8,128)S(1)}, f32[1,32,128]{2,1,0:T(8,128)S(1)}, u32[]{:S(2)}, u32[]{:S(2)}) collective-permute-start(f32[1,32,128]{2,1,0:T(8,128)S(1)} %get-tuple-element.58), channel_id=1, source_target_pairs={{0,704},{64,0},{128,64},{192,128},{256,192},{320,256},{384,320},{4... | collective-permute-start | bytes 49160 | tf_op jit(solution)/shard_map/ppermute | solution.py:404
  111.9 11.3 %collective-permute-start.12 = (f32[1,32,128]{2,1,0:T(8,128)S(1)}, f32[1,32,128]{2,1,0:T(8,128)S(1)}, u32[]{:S(2)}, u32[]{:S(2)}) collective-permute-start(f32[1,32,128]{2,1,0:T(8,128)S(1)} %get-tuple-element.59), channel_id=1, source_target_pairs={{0,64},{64,128},{128,192},{192,256},{256,320},{320,384},{384,448},... | collective-permute-start | bytes 49160 | tf_op jit(solution)/shard_map/ppermute | solution.py:404
  119.7 12.2 %all-to-all-start.2 = ((f32[12,1,128]{2,1,0:T(1,128)}), f32[12,1,128]{2,1,0:T(1,128)S(1)}, u32[]{:S(2)}, u32[]{:S(2)}) async-start(f32[12,1,128]{2,1,0:T(1,128)} %shard_map.94), calls=%async_computation.2 | async-start | bytes 12288 | tf_op jit(solution)/shard_map/all_to_all | solution.py:459
  131.9 5.0 %collective-permute-start.13 = (f32[24,32,128]{2,1,0:T(8,128)S(1)}, f32[24,32,128]{2,1,0:T(8,128)S(1)}, u32[]{:S(2)}, u32[]{:S(2)}) collective-permute-start(f32[24,32,128]{2,1,0:T(8,128)S(1)} %get-tuple-element.64), channel_id=1, source_target_pairs={{0,1},{1,0},{2,3},{3,2},{4,5},{5,4},{6,7},{7,6},{8,9},{9,8},{10,11... | collective-permute-start | bytes 1179656 | tf_op jit(solution)/shard_map/ppermute | solution.py:407

commit v5 on v4

--- a/solution.py
+++ b/solution.py
@@ -80,7 +80,7 @@
 
 def route(own_ref, inv_ref, inno_ref, out_ref, pad_ref):
     count = own_ref.shape[1]
-    tiles = out_ref.shape[0] // CAP
+    tiles = out_ref.shape[0] // (2 * CAP)
     chips = tiles // 2
     own = own_ref[...]
     owners = lax.broadcasted_iota(jnp.int32, (tiles, count), 0)
@@ -115,49 +115,86 @@
         total = total + dot(pick, second, ((1,), (1,)))
         total = total + dot(pick, third, ((1,), (1,)))
         for r in range(CAP):
-            out_ref[pl.ds(core * CAP + r, chips, stride=2 * CAP), :] = total[r * chips : (r + 1) * chips]
+            part = total[r * chips : (r + 1) * chips]
+            edge = jnp.zeros((1, COLS), jnp.float32)
+            below = jnp.concatenate([edge, part[: chips - 1]], axis=0)
+            above = jnp.concatenate([part[1:], edge], axis=0)
+            lane = lax.broadcasted_iota(jnp.int32, (chips, COLS), 1)
+            low = jnp.where(lane < WIN, pltpu.roll(below, COLS - WIN, 1), pltpu.roll(below, 2 * WIN, 1))
+            high = jnp.where(lane < 3 * WIN, pltpu.roll(above, WIN, 1), above)
+            at = 2 * core * CAP + r
+            out_ref[pl.ds(at, chips, stride=4 * CAP), :] = part
+            out_ref[pl.ds(at + CAP, chips, stride=4 * CAP), :] = jnp.where(lane < 2 * WIN, low, high)
+
+
+def spread_out(misfit, high_ref, low_ref):
+    high, low = split(misfit)
+    wide = dot(jnp.concatenate([high, low], axis=0), high_ref[...], ((1,), (1,)))
+    return wide[:WIN] + wide[WIN:] + dot(high, low_ref[...], ((1,), (1,)))
 
 
 def adjoint(misfits, high_ref, low_ref, store):
     for tile in range(2):
-        high, low = split(misfits[tile])
-        both = jnp.concatenate([high, low], axis=0)
-        wide = dot(both, high_ref[tile], ((1,), (1,)))
-        flat = wide[:WIN] + wide[WIN:] + dot(high, low_ref[tile], ((1,), (1,)))
+        flat = spread_out(misfits[tile], high_ref.at[tile], low_ref.at[tile])
         for r in range(CY):
             store(tile * CY + r, flat[:, r * COLS : (r + 1) * COLS])
 
 
-def seed_body(core_ref, mine_ref, theirs_ref, table_ref, rec_ref, *outs):
-    d_ref, high_ref, low_ref, weight_ref, g_ref, up_ref, down_ref = outs
+def fill(table, rows, high_ref, low_ref):
+    columns = lax.broadcasted_iota(jnp.int32, (COLS, table.shape[1]), 0)
+    cell = table[0:1].astype(jnp.int32)
+    row = jnp.zeros_like(cell)
+    for edge in range(1, CY - 1):
+        row = row + jnp.where(cell >= edge * (COLS - 1), 1, 0)
+    col = cell - row * (COLS - 1)
+    at_col, at_next = col == columns, col + 1 == columns
+    for n, r in enumerate(rows):
+        lower, upper = row == r, row == r - 1
+        west = jnp.where(lower, table[1:2], 0.0) + jnp.where(upper, table[3:4], 0.0)
+        east = jnp.where(lower, table[2:3], 0.0) + jnp.where(upper, table[4:5], 0.0)
+        matrix = jnp.where(at_col, west, 0.0) + jnp.where(at_next, east, 0.0)
+        high, low = split(matrix)
+        high_ref[n * COLS : (n + 1) * COLS, :] = high
+        low_ref[n * COLS : (n + 1) * COLS, :] = low
+
+
+def chip_body(core_ref, mine_ref, theirs_ref, table_ref, d_ref, tables_ref, up_ref, down_ref):
     core = core_ref[0]
     slots = table_ref.shape[1]
+    parts = slots // COLS
     base = CY * WIN
-    other = jnp.concatenate(
-        [theirs_ref[base + 8 * part : base + 8 * part + 8, :] for part in range(slots // COLS)], axis=1
-    )
+    other = jnp.concatenate([theirs_ref[base + 8 * n : base + 8 * n + 8, :] for n in range(parts)], axis=1)
     here = table_ref[...]
-    columns = lax.broadcasted_iota(jnp.int32, (COLS, slots), 0)
-    slot_t = rec_ref[...].T
-    targets = []
+    up_ref[FAR] = jnp.zeros((WIN, COLS), jnp.float32)
     for tile in range(2):
         first = core == tile
         table = jnp.where(first, here, other)
-        cell = table[0:1].astype(jnp.int32)
-        row = jnp.zeros_like(cell)
-        for edge in range(1, CY - 1):
-            row = row + jnp.where(cell >= edge * (COLS - 1), 1, 0)
-        col = cell - row * (COLS - 1)
-        at_col, at_next = col == columns, col + 1 == columns
+        tables_ref[tile] = table
         for r in range(CY):
-            lower, upper = row == r, row == r - 1
-            west = jnp.where(lower, table[1:2], 0.0) + jnp.where(upper, table[3:4], 0.0)
-            east = jnp.where(lower, table[2:3], 0.0) + jnp.where(upper, table[4:5], 0.0)
-            matrix = jnp.where(at_col, west, 0.0) + jnp.where(at_next, east, 0.0)
-            high, low = split(matrix)
-            high_ref[tile, r * COLS : (r + 1) * COLS, :] = high
-            low_ref[tile, r * COLS : (r + 1) * COLS, :] = low
             d_ref[tile * CY + r] = jnp.where(first, mine_ref[r], theirs_ref[r * WIN : (r + 1) * WIN, :])
+        for n in range(parts):
+            at = (tile * parts + n) * 8
+            up_ref[FAR, at : at + 8, :] = table[:, n * COLS : (n + 1) * COLS]
+    up_ref[0:FAR] = d_ref[0:FAR]
+    down_ref[0:FAR] = d_ref[ROWS - FAR : ROWS]
+    down_ref[FAR] = up_ref[FAR]
+
+
+def seed_body(d_ref, tables_ref, south_d, north_d, rec_ref, *outs):
+    high_ref, low_ref, weight_ref, g_ref, south_ref, north_ref, slot_ref, beside_high, beside_low = outs
+    count = rec_ref.shape[0] // (2 * CAP)
+    parts = slot_ref.shape[0] // COLS
+
+    def received(half):
+        for r in range(CAP):
+            at = half * CAP + r
+            slot_ref[pl.ds(r, count, stride=CAP), :] = rec_ref[pl.ds(at, count, stride=2 * CAP), :]
+        return slot_ref[...].T
+
+    slot_t = received(0)
+    targets = []
+    for tile in range(2):
+        fill(tables_ref[tile], range(CY), high_ref.at[tile], low_ref.at[tile])
         weight_ref[tile] = slot_t[tile * 2 * WIN : tile * 2 * WIN + WIN]
         targets.append(slot_t[tile * 2 * WIN + WIN : (tile + 1) * 2 * WIN])
 
@@ -165,10 +202,22 @@
         g_ref[row] = jnp.sqrt(d_ref[row]) * value
 
     adjoint(targets, high_ref, low_ref, store)
-    up_ref[0:FAR] = g_ref[0:FAR]
-    up_ref[FAR : 2 * FAR] = d_ref[0:FAR]
-    down_ref[0:FAR] = g_ref[ROWS - FAR : ROWS]
-    down_ref[FAR : 2 * FAR] = d_ref[ROWS - FAR : ROWS]
+    beside = received(1)
+    for n, (halo_d, out_ref) in enumerate(((south_d, south_ref), (north_d, north_ref))):
+        out_ref[FAR : 2 * FAR] = halo_d[0:FAR]
+        for tile in range(2):
+            whole = tile == 1 - n
+            rows = range(CY) if whole else (range(2 * CY - FAR, CY) if n == 0 else range(FAR - CY))
+            at = (0, FAR - CY)[tile] if n == 0 else (0, CY)[tile]
+            table = jnp.concatenate(
+                [halo_d[FAR, (tile * parts + m) * 8 : (tile * parts + m + 1) * 8, :] for m in range(parts)], axis=1
+            )
+            size = len(rows) * COLS
+            fill(table, rows, beside_high, beside_low)
+            target = beside[(2 * n + tile) * WIN : (2 * n + tile + 1) * WIN]
+            flat = spread_out(target, beside_high.at[0:size], beside_low.at[0:size])
+            for m in range(len(rows)):
+                out_ref[at + m] = jnp.sqrt(halo_d[at + m]) * flat[:, m * COLS : (m + 1) * COLS]
 
 
 def places(halo):
@@ -321,7 +370,7 @@
         values = [whole_sum(s * keep) for s in sums]
         quad = sum(weight_ref[tile] * (samples[tile] * iv) * (samples[tile] * iv) for tile in range(2))
         values += [whole_sum(quad * keep), t0, t1, v1]
-        stats_ref[...] = jnp.broadcast_to(as_row(values)[None], stats_ref.shape)
+        stats_ref[...] = jnp.broadcast_to(as_row(values), stats_ref.shape)
 
 
 def as_row(values):
@@ -341,7 +390,7 @@
 
 
 def merge_body(in_ref, out_ref):
-    out_ref[...] = jnp.broadcast_to(as_row(merged(in_ref[:, 0, :]))[None], out_ref.shape)
+    out_ref[...] = jnp.broadcast_to(as_row(merged(in_ref[...]))[None], out_ref.shape)
 
 
 def last_body(core_ref, here_ref, south_ref, north_ref, east_ref, west_ref, wide_d, q0_ref, q1_ref, *outs):
@@ -407,9 +456,11 @@
         return lax.ppermute(value, "gy", [(i, i ^ 1) for i in range(count_y)])
 
     def exchange(heres, up, down, halo):
+        return sideways(heres, along_y(down, 2), along_y(up, -2), halo)
+
+    def sideways(heres, south, north, halo):
         kinds = len(heres)
         tiles = places(halo)[1]
-        south, north = along_y(down, 2), along_y(up, -2)
         pack = call(functools.partial(strips_body, halo, kinds), [f32(kinds * tiles, WIN, COLS)] * 2, 10**6)
         west, east = pack(*heres, south, north)
         return south, north, along_x(west, -1), along_x(east, 1)
@@ -422,7 +473,7 @@
     space += [pltpu.VMEM((2 * FULL, count), jnp.float32), pltpu.VMEM((FULL * CY, COLS), jnp.float32)]
     chunks, mine, mate, table = call(
         first_body,
-        [f32(slots, COLS), f32(CY, WIN, COLS), f32(CY * WIN + 8 * (slots // COLS), COLS), f32(8, slots)],
+        [f32(2 * slots, COLS), f32(CY, WIN, COLS), f32(CY * WIN + 8 * (slots // COLS), COLS), f32(8, slots)],
         10**7,
         space + [pltpu.SemaphoreType.DMA((len(ins),))],
         1,
@@ -431,13 +482,19 @@
     theirs = across(mate)
     received = lax.all_to_all(chunks, "gy", split_axis=0, concat_axis=0, tiled=True)
     matrix = jax.ShapeDtypeStruct((2, CY * COLS, slots), jnp.bfloat16)
+    sent = f32(FAR + 1, WIN, COLS)
+    d, tables, up, down = call(chip_body, [field, f32(2, 8, slots), sent, sent], 10**6, (), 1)(
+        core, mine, theirs, table
+    )
     both = f32(2 * FAR, WIN, COLS)
-    d, high, low, weights, g, up, down = call(
-        seed_body, [field, matrix, matrix, f32(2, WIN, slots), field, both, both], 10**8, (), 1
-    )(core, mine, theirs, table, received)
+    space = [pltpu.VMEM((slots, COLS), jnp.float32)] + [pltpu.VMEM((CY * COLS, slots), jnp.bfloat16)] * 2
+    outs = [matrix, matrix, f32(2, WIN, slots), field, both, both]
+    high, low, weights, g, south, north = call(seed_body, outs, 10**8, space)(
+        d, tables, along_y(down, 2), along_y(up, -2), received
+    )
     wide = (ROWS + 2 * FAR, WIN, 2 * COLS)
     space = [pltpu.VMEM(wide, jnp.float32)] * 2
-    south, north, east, west = exchange([g, d], up, down, FAR)
+    south, north, east, west = sideways([g, d], south, north, FAR)
     q0, u0, wide_d, up, down, g = call(
         functools.partial(pair_body, False),
         [field, field, f32(*wide), f32(FAR, WIN, COLS), f32(FAR, WIN, COLS), field],
@@ -448,7 +505,7 @@
     south, north, east, west = exchange([g], up, down, FAR)
     q1, up, down, g, stats = call(
         functools.partial(pair_body, True),
-        [field, f32(STEPS, WIN, COLS), f32(STEPS, WIN, COLS), field, f32(count_y, 1, COLS)],
+        [field, f32(STEPS, WIN, COLS), f32(STEPS, WIN, COLS), field, f32(count_y, COLS)],
         2 * 10**8,
         space,
         1,

time: 139 us -> 132 us (0.950)
  waiting for transfers between devices: 40.7 us -> 31.6 us
    all_to_all x1, waiting for transfers between devices: 7.02 us -> 0.01 us  [on_device(): lax.all_to_all(chunks, 'gy', split_axis=0, concat_axis=0, tiled=True)]
    ppermute x6, starting transfers between devices: 12 us -> 14.3 us  [along_y(): return lax.ppermute(value, 'gy', pairs)]
    ppermute x6, waiting for transfers between devices: 13.9 us -> 11.8 us  [along_y(): return lax.ppermute(value, 'gy', pairs)]
    pallas_call x10 -> x11, Pallas kernels: 20 us -> 21.3 us  [run(): pl.pallas_call(body, out_shape=tuple(outs), in_specs=specs, out_specs=tup...]
  transfers between devices with their start and end apart: 17 -> 17, of which waited for: 11 -> 10; matrix products, arithmetic and copies ran while one was open for 0% -> 0% of each run, Pallas kernels for 2% -> 2%
where the time goes in v5:
time: 132 us
  starting transfers between devices  77.9 us (59%)
  waiting for transfers between devices  31.6 us (24%)
  Pallas kernels  21.3 us (16%)
    ppermute x6, starting transfers between devices, along_x(): lax.ppermute(value, 'gx', [(i, (i + by) % count_x) for i in range(count_x)])  24 us
    pallas_call x11, Pallas kernels, run(): pl.pallas_call(body, out_shape=tuple(outs), in_specs=specs, out_specs=tup...  21.3 us
    all_to_all x1, starting transfers between devices, on_device(): stats = lax.all_to_all(stats, 'gy', split_axis=0, concat_axis=0, tiled=True)  15.3 us
    all_to_all x1, starting transfers between devices, on_device(): lax.all_to_all(chunks, 'gy', split_axis=0, concat_axis=0, tiled=True)  14.6 us
    ppermute x6, starting transfers between devices, along_y(): return lax.ppermute(value, 'gy', pairs)  14.3 us
    ppermute x6, waiting for transfers between devices, along_y(): return lax.ppermute(value, 'gy', pairs)  11.8 us
    ppermute x6, waiting for transfers between devices, along_x(): lax.ppermute(value, 'gx', [(i, (i + by) % count_x) for i in range(count_x)])  7.13 us
    all_to_all x1, waiting for transfers between devices, on_device(): stats = lax.all_to_all(stats, 'gx', split_axis=0, concat_axis=0, tiled=True)  6.72 us
  transfers between devices with their start and end apart: 17, of which 10 were waited for; matrix products, arithmetic and copies ran while one was open for 0% of the time, Pallas kernels for 2%

profile of v5, /device:TPU:1, one launch (start us, length us, event | category | flops | bytes accessed | tf_op | source)
XLA Modules:
  0.0 131.6 jit_solution(17633305043057429616)
XLA Ops:
  0.6 2.3 %shard_map.86 = (f32[512,128]{1,0:T(8,128)}, f32[8,32,128]{2,1,0:T(8,128)S(1)}, f32[272,128]{1,0:T(8,128)S(1)}, f32[8,256]{1,0:T(8,128)S(1)}) custom-call(s32[1]{0:T(128)} %bitcast.core_ref.refs_0_, s32[1,128]{1,0:T(1,128)} %bitcast.10, f32[50,128]{1,0:T(8,128)} %refs_1_.1, f32[50,128]{1,0:T(8,128)} %refs_2_.1, f32[50,8,128]{2,1,0:T(8,128)} %refs_3_.1, ...), custom_call_target="tpu_custom_call" | custom-call | flops 10000000 | bytes 806404 | tf_op jit(solution)/shard_map/pallas_call | solution.py:27
  3.0 14.6 %all-to-all-start = ((f32[64,8,128]{2,1,0:T(8,128)}), f32[64,8,128]{2,1,0:T(8,128)S(1)}, u32[]{:S(2)}, u32[]{:S(2)}) async-start(f32[64,8,128]{2,1,0:T(8,128)} %bitcast.2), calls=%async_computation | async-start | bytes 524288 | tf_op jit(solution)/shard_map/all_to_all | solution.py:483
  17.5 2.5 %collective-permute-start = (f32[272,128]{1,0:T(8,128)S(1)}, f32[272,128]{1,0:T(8,128)S(1)}, u32[]{:S(2)}, u32[]{:S(2)}) collective-permute-start(f32[272,128]{1,0:T(8,128)S(1)} %get-tuple-element.38), channel_id=1, source_target_pairs={{0,1},{1,0},{2,3},{3,2},{4,5},{5,4},{6,7},{7,6},{8,9},{9,8},{10,11... | collective-permute-start | bytes 417800 | tf_op jit(solution)/shard_map/ppermute | solution.py:456
  20.0 1.0 collective-permute-done.theirs_ref
  21.0 3.1 %collective-permute-start.1 = (f32[11,32,128]{2,1,0:T(8,128)S(1)}, f32[11,32,128]{2,1,0:T(8,128)S(1)}, u32[]{:S(2)}, u32[]{:S(2)}) collective-permute-start(f32[11,32,128]{2,1,0:T(8,128)S(1)} %get-tuple-element.42), channel_id=1, source_target_pairs={{0,2},{1,3},{2,4},{3,5},{4,6},{5,7},{6,8},{7,9},{8,10},{9,11},{10,... | collective-permute-start | bytes 540680 | tf_op jit(solution)/shard_map/ppermute | solution.py:450
  24.2 1.3 collective-permute-start.2
  25.5 2.8 %collective-permute-done.1.south_d = f32[11,32,128]{2,1,0:T(8,128)S(1)} collective-permute-done((f32[11,32,128]{2,1,0:T(8,128)S(1)}, f32[11,32,128]{2,1,0:T(8,128)S(1)}, u32[]{:S(2)}, u32[]{:S(2)}) %collective-permute-start.1) | collective-permute-done | bytes 180256 | tf_op jit(solution)/shard_map/ppermute | solution.py:450
  28.3 3.2 %collective-permute-done.2.north_d = f32[11,32,128]{2,1,0:T(8,128)S(1)} collective-permute-done((f32[11,32,128]{2,1,0:T(8,128)S(1)}, f32[11,32,128]{2,1,0:T(8,128)S(1)}, u32[]{:S(2)}, u32[]{:S(2)}) %collective-permute-start.2) | collective-permute-done | bytes 180256 | tf_op jit(solution)/shard_map/ppermute | solution.py:450
  31.5 0.0 all-to-all-done
  31.5 2.0 %shard_map.88 = (bf16[2,1024,256]{2,1,0:T(8,128)(2,1)S(1)}, bf16[2,1024,256]{2,1,0:T(8,128)(2,1)S(1)}, f32[2,32,256]{2,1,0:T(8,128)S(1)}, f32[16,32,128]{2,1,0:T...) custom-call(f32[16,32,128]{2,1,0:T(8,128)S(1)} %get-tuple-element.40.d_ref.refs_1_.refs_6_, ...), custom_call_target="tpu_custom_call" | custom-call | flops 100000000 | bytes 3981312 | tf_op jit(solution)/shard_map/pallas_call | solution.py:27
  33.5 0.6 shard_map.89
  34.1 11.4 %collective-permute-start.3 = (f32[6,32,128]{2,1,0:T(8,128)S(1)}, f32[6,32,128]{2,1,0:T(8,128)S(1)}, u32[]{:S(2)}, u32[]{:S(2)}) collective-permute-start(f32[6,32,128]{2,1,0:T(8,128)S(1)} %get-tuple-element.48), channel_id=1, source_target_pairs={{0,704},{64,0},{128,64},{192,128},{256,192},{320,256},{384,320},{4... | collective-permute-start | bytes 294920 | tf_op jit(solution)/shard_map/ppermute | solution.py:453
  45.5 1.9 %collective-permute-start.4 = (f32[6,32,128]{2,1,0:T(8,128)S(1)}, f32[6,32,128]{2,1,0:T(8,128)S(1)}, u32[]{:S(2)}, u32[]{:S(2)}) collective-permute-start(f32[6,32,128]{2,1,0:T(8,128)S(1)} %get-tuple-element.49), channel_id=1, source_target_pairs={{0,64},{64,128},{128,192},{192,256},{256,320},{320,384},{384,448},... | collective-permute-start | bytes 294920 | tf_op jit(solution)/shard_map/ppermute | solution.py:453
  47.4 0.0 collective-permute-done.3.refs_4_
  47.4 4.6 %collective-permute-done.4.refs_5_ = f32[6,32,128]{2,1,0:T(8,128)S(1)} collective-permute-done((f32[6,32,128]{2,1,0:T(8,128)S(1)}, f32[6,32,128]{2,1,0:T(8,128)S(1)}, u32[]{:S(2)}, u32[]{:S(2)}) %collective-permute-start.4) | collective-permute-done | bytes 98336 | tf_op jit(solution)/shard_map/ppermute | solution.py:453
  52.1 5.8 %shard_map.90 = (f32[16,32,128]{2,1,0:T(8,128)S(1)}, f32[16,32,128]{2,1,0:T(8,128)S(1)}, f32[36,32,256]{2,1,0:T(8,128)S(1)}, f32[10,32,128]{2,1,0:T(8,128)S(1)},...) custom-call(s32[1]{0:T(128)} %bitcast.core_ref.refs_0_, f32[16,32,128]{2,1,0:T(8,128)S(1)} %get-tuple-element.45.refs_0_.refs_1_, ...), custom_call_target="tpu_custom_call" | custom-call | flops 200000000 | bytes 5832708 | tf_op jit(solution)/shard_map/pallas_call | solution.py:27
  57.9 3.1 %collective-permute-start.5 = (f32[10,32,128]{2,1,0:T(8,128)S(1)}, f32[10,32,128]{2,1,0:T(8,128)S(1)}, u32[]{:S(2)}, u32[]{:S(2)}) collective-permute-start(f32[10,32,128]{2,1,0:T(8,128)S(1)} %get-tuple-element.54), channel_id=1, source_target_pairs={{0,2},{1,3},{2,4},{3,5},{4,6},{5,7},{6,8},{7,9},{8,10},{9,11},{10,... | collective-permute-start | bytes 491528 | tf_op jit(solution)/shard_map/ppermute | solution.py:450
  61.0 1.3 collective-permute-start.6
  62.3 0.9 collective-permute-done.5.refs_1_.refs_2_
  63.2 4.8 %collective-permute-done.6.refs_2_.refs_3_ = f32[10,32,128]{2,1,0:T(8,128)S(1)} collective-permute-done((f32[10,32,128]{2,1,0:T(8,128)S(1)}, f32[10,32,128]{2,1,0:T(8,128)S(1)}, u32[]{:S(2)}, u32[]{:S(2)}) %collective-permute-start.6) | collective-permute-done | bytes 163872 | tf_op jit(solution)/shard_map/ppermute | solution.py:450
  68.0 0.3 shard_map.91
  68.4 1.9 %collective-permute-start.7 = (f32[3,32,128]{2,1,0:T(8,128)S(1)}, f32[3,32,128]{2,1,0:T(8,128)S(1)}, u32[]{:S(2)}, u32[]{:S(2)}) collective-permute-start(f32[3,32,128]{2,1,0:T(8,128)S(1)} %get-tuple-element.56), channel_id=1, source_target_pairs={{0,704},{64,0},{128,64},{192,128},{256,192},{320,256},{384,320},{4... | collective-permute-start | bytes 147464 | tf_op jit(solution)/shard_map/ppermute | solution.py:453
  70.3 3.5 %collective-permute-start.8 = (f32[3,32,128]{2,1,0:T(8,128)S(1)}, f32[3,32,128]{2,1,0:T(8,128)S(1)}, u32[]{:S(2)}, u32[]{:S(2)}) collective-permute-start(f32[3,32,128]{2,1,0:T(8,128)S(1)} %get-tuple-element.57), channel_id=1, source_target_pairs={{0,64},{64,128},{128,192},{192,256},{256,320},{320,384},{384,448},... | collective-permute-start | bytes 147464 | tf_op jit(solution)/shard_map/ppermute | solution.py:453
  73.8 0.0 collective-permute-done.7.refs_4_
  73.8 2.5 %collective-permute-done.8.refs_5_ = f32[3,32,128]{2,1,0:T(8,128)S(1)} collective-permute-done((f32[3,32,128]{2,1,0:T(8,128)S(1)}, f32[3,32,128]{2,1,0:T(8,128)S(1)}, u32[]{:S(2)}, u32[]{:S(2)}) %collective-permute-start.8) | collective-permute-done | bytes 49184 | tf_op jit(solution)/shard_map/ppermute | solution.py:453
  76.3 5.8 %shard_map.92 = (f32[16,32,128]{2,1,0:T(8,128)S(1)}, f32[5,32,128]{2,1,0:T(8,128)S(1)}, f32[5,32,128]{2,1,0:T(8,128)S(1)}, f32[16,32,128]{2,1,0:T(8,128)S(1)}, f32[64,128]{1,0:T(8,128)}) custom-call(s32[1]{0:T(128)} %bitcast.core_ref.refs_0_, f32[16,32,128]{2,1,0:T(8,128)S(1)} %get-tuple-element.53.refs_0_.refs_1_, ...), custom_call_target="tpu_custom_call" | custom-call | flops 200000000 | bytes 5275652 | tf_op jit(solution)/shard_map/pallas_call | solution.py:27
  82.2 4.2 %collective-permute-start.9 = (f32[5,32,128]{2,1,0:T(8,128)S(1)}, f32[5,32,128]{2,1,0:T(8,128)S(1)}, u32[]{:S(2)}, u32[]{:S(2)}) collective-permute-start(f32[5,32,128]{2,1,0:T(8,128)S(1)} %get-tuple-element.62), channel_id=1, source_target_pairs={{0,2},{1,3},{2,4},{3,5},{4,6},{5,7},{6,8},{7,9},{8,10},{9,11},{10,... | collective-permute-start | bytes 245768 | tf_op jit(solution)/shard_map/ppermute | solution.py:450
  86.4 1.3 collective-permute-start.10
  87.7 15.3 %all-to-all-start.1 = ((f32[64,1,128]{2,1,0:T(1,128)}), f32[64,1,128]{2,1,0:T(1,128)S(1)}, u32[]{:S(2)}, u32[]{:S(2)}) async-start(f32[64,1,128]{2,1,0:T(1,128)} %bitcast.5), calls=%async_computation.1 | async-start | bytes 65536 | tf_op jit(solution)/shard_map/all_to_all | solution.py:513
  103.1 0.0 collective-permute-done.9.refs_1_.south_ref
  103.1 0.0 collective-permute-done.10.refs_2_.north_ref
  103.1 0.3 shard_map.93
  103.4 1.9 %collective-permute-start.11 = (f32[1,32,128]{2,1,0:T(8,128)S(1)}, f32[1,32,128]{2,1,0:T(8,128)S(1)}, u32[]{:S(2)}, u32[]{:S(2)}) collective-permute-start(f32[1,32,128]{2,1,0:T(8,128)S(1)} %get-tuple-element.64), channel_id=1, source_target_pairs={{0,704},{64,0},{128,64},{192,128},{256,192},{320,256},{384,320},{4... | collective-permute-start | bytes 49160 | tf_op jit(solution)/shard_map/ppermute | solution.py:453
  105.3 3.4 %collective-permute-start.12 = (f32[1,32,128]{2,1,0:T(8,128)S(1)}, f32[1,32,128]{2,1,0:T(8,128)S(1)}, u32[]{:S(2)}, u32[]{:S(2)}) collective-permute-start(f32[1,32,128]{2,1,0:T(8,128)S(1)} %get-tuple-element.65), channel_id=1, source_target_pairs={{0,64},{64,128},{128,192},{192,256},{256,320},{320,384},{384,448},... | collective-permute-start | bytes 49160 | tf_op jit(solution)/shard_map/ppermute | solution.py:453
  108.7 3.6 %all-to-all-done.1 = f32[64,1,128]{2,1,0:T(1,128)S(1)} async-done(((f32[64,1,128]{2,1,0:T(1,128)}), f32[64,1,128]{2,1,0:T(1,128)S(1)}, u32[]{:S(2)}, u32[]{:S(2)}) %all-to-all-start.1) | async-done | bytes 32800 | tf_op jit(solution)/shard_map/all_to_all | solution.py:513
  112.3 0.8 shard_map.95
  113.1 3.5 %all-to-all-start.2 = ((f32[12,1,128]{2,1,0:T(1,128)}), f32[12,1,128]{2,1,0:T(1,128)S(1)}, u32[]{:S(2)}, u32[]{:S(2)}) async-start(f32[12,1,128]{2,1,0:T(1,128)} %shard_map.95), calls=%async_computation.2 | async-start | bytes 12288 | tf_op jit(solution)/shard_map/all_to_all | solution.py:516
  116.6 0.0 collective-permute-done.11.east_ref
  116.6 0.0 collective-permute-done.12.west_ref
  116.6 2.0 %shard_map.94 = (f32[24,32,128]{2,1,0:T(8,128)S(1)}, f32[24,32,128]{2,1,0:T(8,128)S(1)}) custom-call(s32[1]{0:T(128)} %bitcast.core_ref.refs_0_, f32[16,32,128]{2,1,0:T(8,128)S(1)} %get-tuple-element.61.refs_0_.here_ref, f32[5,32,128]{2,1,0:T(8,128)S(1)} %collective-permute-done.9.refs_1_.south_ref, ...), custom_call_target="tpu_custom_call" | custom-call | flops 100000000 | bytes 2949124 | tf_op jit(solution)/shard_map/pallas_call | solution.py:27
  118.6 6.7 %all-to-all-done.2.stats_ref = f32[12,1,128]{2,1,0:T(1,128)S(1)} async-done(((f32[12,1,128]{2,1,0:T(1,128)}), f32[12,1,128]{2,1,0:T(1,128)S(1)}, u32[]{:S(2)}, u32[]{:S(2)}) %all-to-all-start.2) | async-done | bytes 6176 | tf_op jit(solution)/shard_map/all_to_all | solution.py:516
  125.3 3.7 %collective-permute-start.13 = (f32[24,32,128]{2,1,0:T(8,128)S(1)}, f32[24,32,128]{2,1,0:T(8,128)S(1)}, u32[]{:S(2)}, u32[]{:S(2)}) collective-permute-start(f32[24,32,128]{2,1,0:T(8,128)S(1)} %get-tuple-element.70), channel_id=1, source_target_pairs={{0,1},{1,0},{2,3},{3,2},{4,5},{5,4},{6,7},{7,6},{8,9},{9,8},{10,11... | collective-permute-start | bytes 1179656 | tf_op jit(solution)/shard_map/ppermute | solution.py:456
  129.0 1.3 %collective-permute-done.13.theirs_ref = f32[24,32,128]{2,1,0:T(8,128)S(1)} collective-permute-done((f32[24,32,128]{2,1,0:T(8,128)S(1)}, f32[24,32,128]{2,1,0:T(8,128)S(1)}, u32[]{:S(2)}, u32[]{:S(2)}) %collective-permute-start.13) | collective-permute-done | bytes 393248 | tf_op jit(solution)/shard_map/ppermute | solution.py:456
  130.4 1.2 shard_map.96
  (1 shorter events, 0.0 us)
Async XLA Ops:
  3.0 28.6 %all-to-all-start = ((f32[64,8,128]{2,1,0:T(8,128)}), f32[64,8,128]{2,1,0:T(8,128)S(1)}, u32[]{:S(2)}, u32[]{:S(2)}) async-start(f32[64,8,128]{2,1,0:T(8,128)} %bitcast.2), calls=%async_computation | async-start | bytes 524288 | tf_op jit(solution)/shard_map/all_to_all | solution.py:483
  17.5 3.5 %collective-permute-start = (f32[272,128]{1,0:T(8,128)S(1)}, f32[272,128]{1,0:T(8,128)S(1)}, u32[]{:S(2)}, u32[]{:S(2)}) collective-permute-start(f32[272,128]{1,0:T(8,128)S(1)} %get-tuple-element.38), channel_id=1, source_target_pairs={{0,1},{1,0},{2,3},{3,2},{4,5},{5,4},{6,7},{7,6},{8,9},{9,8},{10,11... | collective-permute-start | bytes 417800 | tf_op jit(solution)/shard_map/ppermute | solution.py:456
  21.0 7.2 %collective-permute-start.1 = (f32[11,32,128]{2,1,0:T(8,128)S(1)}, f32[11,32,128]{2,1,0:T(8,128)S(1)}, u32[]{:S(2)}, u32[]{:S(2)}) collective-permute-start(f32[11,32,128]{2,1,0:T(8,128)S(1)} %get-tuple-element.42), channel_id=1, source_target_pairs={{0,2},{1,3},{2,4},{3,5},{4,6},{5,7},{6,8},{7,9},{8,10},{9,11},{10,... | collective-permute-start | bytes 540680 | tf_op jit(solution)/shard_map/ppermute | solution.py:450
  24.2 7.4 %collective-permute-start.2 = (f32[11,32,128]{2,1,0:T(8,128)S(1)}, f32[11,32,128]{2,1,0:T(8,128)S(1)}, u32[]{:S(2)}, u32[]{:S(2)}) collective-permute-start(f32[11,32,128]{2,1,0:T(8,128)S(1)} %get-tuple-element.43), channel_id=1, source_target_pairs={{2,0},{3,1},{4,2},{5,3},{6,4},{7,5},{8,6},{9,7},{10,8},{11,9},{12,... | collective-permute-start | bytes 540680 | tf_op jit(solution)/shard_map/ppermute | solution.py:450
  34.1 13.3 %collective-permute-start.3 = (f32[6,32,128]{2,1,0:T(8,128)S(1)}, f32[6,32,128]{2,1,0:T(8,128)S(1)}, u32[]{:S(2)}, u32[]{:S(2)}) collective-permute-start(f32[6,32,128]{2,1,0:T(8,128)S(1)} %get-tuple-element.48), channel_id=1, source_target_pairs={{0,704},{64,0},{128,64},{192,128},{256,192},{320,256},{384,320},{4... | collective-permute-start | bytes 294920 | tf_op jit(solution)/shard_map/ppermute | solution.py:453
  45.5 6.6 %collective-permute-start.4 = (f32[6,32,128]{2,1,0:T(8,128)S(1)}, f32[6,32,128]{2,1,0:T(8,128)S(1)}, u32[]{:S(2)}, u32[]{:S(2)}) collective-permute-start(f32[6,32,128]{2,1,0:T(8,128)S(1)} %get-tuple-element.49), channel_id=1, source_target_pairs={{0,64},{64,128},{128,192},{192,256},{256,320},{320,384},{384,448},... | collective-permute-start | bytes 294920 | tf_op jit(solution)/shard_map/ppermute | solution.py:453
  57.9 5.3 %collective-permute-start.5 = (f32[10,32,128]{2,1,0:T(8,128)S(1)}, f32[10,32,128]{2,1,0:T(8,128)S(1)}, u32[]{:S(2)}, u32[]{:S(2)}) collective-permute-start(f32[10,32,128]{2,1,0:T(8,128)S(1)} %get-tuple-element.54), channel_id=1, source_target_pairs={{0,2},{1,3},{2,4},{3,5},{4,6},{5,7},{6,8},{7,9},{8,10},{9,11},{10,... | collective-permute-start | bytes 491528 | tf_op jit(solution)/shard_map/ppermute | solution.py:450
  61.0 7.0 %collective-permute-start.6 = (f32[10,32,128]{2,1,0:T(8,128)S(1)}, f32[10,32,128]{2,1,0:T(8,128)S(1)}, u32[]{:S(2)}, u32[]{:S(2)}) collective-permute-start(f32[10,32,128]{2,1,0:T(8,128)S(1)} %get-tuple-element.55), channel_id=1, source_target_pairs={{2,0},{3,1},{4,2},{5,3},{6,4},{7,5},{8,6},{9,7},{10,8},{11,9},{12,... | collective-permute-start | bytes 491528 | tf_op jit(solution)/shard_map/ppermute | solution.py:450
  68.4 5.5 %collective-permute-start.7 = (f32[3,32,128]{2,1,0:T(8,128)S(1)}, f32[3,32,128]{2,1,0:T(8,128)S(1)}, u32[]{:S(2)}, u32[]{:S(2)}) collective-permute-start(f32[3,32,128]{2,1,0:T(8,128)S(1)} %get-tuple-element.56), channel_id=1, source_target_pairs={{0,704},{64,0},{128,64},{192,128},{256,192},{320,256},{384,320},{4... | collective-permute-start | bytes 147464 | tf_op jit(solution)/shard_map/ppermute | solution.py:453
  70.3 6.0 %collective-permute-start.8 = (f32[3,32,128]{2,1,0:T(8,128)S(1)}, f32[3,32,128]{2,1,0:T(8,128)S(1)}, u32[]{:S(2)}, u32[]{:S(2)}) collective-permute-start(f32[3,32,128]{2,1,0:T(8,128)S(1)} %get-tuple-element.57), channel_id=1, source_target_pairs={{0,64},{64,128},{128,192},{192,256},{256,320},{320,384},{384,448},... | collective-permute-start | bytes 147464 | tf_op jit(solution)/shard_map/ppermute | solution.py:453
  82.2 20.9 %collective-permute-start.9 = (f32[5,32,128]{2,1,0:T(8,128)S(1)}, f32[5,32,128]{2,1,0:T(8,128)S(1)}, u32[]{:S(2)}, u32[]{:S(2)}) collective-permute-start(f32[5,32,128]{2,1,0:T(8,128)S(1)} %get-tuple-element.62), channel_id=1, source_target_pairs={{0,2},{1,3},{2,4},{3,5},{4,6},{5,7},{6,8},{7,9},{8,10},{9,11},{10,... | collective-permute-start | bytes 245768 | tf_op jit(solution)/shard_map/ppermute | solution.py:450
  86.4 16.6 %collective-permute-start.10 = (f32[5,32,128]{2,1,0:T(8,128)S(1)}, f32[5,32,128]{2,1,0:T(8,128)S(1)}, u32[]{:S(2)}, u32[]{:S(2)}) collective-permute-start(f32[5,32,128]{2,1,0:T(8,128)S(1)} %get-tuple-element.63), channel_id=1, source_target_pairs={{2,0},{3,1},{4,2},{5,3},{6,4},{7,5},{8,6},{9,7},{10,8},{11,9},{12,... | collective-permute-start | bytes 245768 | tf_op jit(solution)/shard_map/ppermute | solution.py:450
  87.7 24.5 %all-to-all-start.1 = ((f32[64,1,128]{2,1,0:T(1,128)}), f32[64,1,128]{2,1,0:T(1,128)S(1)}, u32[]{:S(2)}, u32[]{:S(2)}) async-start(f32[64,1,128]{2,1,0:T(1,128)} %bitcast.5), calls=%async_computation.1 | async-start | bytes 65536 | tf_op jit(solution)/shard_map/all_to_all | solution.py:513
  103.4 13.2 %collective-permute-start.11 = (f32[1,32,128]{2,1,0:T(8,128)S(1)}, f32[1,32,128]{2,1,0:T(8,128)S(1)}, u32[]{:S(2)}, u32[]{:S(2)}) collective-permute-start(f32[1,32,128]{2,1,0:T(8,128)S(1)} %get-tuple-element.64), channel_id=1, source_target_pairs={{0,704},{64,0},{128,64},{192,128},{256,192},{320,256},{384,320},{4... | collective-permute-start | bytes 49160 | tf_op jit(solution)/shard_map/ppermute | solution.py:453
  105.3 11.3 %collective-permute-start.12 = (f32[1,32,128]{2,1,0:T(8,128)S(1)}, f32[1,32,128]{2,1,0:T(8,128)S(1)}, u32[]{:S(2)}, u32[]{:S(2)}) collective-permute-start(f32[1,32,128]{2,1,0:T(8,128)S(1)} %get-tuple-element.65), channel_id=1, source_target_pairs={{0,64},{64,128},{128,192},{192,256},{256,320},{320,384},{384,448},... | collective-permute-start | bytes 49160 | tf_op jit(solution)/shard_map/ppermute | solution.py:453
  113.1 12.2 %all-to-all-start.2 = ((f32[12,1,128]{2,1,0:T(1,128)}), f32[12,1,128]{2,1,0:T(1,128)S(1)}, u32[]{:S(2)}, u32[]{:S(2)}) async-start(f32[12,1,128]{2,1,0:T(1,128)} %shard_map.95), calls=%async_computation.2 | async-start | bytes 12288 | tf_op jit(solution)/shard_map/all_to_all | solution.py:516
  125.3 5.0 %collective-permute-start.13 = (f32[24,32,128]{2,1,0:T(8,128)S(1)}, f32[24,32,128]{2,1,0:T(8,128)S(1)}, u32[]{:S(2)}, u32[]{:S(2)}) collective-permute-start(f32[24,32,128]{2,1,0:T(8,128)S(1)} %get-tuple-element.70), channel_id=1, source_target_pairs={{0,1},{1,0},{2,3},{3,2},{4,5},{5,4},{6,7},{7,6},{8,9},{9,8},{10,11... | collective-permute-start | bytes 1179656 | tf_op jit(solution)/shard_map/ppermute | solution.py:456

commit v6 on v5

--- a/solution.py
+++ b/solution.py
@@ -273,24 +273,26 @@
 
 
 def sweep(src, dst, d_ref, low, high):
+    at = lax.broadcasted_iota(jnp.int32, (COLS, 2 * COLS), 0)
+    to = lax.broadcasted_iota(jnp.int32, (COLS, 2 * COLS), 1)
+    near = (jnp.abs(at - to) == 1) & (to < COLS)
+    cross = ((at == 0) & (to == 2 * COLS - 1)) | ((at == COLS - 1) & (to == COLS))
+    shift = jnp.where(near | cross, 1.0, 0.0).astype(jnp.bfloat16)
     lane = lax.broadcasted_iota(jnp.int32, (WIN, COLS), 1)
     last, first = lane == COLS - 1, lane == 0
-
-    def body(row, carry):
-        before, now = carry
+    before, now = src[low - 1], src[low]
+    for row in range(low, high):
         after = src[row + 1]
         a, b = now[:, :COLS], now[:, COLS:]
-        east_a, east_b = pltpu.roll(a, COLS - 1, 1), pltpu.roll(b, COLS - 1, 1)
-        west_a, west_b = pltpu.roll(a, 1, 1), pltpu.roll(b, 1, 1)
-        beside_a = jnp.where(last, east_b, east_a) + jnp.where(first, west_b, west_a)
-        beside_b = jnp.where(last, east_a, east_b) + jnp.where(first, west_a, west_b)
+        x, y = split(a)
+        both = dot(jnp.concatenate([x, y], axis=0), shift, ((1,), (0,)))
+        both = both[:WIN] + both[WIN:]
+        e, w = pltpu.roll(b, COLS - 1, 1), pltpu.roll(b, 1, 1)
+        beside_a = both[:, :COLS] + jnp.where(last, e, jnp.where(first, w, 0.0))
+        beside_b = both[:, COLS:] + jnp.where(last, 0.0, e) + jnp.where(first, 0.0, w)
         beside = jnp.concatenate([beside_a, beside_b], axis=1)
         dst[row] = now + d_ref[row] * (before + after + beside - 4.0 * now)
-        return now, after
-
-    carry = (src[low - 1], src[low])
-    for row in range(low, high):
-        carry = body(row, carry)
+        before, now = now, after
 
 
 def unscale(value, d):

time: 132 us -> 131 us (level)
  Pallas kernels: 21.3 us -> 19.2 us
    pallas_call x11, Pallas kernels: 21.3 us -> 19.2 us  [run(): pl.pallas_call(body, out_shape=tuple(outs), in_specs=specs, out_specs=tup...]
where the time goes in v6:
time: 131 us; the launch traced here: 130 us
  starting transfers between devices  77.9 us (59%)
  waiting for transfers between devices  32.1 us (25%)
  Pallas kernels  19.2 us (15%)
    ppermute x6, starting transfers between devices, along_x(): lax.ppermute(value, 'gx', [(i, (i + by) % count_x) for i in range(count_x)])  24 us
    pallas_call x11, Pallas kernels, run(): pl.pallas_call(body, out_shape=tuple(outs), in_specs=specs, out_specs=tup...  19.2 us
    all_to_all x1, starting transfers between devices, on_device(): stats = lax.all_to_all(stats, 'gy', split_axis=0, concat_axis=0, tiled=True)  15.3 us
    all_to_all x1, starting transfers between devices, on_device(): lax.all_to_all(chunks, 'gy', split_axis=0, concat_axis=0, tiled=True)  14.6 us
    ppermute x6, starting transfers between devices, along_y(): return lax.ppermute(value, 'gy', pairs)  14.3 us
    ppermute x6, waiting for transfers between devices, along_y(): return lax.ppermute(value, 'gy', pairs)  11.8 us
    all_to_all x1, waiting for transfers between devices, on_device(): stats = lax.all_to_all(stats, 'gx', split_axis=0, concat_axis=0, tiled=True)  7.2 us
    ppermute x6, waiting for transfers between devices, along_x(): lax.ppermute(value, 'gx', [(i, (i + by) % count_x) for i in range(count_x)])  7.13 us
  transfers between devices with their start and end apart: 17, of which 10 were waited for; matrix products, arithmetic and copies ran while one was open for 0% of the time, Pallas kernels for 2%

profile of v6, /device:TPU:1, one launch (start us, length us, event | category | flops | bytes accessed | tf_op | source)
XLA Modules:
  0.0 130.0 jit_solution(620189284645479636)
XLA Ops:
  0.6 2.3 %shard_map.86 = (f32[512,128]{1,0:T(8,128)}, f32[8,32,128]{2,1,0:T(8,128)S(1)}, f32[272,128]{1,0:T(8,128)S(1)}, f32[8,256]{1,0:T(8,128)S(1)}) custom-call(s32[1]{0:T(128)} %bitcast.core_ref.refs_0_, s32[1,128]{1,0:T(1,128)} %bitcast.10, f32[50,128]{1,0:T(8,128)} %refs_1_.1, f32[50,128]{1,0:T(8,128)} %refs_2_.1, f32[50,8,128]{2,1,0:T(8,128)} %refs_3_.1, ...), custom_call_target="tpu_custom_call" | custom-call | flops 10000000 | bytes 806404 | tf_op jit(solution)/shard_map/pallas_call | solution.py:27
  3.0 14.6 %all-to-all-start = ((f32[64,8,128]{2,1,0:T(8,128)}), f32[64,8,128]{2,1,0:T(8,128)S(1)}, u32[]{:S(2)}, u32[]{:S(2)}) async-start(f32[64,8,128]{2,1,0:T(8,128)} %bitcast.2), calls=%async_computation | async-start | bytes 524288 | tf_op jit(solution)/shard_map/all_to_all | solution.py:485
  17.5 2.5 %collective-permute-start = (f32[272,128]{1,0:T(8,128)S(1)}, f32[272,128]{1,0:T(8,128)S(1)}, u32[]{:S(2)}, u32[]{:S(2)}) collective-permute-start(f32[272,128]{1,0:T(8,128)S(1)} %get-tuple-element.38), channel_id=1, source_target_pairs={{0,1},{1,0},{2,3},{3,2},{4,5},{5,4},{6,7},{7,6},{8,9},{9,8},{10,11... | collective-permute-start | bytes 417800 | tf_op jit(solution)/shard_map/ppermute | solution.py:458
  20.0 1.0 collective-permute-done.theirs_ref
  21.0 3.1 %collective-permute-start.1 = (f32[11,32,128]{2,1,0:T(8,128)S(1)}, f32[11,32,128]{2,1,0:T(8,128)S(1)}, u32[]{:S(2)}, u32[]{:S(2)}) collective-permute-start(f32[11,32,128]{2,1,0:T(8,128)S(1)} %get-tuple-element.42), channel_id=1, source_target_pairs={{0,2},{1,3},{2,4},{3,5},{4,6},{5,7},{6,8},{7,9},{8,10},{9,11},{10,... | collective-permute-start | bytes 540680 | tf_op jit(solution)/shard_map/ppermute | solution.py:452
  24.2 1.3 collective-permute-start.2
  25.5 2.8 %collective-permute-done.1.south_d = f32[11,32,128]{2,1,0:T(8,128)S(1)} collective-permute-done((f32[11,32,128]{2,1,0:T(8,128)S(1)}, f32[11,32,128]{2,1,0:T(8,128)S(1)}, u32[]{:S(2)}, u32[]{:S(2)}) %collective-permute-start.1) | collective-permute-done | bytes 180256 | tf_op jit(solution)/shard_map/ppermute | solution.py:452
  28.3 3.2 %collective-permute-done.2.north_d = f32[11,32,128]{2,1,0:T(8,128)S(1)} collective-permute-done((f32[11,32,128]{2,1,0:T(8,128)S(1)}, f32[11,32,128]{2,1,0:T(8,128)S(1)}, u32[]{:S(2)}, u32[]{:S(2)}) %collective-permute-start.2) | collective-permute-done | bytes 180256 | tf_op jit(solution)/shard_map/ppermute | solution.py:452
  31.5 0.0 all-to-all-done
  31.5 2.0 %shard_map.88 = (bf16[2,1024,256]{2,1,0:T(8,128)(2,1)S(1)}, bf16[2,1024,256]{2,1,0:T(8,128)(2,1)S(1)}, f32[2,32,256]{2,1,0:T(8,128)S(1)}, f32[16,32,128]{2,1,0:T...) custom-call(f32[16,32,128]{2,1,0:T(8,128)S(1)} %get-tuple-element.40.d_ref.refs_1_.refs_6_, ...), custom_call_target="tpu_custom_call" | custom-call | flops 100000000 | bytes 3981312 | tf_op jit(solution)/shard_map/pallas_call | solution.py:27
  33.5 0.6 shard_map.89
  34.1 11.4 %collective-permute-start.3 = (f32[6,32,128]{2,1,0:T(8,128)S(1)}, f32[6,32,128]{2,1,0:T(8,128)S(1)}, u32[]{:S(2)}, u32[]{:S(2)}) collective-permute-start(f32[6,32,128]{2,1,0:T(8,128)S(1)} %get-tuple-element.48), channel_id=1, source_target_pairs={{0,704},{64,0},{128,64},{192,128},{256,192},{320,256},{384,320},{4... | collective-permute-start | bytes 294920 | tf_op jit(solution)/shard_map/ppermute | solution.py:455
  45.5 1.9 %collective-permute-start.4 = (f32[6,32,128]{2,1,0:T(8,128)S(1)}, f32[6,32,128]{2,1,0:T(8,128)S(1)}, u32[]{:S(2)}, u32[]{:S(2)}) collective-permute-start(f32[6,32,128]{2,1,0:T(8,128)S(1)} %get-tuple-element.49), channel_id=1, source_target_pairs={{0,64},{64,128},{128,192},{192,256},{256,320},{320,384},{384,448},... | collective-permute-start | bytes 294920 | tf_op jit(solution)/shard_map/ppermute | solution.py:455
  47.4 0.0 collective-permute-done.3.refs_4_
  47.4 4.6 %collective-permute-done.4.refs_5_ = f32[6,32,128]{2,1,0:T(8,128)S(1)} collective-permute-done((f32[6,32,128]{2,1,0:T(8,128)S(1)}, f32[6,32,128]{2,1,0:T(8,128)S(1)}, u32[]{:S(2)}, u32[]{:S(2)}) %collective-permute-start.4) | collective-permute-done | bytes 98336 | tf_op jit(solution)/shard_map/ppermute | solution.py:455
  52.1 4.8 %shard_map.90 = (f32[16,32,128]{2,1,0:T(8,128)S(1)}, f32[16,32,128]{2,1,0:T(8,128)S(1)}, f32[36,32,256]{2,1,0:T(8,128)S(1)}, f32[10,32,128]{2,1,0:T(8,128)S(1)},...) custom-call(s32[1]{0:T(128)} %bitcast.core_ref.refs_0_, f32[16,32,128]{2,1,0:T(8,128)S(1)} %get-tuple-element.45.refs_0_.refs_1_, ...), custom_call_target="tpu_custom_call" | custom-call | flops 200000000 | bytes 5832708 | tf_op jit(solution)/shard_map/pallas_call | solution.py:27
  56.9 3.1 %collective-permute-start.5 = (f32[10,32,128]{2,1,0:T(8,128)S(1)}, f32[10,32,128]{2,1,0:T(8,128)S(1)}, u32[]{:S(2)}, u32[]{:S(2)}) collective-permute-start(f32[10,32,128]{2,1,0:T(8,128)S(1)} %get-tuple-element.54), channel_id=1, source_target_pairs={{0,2},{1,3},{2,4},{3,5},{4,6},{5,7},{6,8},{7,9},{8,10},{9,11},{10,... | collective-permute-start | bytes 491528 | tf_op jit(solution)/shard_map/ppermute | solution.py:452
  60.0 1.3 collective-permute-start.6
  61.3 0.9 collective-permute-done.5.refs_1_.refs_2_
  62.2 4.8 %collective-permute-done.6.refs_2_.refs_3_ = f32[10,32,128]{2,1,0:T(8,128)S(1)} collective-permute-done((f32[10,32,128]{2,1,0:T(8,128)S(1)}, f32[10,32,128]{2,1,0:T(8,128)S(1)}, u32[]{:S(2)}, u32[]{:S(2)}) %collective-permute-start.6) | collective-permute-done | bytes 163872 | tf_op jit(solution)/shard_map/ppermute | solution.py:452
  67.0 0.3 shard_map.91
  67.3 1.9 %collective-permute-start.7 = (f32[3,32,128]{2,1,0:T(8,128)S(1)}, f32[3,32,128]{2,1,0:T(8,128)S(1)}, u32[]{:S(2)}, u32[]{:S(2)}) collective-permute-start(f32[3,32,128]{2,1,0:T(8,128)S(1)} %get-tuple-element.56), channel_id=1, source_target_pairs={{0,704},{64,0},{128,64},{192,128},{256,192},{320,256},{384,320},{4... | collective-permute-start | bytes 147464 | tf_op jit(solution)/shard_map/ppermute | solution.py:455
  69.3 3.5 %collective-permute-start.8 = (f32[3,32,128]{2,1,0:T(8,128)S(1)}, f32[3,32,128]{2,1,0:T(8,128)S(1)}, u32[]{:S(2)}, u32[]{:S(2)}) collective-permute-start(f32[3,32,128]{2,1,0:T(8,128)S(1)} %get-tuple-element.57), channel_id=1, source_target_pairs={{0,64},{64,128},{128,192},{192,256},{256,320},{320,384},{384,448},... | collective-permute-start | bytes 147464 | tf_op jit(solution)/shard_map/ppermute | solution.py:455
  72.8 0.0 collective-permute-done.7.refs_4_
  72.8 2.5 %collective-permute-done.8.refs_5_ = f32[3,32,128]{2,1,0:T(8,128)S(1)} collective-permute-done((f32[3,32,128]{2,1,0:T(8,128)S(1)}, f32[3,32,128]{2,1,0:T(8,128)S(1)}, u32[]{:S(2)}, u32[]{:S(2)}) %collective-permute-start.8) | collective-permute-done | bytes 49184 | tf_op jit(solution)/shard_map/ppermute | solution.py:455
  75.3 5.3 %shard_map.92 = (f32[16,32,128]{2,1,0:T(8,128)S(1)}, f32[5,32,128]{2,1,0:T(8,128)S(1)}, f32[5,32,128]{2,1,0:T(8,128)S(1)}, f32[16,32,128]{2,1,0:T(8,128)S(1)}, f32[64,128]{1,0:T(8,128)}) custom-call(s32[1]{0:T(128)} %bitcast.core_ref.refs_0_, f32[16,32,128]{2,1,0:T(8,128)S(1)} %get-tuple-element.53.refs_0_.refs_1_, ...), custom_call_target="tpu_custom_call" | custom-call | flops 200000000 | bytes 5275652 | tf_op jit(solution)/shard_map/pallas_call | solution.py:27
  80.6 4.3 %collective-permute-start.9 = (f32[5,32,128]{2,1,0:T(8,128)S(1)}, f32[5,32,128]{2,1,0:T(8,128)S(1)}, u32[]{:S(2)}, u32[]{:S(2)}) collective-permute-start(f32[5,32,128]{2,1,0:T(8,128)S(1)} %get-tuple-element.62), channel_id=1, source_target_pairs={{0,2},{1,3},{2,4},{3,5},{4,6},{5,7},{6,8},{7,9},{8,10},{9,11},{10,... | collective-permute-start | bytes 245768 | tf_op jit(solution)/shard_map/ppermute | solution.py:452
  84.9 1.3 collective-permute-start.10
  86.2 15.3 %all-to-all-start.1 = ((f32[64,1,128]{2,1,0:T(1,128)}), f32[64,1,128]{2,1,0:T(1,128)S(1)}, u32[]{:S(2)}, u32[]{:S(2)}) async-start(f32[64,1,128]{2,1,0:T(1,128)} %bitcast.5), calls=%async_computation.1 | async-start | bytes 65536 | tf_op jit(solution)/shard_map/all_to_all | solution.py:515
  101.5 0.0 collective-permute-done.9.refs_1_.south_ref
  101.5 0.0 collective-permute-done.10.refs_2_.north_ref
  101.5 0.3 shard_map.93
  101.8 1.9 %collective-permute-start.11 = (f32[1,32,128]{2,1,0:T(8,128)S(1)}, f32[1,32,128]{2,1,0:T(8,128)S(1)}, u32[]{:S(2)}, u32[]{:S(2)}) collective-permute-start(f32[1,32,128]{2,1,0:T(8,128)S(1)} %get-tuple-element.64), channel_id=1, source_target_pairs={{0,704},{64,0},{128,64},{192,128},{256,192},{320,256},{384,320},{4... | collective-permute-start | bytes 49160 | tf_op jit(solution)/shard_map/ppermute | solution.py:455
  103.7 3.4 %collective-permute-start.12 = (f32[1,32,128]{2,1,0:T(8,128)S(1)}, f32[1,32,128]{2,1,0:T(8,128)S(1)}, u32[]{:S(2)}, u32[]{:S(2)}) collective-permute-start(f32[1,32,128]{2,1,0:T(8,128)S(1)} %get-tuple-element.65), channel_id=1, source_target_pairs={{0,64},{64,128},{128,192},{192,256},{256,320},{320,384},{384,448},... | collective-permute-start | bytes 49160 | tf_op jit(solution)/shard_map/ppermute | solution.py:455
  107.1 3.6 %all-to-all-done.1 = f32[64,1,128]{2,1,0:T(1,128)S(1)} async-done(((f32[64,1,128]{2,1,0:T(1,128)}), f32[64,1,128]{2,1,0:T(1,128)S(1)}, u32[]{:S(2)}, u32[]{:S(2)}) %all-to-all-start.1) | async-done | bytes 32800 | tf_op jit(solution)/shard_map/all_to_all | solution.py:515
  110.7 0.8 shard_map.95
  111.5 3.5 %all-to-all-start.2 = ((f32[12,1,128]{2,1,0:T(1,128)}), f32[12,1,128]{2,1,0:T(1,128)S(1)}, u32[]{:S(2)}, u32[]{:S(2)}) async-start(f32[12,1,128]{2,1,0:T(1,128)} %shard_map.95), calls=%async_computation.2 | async-start | bytes 12288 | tf_op jit(solution)/shard_map/all_to_all | solution.py:518
  115.0 0.0 collective-permute-done.11.east_ref
  115.0 0.0 collective-permute-done.12.west_ref
  115.0 1.5 %shard_map.94 = (f32[24,32,128]{2,1,0:T(8,128)S(1)}, f32[24,32,128]{2,1,0:T(8,128)S(1)}) custom-call(s32[1]{0:T(128)} %bitcast.core_ref.refs_0_, f32[16,32,128]{2,1,0:T(8,128)S(1)} %get-tuple-element.61.refs_0_.here_ref, f32[5,32,128]{2,1,0:T(8,128)S(1)} %collective-permute-done.9.refs_1_.south_ref, ...), custom_call_target="tpu_custom_call" | custom-call | flops 100000000 | bytes 2949124 | tf_op jit(solution)/shard_map/pallas_call | solution.py:27
  116.5 7.2 %all-to-all-done.2.stats_ref = f32[12,1,128]{2,1,0:T(1,128)S(1)} async-done(((f32[12,1,128]{2,1,0:T(1,128)}), f32[12,1,128]{2,1,0:T(1,128)S(1)}, u32[]{:S(2)}, u32[]{:S(2)}) %all-to-all-start.2) | async-done | bytes 6176 | tf_op jit(solution)/shard_map/all_to_all | solution.py:518
  123.7 3.7 %collective-permute-start.13 = (f32[24,32,128]{2,1,0:T(8,128)S(1)}, f32[24,32,128]{2,1,0:T(8,128)S(1)}, u32[]{:S(2)}, u32[]{:S(2)}) collective-permute-start(f32[24,32,128]{2,1,0:T(8,128)S(1)} %get-tuple-element.70), channel_id=1, source_target_pairs={{0,1},{1,0},{2,3},{3,2},{4,5},{5,4},{6,7},{7,6},{8,9},{9,8},{10,11... | collective-permute-start | bytes 1179656 | tf_op jit(solution)/shard_map/ppermute | solution.py:458
  127.5 1.3 %collective-permute-done.13.theirs_ref = f32[24,32,128]{2,1,0:T(8,128)S(1)} collective-permute-done((f32[24,32,128]{2,1,0:T(8,128)S(1)}, f32[24,32,128]{2,1,0:T(8,128)S(1)}, u32[]{:S(2)}, u32[]{:S(2)}) %collective-permute-start.13) | collective-permute-done | bytes 393248 | tf_op jit(solution)/shard_map/ppermute | solution.py:458
  128.8 1.2 shard_map.96
  (1 shorter events, 0.0 us)
Async XLA Ops:
  3.0 28.6 %all-to-all-start = ((f32[64,8,128]{2,1,0:T(8,128)}), f32[64,8,128]{2,1,0:T(8,128)S(1)}, u32[]{:S(2)}, u32[]{:S(2)}) async-start(f32[64,8,128]{2,1,0:T(8,128)} %bitcast.2), calls=%async_computation | async-start | bytes 524288 | tf_op jit(solution)/shard_map/all_to_all | solution.py:485
  17.5 3.5 %collective-permute-start = (f32[272,128]{1,0:T(8,128)S(1)}, f32[272,128]{1,0:T(8,128)S(1)}, u32[]{:S(2)}, u32[]{:S(2)}) collective-permute-start(f32[272,128]{1,0:T(8,128)S(1)} %get-tuple-element.38), channel_id=1, source_target_pairs={{0,1},{1,0},{2,3},{3,2},{4,5},{5,4},{6,7},{7,6},{8,9},{9,8},{10,11... | collective-permute-start | bytes 417800 | tf_op jit(solution)/shard_map/ppermute | solution.py:458
  21.0 7.2 %collective-permute-start.1 = (f32[11,32,128]{2,1,0:T(8,128)S(1)}, f32[11,32,128]{2,1,0:T(8,128)S(1)}, u32[]{:S(2)}, u32[]{:S(2)}) collective-permute-start(f32[11,32,128]{2,1,0:T(8,128)S(1)} %get-tuple-element.42), channel_id=1, source_target_pairs={{0,2},{1,3},{2,4},{3,5},{4,6},{5,7},{6,8},{7,9},{8,10},{9,11},{10,... | collective-permute-start | bytes 540680 | tf_op jit(solution)/shard_map/ppermute | solution.py:452
  24.2 7.4 %collective-permute-start.2 = (f32[11,32,128]{2,1,0:T(8,128)S(1)}, f32[11,32,128]{2,1,0:T(8,128)S(1)}, u32[]{:S(2)}, u32[]{:S(2)}) collective-permute-start(f32[11,32,128]{2,1,0:T(8,128)S(1)} %get-tuple-element.43), channel_id=1, source_target_pairs={{2,0},{3,1},{4,2},{5,3},{6,4},{7,5},{8,6},{9,7},{10,8},{11,9},{12,... | collective-permute-start | bytes 540680 | tf_op jit(solution)/shard_map/ppermute | solution.py:452
  34.1 13.3 %collective-permute-start.3 = (f32[6,32,128]{2,1,0:T(8,128)S(1)}, f32[6,32,128]{2,1,0:T(8,128)S(1)}, u32[]{:S(2)}, u32[]{:S(2)}) collective-permute-start(f32[6,32,128]{2,1,0:T(8,128)S(1)} %get-tuple-element.48), channel_id=1, source_target_pairs={{0,704},{64,0},{128,64},{192,128},{256,192},{320,256},{384,320},{4... | collective-permute-start | bytes 294920 | tf_op jit(solution)/shard_map/ppermute | solution.py:455
  45.5 6.6 %collective-permute-start.4 = (f32[6,32,128]{2,1,0:T(8,128)S(1)}, f32[6,32,128]{2,1,0:T(8,128)S(1)}, u32[]{:S(2)}, u32[]{:S(2)}) collective-permute-start(f32[6,32,128]{2,1,0:T(8,128)S(1)} %get-tuple-element.49), channel_id=1, source_target_pairs={{0,64},{64,128},{128,192},{192,256},{256,320},{320,384},{384,448},... | collective-permute-start | bytes 294920 | tf_op jit(solution)/shard_map/ppermute | solution.py:455
  56.9 5.3 %collective-permute-start.5 = (f32[10,32,128]{2,1,0:T(8,128)S(1)}, f32[10,32,128]{2,1,0:T(8,128)S(1)}, u32[]{:S(2)}, u32[]{:S(2)}) collective-permute-start(f32[10,32,128]{2,1,0:T(8,128)S(1)} %get-tuple-element.54), channel_id=1, source_target_pairs={{0,2},{1,3},{2,4},{3,5},{4,6},{5,7},{6,8},{7,9},{8,10},{9,11},{10,... | collective-permute-start | bytes 491528 | tf_op jit(solution)/shard_map/ppermute | solution.py:452
  60.0 7.0 %collective-permute-start.6 = (f32[10,32,128]{2,1,0:T(8,128)S(1)}, f32[10,32,128]{2,1,0:T(8,128)S(1)}, u32[]{:S(2)}, u32[]{:S(2)}) collective-permute-start(f32[10,32,128]{2,1,0:T(8,128)S(1)} %get-tuple-element.55), channel_id=1, source_target_pairs={{2,0},{3,1},{4,2},{5,3},{6,4},{7,5},{8,6},{9,7},{10,8},{11,9},{12,... | collective-permute-start | bytes 491528 | tf_op jit(solution)/shard_map/ppermute | solution.py:452
  67.3 5.5 %collective-permute-start.7 = (f32[3,32,128]{2,1,0:T(8,128)S(1)}, f32[3,32,128]{2,1,0:T(8,128)S(1)}, u32[]{:S(2)}, u32[]{:S(2)}) collective-permute-start(f32[3,32,128]{2,1,0:T(8,128)S(1)} %get-tuple-element.56), channel_id=1, source_target_pairs={{0,704},{64,0},{128,64},{192,128},{256,192},{320,256},{384,320},{4... | collective-permute-start | bytes 147464 | tf_op jit(solution)/shard_map/ppermute | solution.py:455
  69.3 6.0 %collective-permute-start.8 = (f32[3,32,128]{2,1,0:T(8,128)S(1)}, f32[3,32,128]{2,1,0:T(8,128)S(1)}, u32[]{:S(2)}, u32[]{:S(2)}) collective-permute-start(f32[3,32,128]{2,1,0:T(8,128)S(1)} %get-tuple-element.57), channel_id=1, source_target_pairs={{0,64},{64,128},{128,192},{192,256},{256,320},{320,384},{384,448},... | collective-permute-start | bytes 147464 | tf_op jit(solution)/shard_map/ppermute | solution.py:455
  80.6 20.9 %collective-permute-start.9 = (f32[5,32,128]{2,1,0:T(8,128)S(1)}, f32[5,32,128]{2,1,0:T(8,128)S(1)}, u32[]{:S(2)}, u32[]{:S(2)}) collective-permute-start(f32[5,32,128]{2,1,0:T(8,128)S(1)} %get-tuple-element.62), channel_id=1, source_target_pairs={{0,2},{1,3},{2,4},{3,5},{4,6},{5,7},{6,8},{7,9},{8,10},{9,11},{10,... | collective-permute-start | bytes 245768 | tf_op jit(solution)/shard_map/ppermute | solution.py:452
  84.9 16.6 %collective-permute-start.10 = (f32[5,32,128]{2,1,0:T(8,128)S(1)}, f32[5,32,128]{2,1,0:T(8,128)S(1)}, u32[]{:S(2)}, u32[]{:S(2)}) collective-permute-start(f32[5,32,128]{2,1,0:T(8,128)S(1)} %get-tuple-element.63), channel_id=1, source_target_pairs={{2,0},{3,1},{4,2},{5,3},{6,4},{7,5},{8,6},{9,7},{10,8},{11,9},{12,... | collective-permute-start | bytes 245768 | tf_op jit(solution)/shard_map/ppermute | solution.py:452
  86.2 24.5 %all-to-all-start.1 = ((f32[64,1,128]{2,1,0:T(1,128)}), f32[64,1,128]{2,1,0:T(1,128)S(1)}, u32[]{:S(2)}, u32[]{:S(2)}) async-start(f32[64,1,128]{2,1,0:T(1,128)} %bitcast.5), calls=%async_computation.1 | async-start | bytes 65536 | tf_op jit(solution)/shard_map/all_to_all | solution.py:515
  101.8 13.2 %collective-permute-start.11 = (f32[1,32,128]{2,1,0:T(8,128)S(1)}, f32[1,32,128]{2,1,0:T(8,128)S(1)}, u32[]{:S(2)}, u32[]{:S(2)}) collective-permute-start(f32[1,32,128]{2,1,0:T(8,128)S(1)} %get-tuple-element.64), channel_id=1, source_target_pairs={{0,704},{64,0},{128,64},{192,128},{256,192},{320,256},{384,320},{4... | collective-permute-start | bytes 49160 | tf_op jit(solution)/shard_map/ppermute | solution.py:455
  103.7 11.3 %collective-permute-start.12 = (f32[1,32,128]{2,1,0:T(8,128)S(1)}, f32[1,32,128]{2,1,0:T(8,128)S(1)}, u32[]{:S(2)}, u32[]{:S(2)}) collective-permute-start(f32[1,32,128]{2,1,0:T(8,128)S(1)} %get-tuple-element.65), channel_id=1, source_target_pairs={{0,64},{64,128},{128,192},{192,256},{256,320},{320,384},{384,448},... | collective-permute-start | bytes 49160 | tf_op jit(solution)/shard_map/ppermute | solution.py:455
  111.5 12.2 %all-to-all-start.2 = ((f32[12,1,128]{2,1,0:T(1,128)}), f32[12,1,128]{2,1,0:T(1,128)S(1)}, u32[]{:S(2)}, u32[]{:S(2)}) async-start(f32[12,1,128]{2,1,0:T(1,128)} %shard_map.95), calls=%async_computation.2 | async-start | bytes 12288 | tf_op jit(solution)/shard_map/all_to_all | solution.py:518
  123.7 5.0 %collective-permute-start.13 = (f32[24,32,128]{2,1,0:T(8,128)S(1)}, f32[24,32,128]{2,1,0:T(8,128)S(1)}, u32[]{:S(2)}, u32[]{:S(2)}) collective-permute-start(f32[24,32,128]{2,1,0:T(8,128)S(1)} %get-tuple-element.70), channel_id=1, source_target_pairs={{0,1},{1,0},{2,3},{3,2},{4,5},{5,4},{6,7},{7,6},{8,9},{9,8},{10,11... | collective-permute-start | bytes 1179656 | tf_op jit(solution)/shard_map/ppermute | solution.py:458
